TPU v7x, 32 devices: a whole 2x2x4 slice. The times are simulated.
32 devices in a mesh: parts: 2 (over y), dp: 4 (over x, core), tensor: 4 (over z).
Axes of the slice: x: 2, y: 2, z: 4, core: 2. Of those that a mesh axis runs over, the one named last changes fastest.
Arguments:
- layer_input: bfloat16 [16384, 8192], P(('parts', 'dp'), 'tensor'), parts along dimension 0, may hold values from -6 to 6
- up_grad: bfloat16 [16384, 28672], P(('parts', 'dp'), 'tensor'), parts along dimension 0, may hold values from -6 to 6
- hidden_input: bfloat16 [16384, 28672], P(('parts', 'dp'), 'tensor'), parts along dimension 0, may hold values from -6 to 6
- down_grad: bfloat16 [16384, 8192], P(('parts', 'dp'), 'tensor'), parts along dimension 0, may hold values from -6 to 6
- in_up: bfloat16 [128, 8192], P(None, 'tensor'), may hold values from -0.0625 to 0.0625
- out_up: bfloat16 [128, 28672], P(None, 'tensor'), may hold values from -0.03125 to 0.03125
- in_down: bfloat16 [128, 28672], P(None, 'tensor'), may hold values from -0.03125 to 0.03125
- out_down: bfloat16 [128, 8192], P(None, 'tensor'), may hold values from -0.0625 to 0.0625
- query_sketch: float32 [512, 2, 128, 128], P(('parts', 'dp'), None, 'tensor'), parts along dimension 0, may hold values from -6 to 6
Outputs:
- scores: float32 [64, 256], P(('parts', 'dp')), parts along dimension 0
There are 2 independent parts, one for each index of `parts`. A program takes and returns all parts, laid end to end along the dimension named above; an argument that names none is the same for every part. Nothing has to cross between parts.
All inputs are finite; a program needn't handle non-finite values.
Results may differ from a plain program's by a relative error of at most 0.0003.
Values sent between devices are 32-bit elements; how exact they have to be, the bound alone decides.
No kernel may reach another device: no remote copies, remote signals or barrier semaphores. Data moves between devices by JAX's collectives and lax.ppermute only.
A program may use at most 192 MiB of HBM per device.

v0:
```python
import jax
import jax.numpy as jnp
from jax import lax
from jax.sharding import PartitionSpec as P

K = 128
LEN = 256


def project(act, proj):
    return jnp.dot(act, proj.T, preferred_element_type=jnp.float32)


def own_rows(full, width):
    return lax.dynamic_slice_in_dim(full, lax.axis_index("tensor") * width, width, 1)


def layer_sketch(left, right, examples):
    left3 = left.reshape(examples, LEN, left.shape[1])
    right3 = right.reshape(examples, LEN, right.shape[1])
    return jnp.einsum("elr,elc->erc", left3, right3, precision=lax.Precision.HIGHEST) / jnp.sqrt(
        jnp.float32(LEN)
    )


def local(
    layer_input, up_grad, hidden_input, down_grad, in_up, out_up, in_down, out_down, query_sketch
):
    width = K // lax.axis_size("tensor")
    examples = layer_input.shape[0] // LEN
    a_up = project(layer_input, in_up)
    b_up = project(up_grad, out_up)
    a_down = project(hidden_input, in_down)
    b_down = project(down_grad, out_down)
    a_up, b_up = lax.psum((a_up, b_up), "tensor")
    a_down, b_down = lax.psum((a_down, b_down), "tensor")
    a_up = own_rows(a_up, width)
    a_down = own_rows(a_down, width)
    sketch = jnp.stack(
        [layer_sketch(a_up, b_up, examples), layer_sketch(a_down, b_down, examples)], axis=1
    )
    partial_total = jnp.einsum(
        "elrc,qlrc->qe",
        sketch,
        lax.all_gather(query_sketch, "dp", axis=0, tiled=True),
        precision=lax.Precision.HIGHEST,
    )
    total = lax.psum(partial_total, "tensor")
    return total.T / jnp.float32(K)


def solution(mesh):
    placed = (
        P(("parts", "dp"), "tensor"),
        P(("parts", "dp"), "tensor"),
        P(("parts", "dp"), "tensor"),
        P(("parts", "dp"), "tensor"),
        P(None, "tensor"),
        P(None, "tensor"),
        P(None, "tensor"),
        P(None, "tensor"),
        P(("parts", "dp"), None, "tensor", None),
    )
    return jax.shard_map(
        local, mesh=mesh, in_specs=placed, out_specs=P(("parts", "dp"), None), check_vma=False
    )
```

profile of v0, /device:TPU:0, one launch (start us, length us, event | category | flops | bytes accessed | tf_op | source)
XLA Modules:
  0.0 239.0 jit_solution(12722962920447075287)
XLA Ops:
  7.4 0.0 copy-start
  7.4 0.0 all-reduce.3.cloned.1.call-start
  7.4 7.4 %fusion.7 = f32[2048,128]{0,1:T(8,128)} fusion(bf16[2048,2048]{1,0:T(8,128)(2,1)} %param.9, bf16[128,2048]{1,0:T(8,128)(2,1)} %param.13), kind=kOutput, calls=%fused_computation.14 | convolution fusion | flops 1073741824 | bytes 9961472 | tf_op jit(solution)/shard_map/dot_general | solution.py:11
  14.8 0.0 copy-done
  14.8 0.0 copy-start.2
  14.8 0.0 slice-start
  14.8 14.5 %fusion.8 = f32[2048,128]{1,0:T(8,128)} fusion(bf16[2048,7168]{1,0:T(8,128)(2,1)} %param.10, bf16[128,7168]{1,0:T(8,128)(2,1)S(1)} %copy-done), kind=kOutput, calls=%fused_computation.15 | convolution fusion | flops 3758096384 | bytes 32243712 | tf_op jit(solution)/shard_map/dot_general | solution.py:11
  29.3 0.0 copy-done.2
  29.3 0.0 slice-start.1
  29.3 0.0 copy-start.3
  29.3 15.9 %fusion.9 = f32[2048,128]{0,1:T(8,128)} fusion(bf16[2048,7168]{1,0:T(8,128)(2,1)} %param.11, bf16[128,7168]{1,0:T(8,128)(2,1)S(1)} %copy-done.2), kind=kOutput, calls=%fused_computation.16 | convolution fusion | flops 3758096384 | bytes 32243712 | tf_op jit(solution)/shard_map/dot_general | solution.py:11
  45.2 0.0 slice-done
  45.2 0.0 slice-done.1
  45.2 0.0 copy-done.3
  45.2 3.4 %fusion.10 = f32[2048,128]{1,0:T(8,128)} fusion(bf16[2048,2048]{1,0:T(8,128)(2,1)S(1)} %bitcast.38, bf16[128,2048]{1,0:T(8,128)(2,1)S(1)} %copy-done.3), kind=kOutput, calls=%fused_computation.17 | convolution fusion | flops 1073741824 | bytes 9961472 | tf_op jit(solution)/shard_map/dot_general | solution.py:11
  48.6 0.0 all-reduce.3.cloned.1.call-update
  48.6 0.2 all-gather.2.cloned.1.call-start
  48.8 0.0 copy-start.1
  48.8 4.3 %copy.14 = f32[64,2,32,128]{3,0,2,1:T(8,128)} copy(f32[64,2,32,128]{3,2,1,0:T(8,128)} %param.17) | data formatting | bytes 4194304 | tf_op args[8]
  53.2 0.0 all-gather.2.cloned.1.call-update
  53.2 154.3 %all-reduce.3.cloned.1.call-done = (f32[8,256,128]{2,1,0:T(8,128)}, f32[2048,128]{0,1:T(8,128)}, f32[8,256,128]{2,1,0:T(8,128)}, f32[2048,128]{0,1:T(8,128)}) async-done(((f32[8,256,128]{2,1,0:T(8,128)}, f32[2048,128]{0,1:T(8,128)}, f32[8,256,128]{2,1,0:T(8,128)}, f32[2048,128]{0,1:T(8,128)}), (f32[8,256,128]{2,1,0:T(8,128)}, f32[2048,128]{0,1:T(8,128)}, f32[8,256,128]{2,1,0:T(8,128)}, ...) | async-done | bytes 4194320 | tf_op jit(solution)/shard_map/psum | solution.py:36
  207.5 1.1 constant_dynamic-slice_fusion
  208.6 1.9 fusion
  210.5 1.9 fusion.1
  212.4 0.0 all-gather.2.cloned.1.call-done
  212.4 8.9 %convolution_bitcast_fusion = f32[256,8]{0,1:T(8,128)S(1)} fusion(f32[256,2,32,128]{3,0,2,1:T(8,128)} %all-gather.2.cloned.1.call-done, f32[8,2,32,128]{3,2,0,1:T(8,128)S(1)} %pad_maximum_fusion), kind=kOutput, calls=%fused_computation.4 | convolution fusion | flops 201326592 | bytes 8658944 | tf_op jit(solution)/shard_map/elrc,qlrc->qe/dot_general | solution.py:42
  221.3 9.6 %psum.39 = f32[256,8]{0,1:T(8,128)S(1)} all-reduce(f32[256,8]{0,1:T(8,128)S(1)} %convolution_bitcast_fusion), channel_id=1, replica_groups=mesh['parts'=2,'dp'=4,'tensor'=4] {'tensor'}, use_global_device_ids=true, to_apply=%region_4.0 | all-reduce | flops 2048 | bytes 16384 | tf_op jit(solution)/shard_map/psum | solution.py:48
  231.0 0.6 multiply_bitcast_fusion
  231.6 0.0 copy-done.1
  (2 shorter events, 0.0 us)
Async XLA Ops:
  7.4 7.5 %copy-start = (bf16[128,7168]{1,0:T(8,128)(2,1)S(1)}, bf16[128,7168]{1,0:T(8,128)(2,1)}, u32[]{:S(2)}) copy-start(bf16[128,7168]{1,0:T(8,128)(2,1)} %param.14) | copy-start | bytes 5505028
  7.4 200.1 %all-reduce.3.cloned.1.call-start = ((), (), s32[]{:S(2)}) async-start(), calls=%async_computation.1 | async-start | bytes 8388608 | tf_op jit(solution)/shard_map/psum | solution.py:36
  14.8 14.5 %copy-start.2 = (bf16[128,7168]{1,0:T(8,128)(2,1)S(1)}, bf16[128,7168]{1,0:T(8,128)(2,1)}, u32[]{:S(2)}) copy-start(bf16[128,7168]{1,0:T(8,128)(2,1)} %param.15) | copy-start | bytes 5505028
  14.8 30.3 %slice-start = ((s8[8388608]{0:T(1024)(128)(4,1)}), s8[4194304]{0:T(1024)(128)(4,1)S(1)}, s32[]{:S(2)}) async-start(s8[8388608]{0:T(1024)(128)(4,1)} %bitcast.37), calls=%async_computation.2 | async-start | bytes 8388608
  29.3 15.9 %slice-start.1 = ((s8[8388608]{0:T(1024)(128)(4,1)}), s8[4194304]{0:T(1024)(128)(4,1)S(1)}, s32[]{:S(2)}) async-start(s8[8388608]{0:T(1024)(128)(4,1)} %bitcast.37), calls=%async_computation.3 | async-start | bytes 8388608
  29.3 15.9 %copy-start.3 = (bf16[128,2048]{1,0:T(8,128)(2,1)S(1)}, bf16[128,2048]{1,0:T(8,128)(2,1)}, u32[]{:S(2)}) copy-start(bf16[128,2048]{1,0:T(8,128)(2,1)} %param.16) | copy-start | bytes 1572868
  48.6 163.8 %all-gather.2.cloned.1.call-start = ((), (), s32[]{:S(2)}) async-start(), calls=%async_computation | async-start | bytes 10485760 | tf_op jit(solution)/shard_map/all_gather | solution.py:45
  48.8 182.7 %copy-start.1 = (bf16[128,7168]{1,0:T(8,128)(2,1)S(1)}, bf16[128,7168]{1,0:T(8,128)(2,1)}, u32[]{:S(2)}) copy-start(bf16[128,7168]{1,0:T(8,128)(2,1)} %param.14) | copy-start | bytes 5505028
Sparse Core Ops, SparseCore 0:
  48.7 158.7 all-reduce.2
Sparse Core Ops, SparseCore 1:
  53.3 60.8 all-gather.1
where the time goes:
time: 239 us
  waiting for transfers between devices  154 us (64%)
  matrix products  53.9 us (23%)
  between operations  14.9 us (6%)
  blocking collectives  9.61 us (4%)
  local copies, waits for them, and re-layouts  5.4 us (2%)
    psum x1, waiting for transfers between devices, local(): a_down, b_down = lax.psum((a_down, b_down), 'tensor')  154 us
    dot_general x4, matrix products, project(): return jnp.dot(act, proj.T, preferred_element_type=jnp.float32)  41.2 us
    psum x1, blocking collectives, local(): total = lax.psum(partial_total, 'tensor')  9.61 us
    dot_general x1, matrix products, local(): jnp.einsum('elrc,qlrc->qe', sketch, lax.all_gather(query_sketch, 'dp', ax...  8.89 us
  transfers between devices with their start and end apart: 2, of which 1 were waited for; matrix products, arithmetic and copies ran while one was open for 4% of the time, Pallas kernels for 0%

commit v1 on v0

v1 whole, which is shorter than its diff:
```python
import functools

import jax
import jax.numpy as jnp
from jax import lax
from jax.experimental import pallas as pl
from jax.experimental.pallas import tpu as pltpu
from jax.sharding import PartitionSpec as P

K = 128
LEN = 256
LAG = 3
PIECE = 1024
AHEAD = 4
ROWS_BY_ROWS = (((1,), (1,)), ((), ()))
SIDES = [(0, 1), (1, 0), (2, 3), (3, 2)]
MIDDLE = [(1, 2), (2, 1)]
SKIP = [(0, 2), (3, 1)]
ENDS = [(0, 3), (3, 0)]

WHOLE = pl.BlockSpec(memory_space=pltpu.VMEM)
SCALARS = pl.BlockSpec(memory_space=pltpu.SMEM)
ANYWHERE = pl.BlockSpec(memory_space=pl.ANY)


def send(x, pairs):
    return lax.ppermute(x, "tensor", pairs)


def halves(x):
    high = x.astype(jnp.bfloat16)
    return high, (x - high.astype(jnp.float32)).astype(jnp.bfloat16)


def pieces(width):
    return [(lo, min(lo + PIECE, width)) for lo in range(0, width, PIECE)]


def project_kernel(blocks, index, left, right, p_left, p_right, *refs):
    outs, (held_left, held_right, sem) = refs[:blocks], refs[blocks:]
    steps = []
    for x, held, p, row in ((left, held_left, p_left, 0), (right, held_right, p_right, K)):
        for lo, hi in pieces(x.shape[1]):
            copies = [
                pltpu.make_async_copy(
                    x.at[pl.ds(pl.multiple_of(index[i] * LEN, LEN), LEN), lo:hi],
                    held.at[i * LEN : (i + 1) * LEN, lo:hi],
                    sem.at[len(steps) * blocks + i],
                )
                for i in range(blocks)
            ]
            steps.append((copies, held, p, row, lo, hi))
    for step in steps[:AHEAD]:
        for copy in step[0]:
            copy.start()
    for n, (copies, held, p, row, lo, hi) in enumerate(steps):
        for copy in copies:
            copy.wait()
        if n + AHEAD < len(steps):
            for copy in steps[n + AHEAD][0]:
                copy.start()
        part = lax.dot_general(
            p[:, lo:hi], held[:, lo:hi], ROWS_BY_ROWS, preferred_element_type=jnp.float32
        )
        for i, out in enumerate(outs):
            if lo == 0:
                out[row : row + K, :] = part[:, i * LEN : (i + 1) * LEN]
            else:
                out[row : row + K, :] += part[:, i * LEN : (i + 1) * LEN]


def project(index, left, right, p_left, p_right):
    blocks = index.shape[0]
    widths = left.shape[1], right.shape[1]
    rows = blocks * LEN
    copies = blocks * sum(len(pieces(w)) for w in widths)
    return pl.pallas_call(
        functools.partial(project_kernel, blocks),
        in_specs=[SCALARS, ANYWHERE, ANYWHERE, WHOLE, WHOLE],
        out_specs=[WHOLE] * blocks,
        out_shape=[pltpu.VMEM((2 * K, LEN), jnp.float32)] * blocks,
        scratch_shapes=[
            pltpu.VMEM((rows, widths[0]), left.dtype),
            pltpu.VMEM((rows, widths[1]), right.dtype),
            pltpu.SemaphoreType.DMA((copies,)),
        ],
        compiler_params=pltpu.CompilerParams(vmem_limit_bytes=44 * 2**20),
        cost_estimate=pl.CostEstimate(
            flops=2 * rows * K * sum(widths), bytes_accessed=2 * rows * sum(widths), transcendentals=0
        ),
    )(index, left, right, p_left, p_right)


def sketch_kernel(count, width, dest, *refs):
    own, got, outs, full = refs[:count], refs[count : 2 * count], refs[2 * count : -1], refs[-1]
    for i in range(count):
        both = own[i][...] + got[i][...]
        high, low = halves(both)
        a = jnp.concatenate([high[:K], low[:K]], 0)
        b = jnp.concatenate([high[K:], low[K:]], 0)
        s = lax.dot_general(a, b, ROWS_BY_ROWS, preferred_element_type=jnp.float32)
        full[...] = s[:K, :K] + (s[:K, K:] + s[K:, :K] + s[K:, K:])
        for n, out in enumerate(outs):
            out[i] = full[pl.ds(pl.multiple_of(dest[n] * width, 8), width), :]


def sketches(dest, own, got, width):
    count = len(own)
    return pl.pallas_call(
        functools.partial(sketch_kernel, count, width),
        in_specs=[SCALARS] + [WHOLE] * (2 * count),
        out_specs=[WHOLE] * 4,
        out_shape=[pltpu.VMEM((count, width, K), jnp.float32)] * 4,
        scratch_shapes=[pltpu.VMEM((K, K), jnp.float32)],
        cost_estimate=pl.CostEstimate(
            flops=8 * count * LEN * K * K, bytes_accessed=count * 2**19, transcendentals=0
        ),
    )(dest, *own, *got)


def score_kernel(steps, rows, place, *refs):
    (cuts, queries, out, cat, total) = refs[:-4], *refs[-4:]
    k = pl.program_id(0)
    half = cuts[0].shape[0]

    def gather(layer, first):
        own, near, skip, across = cuts[4 * layer : 4 * layer + 4]
        for i in range(rows):
            r = first + i
            lanes = slice(i * K, (i + 1) * K)
            home = jnp.where(place[0] == 1, own[:, r, :], near[:, r, :])
            far = jnp.where(place[0] == 1, across[:, r, :], skip[:, r, :])
            high, low = halves(jnp.concatenate([home, far], 0))
            cat[: 2 * half, lanes] = high.astype(jnp.float32)
            cat[2 * half :, lanes] = low.astype(jnp.float32)

    for step in range(steps):

        @pl.when(k == step)
        def _():
            layer, part = divmod(step, steps // 2)
            gather(layer, part * rows)

    s = cat[...].astype(jnp.bfloat16)
    high, low = halves(queries[...])
    d = lax.dot_general(s, high, ROWS_BY_ROWS, preferred_element_type=jnp.float32)
    d += lax.dot_general(s, low, ROWS_BY_ROWS, preferred_element_type=jnp.float32)
    d = d[: 2 * half] + d[2 * half :]

    @pl.when(k == 0)
    def _():
        total[...] = d

    @pl.when(k > 0)
    def _():
        total[...] += d

    @pl.when(k == steps - 1)
    def _():
        t = total[...] * (1.0 / (LEN**0.5 * K))
        swapped = jnp.concatenate([t[half:], t[:half]], 0)
        out[...] = jnp.where(place[1] == 1, t, swapped)


def score(place, cuts, queries):
    half, width, _ = cuts[0].shape
    count, depth = queries.shape
    steps = 4
    rows = 2 * width // steps
    return pl.pallas_call(
        functools.partial(score_kernel, steps, rows),
        grid=(steps,),
        in_specs=[SCALARS]
        + [WHOLE] * len(cuts)
        + [pl.BlockSpec((count, depth // steps), lambda k: (0, k))],
        out_specs=WHOLE,
        out_shape=jax.ShapeDtypeStruct((2 * half, count), jnp.float32),
        scratch_shapes=[
            pltpu.VMEM((4 * half, depth // steps), jnp.float32),
            pltpu.VMEM((2 * half, count), jnp.float32),
        ],
        cost_estimate=pl.CostEstimate(
            flops=64 * count * depth, bytes_accessed=4 * count * depth, transcendentals=0
        ),
    )(place, *cuts, queries)


def line(
    layer_input, up_grad, hidden_input, down_grad, in_up, out_up, in_down, out_down, query_sketch
):
    half = layer_input.shape[0] // LEN // 2
    width = K // lax.axis_size("tensor")
    z = lax.axis_index("tensor")
    on_left = z < 2
    at_end = (z == 0) | (z == 3)
    far = jnp.where(on_left, half, 0).astype(jnp.int32)
    home = half - far
    local_queries = query_sketch.shape[0]
    queries = lax.all_gather(query_sketch.reshape(local_queries, -1), "dp", axis=0, tiled=True)

    keep = lambda x: pltpu.with_memory_space_constraint(x, pltpu.VMEM)
    layers = (
        (layer_input, up_grad, keep(in_up), keep(out_up)),
        (hidden_input, down_grad, keep(in_down), keep(out_down)),
    )
    forward, backward = [], []
    for layer, group in ((0, [0]), (0, [1]), (0, [2, 3]), (1, [0, 1]), (1, [2, 3])):
        index = jnp.stack([far + e for e in group] + [home + e for e in group])
        outs = project(index, *layers[layer])
        forward += outs[: len(group)]
        backward += outs[len(group) :]

    chunks = len(forward)
    side, middle = {}, {}
    for k in range(chunks + LAG):
        done = k - LAG
        load = forward[k] if k < chunks else None
        if done >= 0:
            back = backward[done] + middle[done]
            load = back if load is None else jnp.where(at_end, load, back)
        side[k] = send(load, SIDES)
        if 1 <= k <= chunks:
            middle[k - 1] = send(forward[k - 1] + side[k - 1], MIDDLE)

    dest = jnp.stack([z, z ^ 1, z ^ 2, 3 - z]).astype(jnp.int32)
    cuts = []
    for layer in range(2):
        mine = range(layer * half, (layer + 1) * half)
        own, near, skip, across = sketches(
            dest, [backward[i] for i in mine], [side[i + LAG] for i in mine], width
        )
        cuts += [own, send(near, SIDES), send(skip, SKIP), send(across, ENDS)]
    place = jnp.stack([at_end, on_left]).astype(jnp.int32)
    return lax.psum(score(place, cuts, queries), "tensor")


def own_rows(full, width):
    return lax.dynamic_slice_in_dim(full, lax.axis_index("tensor") * width, width, 1)


def layer_sketch(left, right, examples):
    left3 = left.reshape(examples, LEN, left.shape[1])
    right3 = right.reshape(examples, LEN, right.shape[1])
    return jnp.einsum("elr,elc->erc", left3, right3, precision=lax.Precision.HIGHEST) / jnp.sqrt(
        jnp.float32(LEN)
    )


def wide(
    layer_input, up_grad, hidden_input, down_grad, in_up, out_up, in_down, out_down, query_sketch
):
    width = K // lax.axis_size("tensor")
    examples = layer_input.shape[0] // LEN
    pairs = (
        (layer_input, in_up),
        (up_grad, out_up),
        (hidden_input, in_down),
        (down_grad, out_down),
    )
    a_up, b_up, a_down, b_down = lax.psum(
        tuple(jnp.dot(x, p.T, preferred_element_type=jnp.float32) for x, p in pairs), "tensor"
    )
    sketch = jnp.stack(
        [
            layer_sketch(own_rows(a_up, width), b_up, examples),
            layer_sketch(own_rows(a_down, width), b_down, examples),
        ],
        axis=1,
    )
    partial_total = jnp.einsum(
        "elrc,qlrc->qe",
        sketch,
        lax.all_gather(query_sketch, "dp", axis=0, tiled=True),
        precision=lax.Precision.HIGHEST,
    )
    return lax.psum(partial_total, "tensor").T / jnp.float32(K)


def solution(mesh):
    placed = (
        P(("parts", "dp"), "tensor"),
        P(("parts", "dp"), "tensor"),
        P(("parts", "dp"), "tensor"),
        P(("parts", "dp"), "tensor"),
        P(None, "tensor"),
        P(None, "tensor"),
        P(None, "tensor"),
        P(None, "tensor"),
        P(("parts", "dp"), None, "tensor", None),
    )
    return jax.shard_map(
        line if mesh.shape["tensor"] == 4 else wide,
        mesh=mesh,
        in_specs=placed,
        out_specs=P(("parts", "dp"), None),
        check_vma=False,
    )
```

time: 239 us -> 170 us (0.71)
  waiting for transfers between devices: 154 us -> 13.5 us
  starting transfers between devices: 0.23 us -> 57.5 us
  matrix products: 53.9 us -> 0 us
  Pallas kernels: 0 us -> 51.4 us
  other arithmetic: 0.62 us -> 9.89 us
  local copies, waits for them, and re-layouts: 5.4 us -> 11.3 us
    psum x1 -> x0, waiting for transfers between devices: 154 us -> none  [local(): a_down, b_down = lax.psum((a_down, b_down), 'tensor')]
    ppermute x0 -> x25, starting transfers between devices: none -> 57.5 us  [send(): return lax.ppermute(x, 'tensor', pairs)]
    dot_general x7 -> x0, matrix products: 53.9 us -> none  [the longest x4 41.2 us: project(): return jnp.dot(act, proj.T, preferred_element_type=jnp.float32)]
    pallas_call x0 -> x8, Pallas kernels: none -> 51.4 us  [the longest x5 41.4 us: project(): pl.pallas_call(functools.partial(project_kernel, blocks), in_specs=[SCALA...]
    ppermute x0 -> x25, waiting for transfers between devices: none -> 13.5 us  [send(): return lax.ppermute(x, 'tensor', pairs)]
    unnamed x13 -> x79, local copies, waits for them, and re-layouts: 4.34 us -> 11.3 us
    add x0 -> x11, other arithmetic: none -> 5.88 us  [the longest x8 5.78 us: line(): middle[k - 1] = send(forward[k - 1] + side[k - 1], MIDDLE)]
    select_n x0 -> x5, other arithmetic: none -> 2.51 us  [line(): load = back if load is None else jnp.where(at_end, load, back)]
  transfers between devices with their start and end apart: 2 -> 26, of which waited for: 1 -> 5; matrix products, arithmetic and copies ran while one was open for 4% -> 6% of each run, Pallas kernels for 0% -> 27%
where the time goes in v1:
time: 170 us; the launch traced here: 169 us
  starting transfers between devices  57.5 us (34%)
  Pallas kernels  51.4 us (30%)
  between operations  14 us (8%)
  waiting for transfers between devices  13.5 us (8%)
  local copies, waits for them, and re-layouts  11.3 us (7%)
  blocking collectives  11.3 us (7%)
  other arithmetic  9.89 us (6%)
    ppermute x25, starting transfers between devices, send(): return lax.ppermute(x, 'tensor', pairs)  57.5 us
    pallas_call x5, Pallas kernels, project(): pl.pallas_call(functools.partial(project_kernel, blocks), in_specs=[SCALA...  41.4 us
    ppermute x25, waiting for transfers between devices, send(): return lax.ppermute(x, 'tensor', pairs)  13.5 us
    unnamed x79, local copies, waits for them, and re-layouts  11.3 us
    psum x1, blocking collectives, line(): return lax.psum(score(place, cuts, queries), 'tensor')  11.3 us
    pallas_call x1, Pallas kernels, score(): pl.pallas_call(functools.partial(score_kernel, steps, rows), grid=(steps,...  6.25 us
    add x8, other arithmetic, line(): middle[k - 1] = send(forward[k - 1] + side[k - 1], MIDDLE)  5.78 us
    pallas_call x2, Pallas kernels, sketches(): pl.pallas_call(functools.partial(sketch_kernel, count, width), in_specs=[...  3.77 us
  transfers between devices with their start and end apart: 26, of which 5 were waited for; matrix products, arithmetic and copies ran while one was open for 6% of the time, Pallas kernels for 27%

profile of v1, /device:TPU:0, one launch (start us, length us, event | category | flops | bytes accessed | tf_op | source)
XLA Modules:
  0.0 168.9 jit_solution(1215153704972184415)
XLA Ops:
  6.5 4.1 %copy.12 = f32[8,8,64,128]{3,1,2,0:T(8,128)} copy(f32[8,8,64,128]{3,2,1,0:T(8,128)} %bitcast.20) | data formatting | bytes 4194304
  10.8 1.5 copy-done
  13.3 6.4 %shard_map.92 = (f32[256,256]{1,0:T(8,128)}, f32[256,256]{1,0:T(8,128)S(1)}) custom-call(s32[2]{0:T(128)S(1)} %pad_add_fusion.2.index, bf16[2048,2048]{1,0:T(8,128)(2,1)} %left.7, bf16[2048,7168]{1,0:T(8,128)(2,1)} %right.7, bf16[128,2048]{1,0:T(8,128)(2,1)S(1)} %copy-done.4, bf16[128,7168]{1,0:T(8,128)(2,1)S(1)} %copy-done), custom_call_target="tpu_custom_call" | custom-call | flops 1207959552 | bytes 9437184 | tf_op jit(solution)/shard_map/pallas_call | solution.py:77
  19.7 3.1 %collective-permute-start.3 = (f32[256,256]{1,0:T(8,128)}, f32[256,256]{1,0:T(8,128)}, u32[]{:S(2)}, u32[]{:S(2)}) collective-permute-start(f32[256,256]{1,0:T(8,128)} %get-tuple-element.36), channel_id=1, source_target_pairs={{0,1},{1,0},{2,3},{3,2},{4,5},{5,4},{6,7},{7,6},{8,9},{9,8},{10,11... | collective-permute-start | bytes 786440 | tf_op jit(solution)/shard_map/ppermute | solution.py:27
  22.9 7.2 %shard_map.91 = (f32[256,256]{1,0:T(8,128)}, f32[256,256]{1,0:T(8,128)S(1)}) custom-call(s32[2]{0:T(128)S(1)} %pad_add_fusion.1.index, bf16[2048,2048]{1,0:T(8,128)(2,1)} %left.7, bf16[2048,7168]{1,0:T(8,128)(2,1)} %right.7, bf16[128,2048]{1,0:T(8,128)(2,1)S(1)} %copy-done.5, bf16[128,7168]{1,0:T(8,128)(2,1)S(1)} %copy-done.1), custom_call_target="tpu_custom_call" | custom-call | flops 1207959552 | bytes 9437184 | tf_op jit(solution)/shard_map/pallas_call | solution.py:77
  30.6 9.7 %shard_map.93 = (f32[256,256]{1,0:T(8,128)}, f32[256,256]{1,0:T(8,128)S(1)}, f32[256,256]{1,0:T(8,128)S(1)}, f32[256,256]{1,0:T(8,128)S(1)}) custom-call(s32[4]{0:T(128)S(1)} %pad_add_fusion.3.index, bf16[2048,2048]{1,0:T(8,128)(2,1)} %left.7, bf16[2048,7168]{1,0:T(8,128)(2,1)} %right.7, bf16[128,2048]{1,0:T(8,128)(2,1)S(1)} %copy-done.5, ...), custom_call_target="tpu_custom_call" | custom-call | flops 2415919104 | bytes 18874368 | tf_op jit(solution)/shard_map/pallas_call | solution.py:77
  40.3 1.8 %collective-permute-start.6 = (f32[256,256]{1,0:T(8,128)}, f32[256,256]{1,0:T(8,128)}, u32[]{:S(2)}, u32[]{:S(2)}) collective-permute-start(f32[256,256]{1,0:T(8,128)} %get-tuple-element.38), channel_id=1, source_target_pairs={{0,1},{1,0},{2,3},{3,2},{4,5},{5,4},{6,7},{7,6},{8,9},{9,8},{10,11... | collective-permute-start | bytes 786440 | tf_op jit(solution)/shard_map/ppermute | solution.py:27
  42.1 1.7 %add.85 = f32[256,256]{1,0:T(8,128)} add(f32[256,256]{1,0:T(8,128)} %get-tuple-element.36, f32[256,256]{1,0:T(8,128)} %collective-permute-done.3) | non-fusion elementwise | flops 65536 | bytes 786432 | tf_op jit(solution)/shard_map/add | solution.py:223
  43.8 1.4 collective-permute-start.4
  45.2 1.7 %add.83 = f32[256,256]{1,0:T(8,128)} add(f32[256,256]{1,0:T(8,128)} %get-tuple-element.34, f32[256,256]{1,0:T(8,128)} %collective-permute-done) | non-fusion elementwise | flops 65536 | bytes 786432 | tf_op jit(solution)/shard_map/add | solution.py:223
  47.0 1.5 collective-permute-start.1
  48.5 9.1 %shard_map.94 = (f32[256,256]{1,0:T(8,128)S(1)}, f32[256,256]{1,0:T(8,128)S(1)}, f32[256,256]{1,0:T(8,128)S(1)}, f32[256,256]{1,0:T(8,128)S(1)}) custom-call(s32[4]{0:T(128)S(1)} %pad_add_fusion.4.index, bf16[2048,7168]{1,0:T(8,128)(2,1)} %left.9, bf16[2048,2048]{1,0:T(8,128)(2,1)} %right.9, bf16[128,7168]{1,0:T(8,128)(2,1)S(1)} %copy-done.2, ...), custom_call_target="tpu_custom_call" | custom-call | flops 2415919104 | bytes 18874368 | tf_op jit(solution)/shard_map/pallas_call | solution.py:77
  59.0 1.3 add_select_fusion.3
  60.3 4.4 %collective-permute-start.5 = (f32[256,256]{1,0:T(8,128)S(1)}, f32[256,256]{1,0:T(8,128)S(1)}, u32[]{:S(2)}, u32[]{:S(2)}) collective-permute-start(f32[256,256]{1,0:T(8,128)S(1)} %add_select_fusion.3), channel_id=1, source_target_pairs={{0,1},{1,0},{2,3},{3,2},{4,5},{5,4},{6,7},{7,6},{8,9},{9,8},{10,11... | collective-permute-start | bytes 786440 | tf_op jit(solution)/shard_map/ppermute | solution.py:27
  67.6 4.3 %collective-permute-done.5.refs_5_ = f32[256,256]{1,0:T(8,128)S(1)} collective-permute-done((f32[256,256]{1,0:T(8,128)S(1)}, f32[256,256]{1,0:T(8,128)S(1)}, u32[]{:S(2)}, u32[]{:S(2)}) %collective-permute-start.5) | collective-permute-done | bytes 262176 | tf_op jit(solution)/shard_map/ppermute | solution.py:27
  73.9 9.0 %shard_map.95 = (f32[256,256]{1,0:T(8,128)S(1)}, f32[256,256]{1,0:T(8,128)S(1)}, f32[256,256]{1,0:T(8,128)S(1)}, f32[256,256]{1,0:T(8,128)S(1)}) custom-call(s32[4]{0:T(128)S(1)} %pad_add_fusion.3.index, bf16[2048,7168]{1,0:T(8,128)(2,1)} %left.9, bf16[2048,2048]{1,0:T(8,128)(2,1)} %right.9, bf16[128,7168]{1,0:T(8,128)(2,1)S(1)} %copy-done.3, ...), custom_call_target="tpu_custom_call" | custom-call | flops 2415919104 | bytes 18874368 | tf_op jit(solution)/shard_map/pallas_call | solution.py:77
  83.8 6.6 %collective-permute-start.8 = (f32[256,256]{1,0:T(8,128)S(1)}, f32[256,256]{1,0:T(8,128)S(1)}, u32[]{:S(2)}, u32[]{:S(2)}) collective-permute-start(f32[256,256]{1,0:T(8,128)S(1)} %add_select_fusion.2), channel_id=1, source_target_pairs={{0,1},{1,0},{2,3},{3,2},{4,5},{5,4},{6,7},{7,6},{8,9},{9,8},{10,11... | collective-permute-start | bytes 786440 | tf_op jit(solution)/shard_map/ppermute | solution.py:27
  90.6 6.3 %collective-permute-start.10 = (f32[256,256]{1,0:T(8,128)S(1)}, f32[256,256]{1,0:T(8,128)S(1)}, u32[]{:S(2)}, u32[]{:S(2)}) collective-permute-start(f32[256,256]{1,0:T(8,128)S(1)} %add_select_fusion.1), channel_id=1, source_target_pairs={{0,1},{1,0},{2,3},{3,2},{4,5},{5,4},{6,7},{7,6},{8,9},{9,8},{10,11... | collective-permute-start | bytes 786440 | tf_op jit(solution)/shard_map/ppermute | solution.py:27
  98.3 3.1 %collective-permute-done.15.refs_4_ = f32[256,256]{1,0:T(8,128)S(1)} collective-permute-done((f32[256,256]{1,0:T(8,128)S(1)}, f32[256,256]{1,0:T(8,128)S(1)}, u32[]{:S(2)}, u32[]{:S(2)}) %collective-permute-start.15) | collective-permute-done | bytes 262176 | tf_op jit(solution)/shard_map/ppermute | solution.py:27
  102.1 2.1 %collective-permute-done.10.refs_7_ = f32[256,256]{1,0:T(8,128)S(1)} collective-permute-done((f32[256,256]{1,0:T(8,128)S(1)}, f32[256,256]{1,0:T(8,128)S(1)}, u32[]{:S(2)}, u32[]{:S(2)}) %collective-permute-start.10) | collective-permute-done | bytes 262176 | tf_op jit(solution)/shard_map/ppermute | solution.py:27
  105.0 5.3 %collective-permute-start.17 = (f32[256,256]{1,0:T(8,128)S(1)}, f32[256,256]{1,0:T(8,128)S(1)}, u32[]{:S(2)}, u32[]{:S(2)}) collective-permute-start(f32[256,256]{1,0:T(8,128)S(1)} %add.94), channel_id=1, source_target_pairs={{0,1},{1,0},{2,3},{3,2},{4,5},{5,4},{6,7},{7,6},{8,9},{9,8},{10,11... | collective-permute-start | bytes 786440 | tf_op jit(solution)/shard_map/ppermute | solution.py:27
  110.4 3.2 %collective-permute-start.21 = (f32[256,256]{1,0:T(8,128)S(1)}, f32[256,256]{1,0:T(8,128)S(1)}, u32[]{:S(2)}, u32[]{:S(2)}) collective-permute-start(f32[256,256]{1,0:T(8,128)S(1)} %add.98), channel_id=1, source_target_pairs={{0,1},{1,0},{2,3},{3,2},{4,5},{5,4},{6,7},{7,6},{8,9},{9,8},{10,11... | collective-permute-start | bytes 786440 | tf_op jit(solution)/shard_map/ppermute | solution.py:27
  113.7 2.8 %collective-permute-start.19 = (f32[256,256]{1,0:T(8,128)S(1)}, f32[256,256]{1,0:T(8,128)S(1)}, u32[]{:S(2)}, u32[]{:S(2)}) collective-permute-start(f32[256,256]{1,0:T(8,128)S(1)} %add.96), channel_id=1, source_target_pairs={{0,1},{1,0},{2,3},{3,2},{4,5},{5,4},{6,7},{7,6},{8,9},{9,8},{10,11... | collective-permute-start | bytes 786440 | tf_op jit(solution)/shard_map/ppermute | solution.py:27
  117.1 1.9 %shard_map.96 = (f32[4,32,128]{2,1,0:T(8,128)S(1)}, f32[4,32,128]{2,1,0:T(8,128)S(1)}, f32[4,32,128]{2,1,0:T(8,128)S(1)}, f32[4,32,128]{2,1,0:T(8,128)S(1)}) custom-call(s32[4]{0:T(128)} %pad_add_fusion.dest, f32[256,256]{1,0:T(8,128)} %copy-done.11, f32[256,256]{1,0:T(8,128)} %copy-done.10, f32[256,256]{1,0:T(8,128)} %copy-done.14, f32[256,256]{1,0:T(8,128)} %copy-done.16, ...), custom_call_target="tpu_custom_call" | custom-call | flops 134217728 | bytes 2097152 | tf_op jit(solution)/shard_map/pallas_call | solution.py:109
  119.6 4.2 %collective-permute-start.12 = (f32[4,32,128]{2,1,0:T(8,128)S(1)}, f32[4,32,128]{2,1,0:T(8,128)S(1)}, u32[]{:S(2)}, u32[]{:S(2)}) collective-permute-start(f32[4,32,128]{2,1,0:T(8,128)S(1)} %get-tuple-element.42), channel_id=1, source_target_pairs={{0,2},{3,1},{4,6},{7,5},{8,10},{11,9},{12,14},{15,13},{16,18},{19,... | collective-permute-start | bytes 196616 | tf_op jit(solution)/shard_map/ppermute | solution.py:27
  123.8 4.0 %collective-permute-start.13 = (f32[4,32,128]{2,1,0:T(8,128)S(1)}, f32[4,32,128]{2,1,0:T(8,128)S(1)}, u32[]{:S(2)}, u32[]{:S(2)}) collective-permute-start(f32[4,32,128]{2,1,0:T(8,128)S(1)} %get-tuple-element.43), channel_id=1, source_target_pairs={{0,3},{3,0},{4,7},{7,4},{8,11},{11,8},{12,15},{15,12},{16,19},{19,... | collective-permute-start | bytes 196616 | tf_op jit(solution)/shard_map/ppermute | solution.py:27
  129.2 1.9 %shard_map.97 = (f32[4,32,128]{2,1,0:T(8,128)S(1)}, f32[4,32,128]{2,1,0:T(8,128)S(1)}, f32[4,32,128]{2,1,0:T(8,128)S(1)}, f32[4,32,128]{2,1,0:T(8,128)S(1)}) custom-call(s32[4]{0:T(128)} %pad_add_fusion.dest, f32[256,256]{1,0:T(8,128)} %copy-done.12, f32[256,256]{1,0:T(8,128)} %copy-done.7, f32[256,256]{1,0:T(8,128)} %copy-done.8, f32[256,256]{1,0:T(8,128)} %copy-done.9, ...), custom_call_target="tpu_custom_call" | custom-call | flops 134217728 | bytes 2097152 | tf_op jit(solution)/shard_map/pallas_call | solution.py:109
  131.7 4.2 %collective-permute-start.23 = (f32[4,32,128]{2,1,0:T(8,128)S(1)}, f32[4,32,128]{2,1,0:T(8,128)S(1)}, u32[]{:S(2)}, u32[]{:S(2)}) collective-permute-start(f32[4,32,128]{2,1,0:T(8,128)S(1)} %get-tuple-element.51), channel_id=1, source_target_pairs={{0,2},{3,1},{4,6},{7,5},{8,10},{11,9},{12,14},{15,13},{16,18},{19,... | collective-permute-start | bytes 196616 | tf_op jit(solution)/shard_map/ppermute | solution.py:27
  135.9 4.0 %collective-permute-start.24 = (f32[4,32,128]{2,1,0:T(8,128)S(1)}, f32[4,32,128]{2,1,0:T(8,128)S(1)}, u32[]{:S(2)}, u32[]{:S(2)}) collective-permute-start(f32[4,32,128]{2,1,0:T(8,128)S(1)} %get-tuple-element.52), channel_id=1, source_target_pairs={{0,3},{3,0},{4,7},{7,4},{8,11},{11,8},{12,15},{15,12},{16,19},{19,... | collective-permute-start | bytes 196616 | tf_op jit(solution)/shard_map/ppermute | solution.py:27
  140.6 3.3 %collective-permute-done.24.refs_7_ = f32[4,32,128]{2,1,0:T(8,128)S(1)} collective-permute-done((f32[4,32,128]{2,1,0:T(8,128)S(1)}, f32[4,32,128]{2,1,0:T(8,128)S(1)}, u32[]{:S(2)}, u32[]{:S(2)}) %collective-permute-start.24) | collective-permute-done | bytes 65568 | tf_op jit(solution)/shard_map/ppermute | solution.py:27
  144.5 6.3 %shard_map.98 = f32[8,256]{1,0:T(8,128)} custom-call(s32[2]{0:T(128)} %add_convert_fusion.place, f32[4,32,128]{2,1,0:T(8,128)} %copy-done.23, f32[4,32,128]{2,1,0:T(8,128)} %copy-done.33, f32[4,32,128]{2,1,0:T(8,128)} %copy-done.34, f32[4,32,128]{2,1,0:T(8,128)} %copy-done.35, f32[4,32,128]{2,1,0:T(8,128)} %copy-done.24, f32[4,32,128]{2,1,0:T(8,128)} %copy-done.36, ...), custom_call_target="tpu_custom_call" | custom-call | flops 134217728 | bytes 8388608 | tf_op jit(solution)/shard_map/pallas_call | solution.py:170
  150.8 11.3 %psum.7 = f32[8,256]{1,0:T(8,128)} all-reduce(f32[8,256]{1,0:T(8,128)} %shard_map.98), channel_id=1, replica_groups=mesh['parts'=2,'dp'=4,'tensor'=4] {'tensor'}, use_global_device_ids=true, to_apply=%region_0.1 | all-reduce | flops 2048 | bytes 16384 | tf_op jit(solution)/shard_map/psum | solution.py:234
  (131 shorter events, 16.3 us)
Async XLA Ops:
  6.5 137.4 %all-gather.2.cloned.1.call-start = ((), (), s32[]{:S(2)}) async-start(), calls=%async_computation | async-start | bytes 10485760 | tf_op jit(solution)/shard_map/all_gather | solution.py:199
  19.7 39.3 %copy-start.10 = (f32[256,256]{1,0:T(8,128)}, f32[256,256]{1,0:T(8,128)S(1)}, u32[]{:S(2)}) copy-start(f32[256,256]{1,0:T(8,128)S(1)} %get-tuple-element.30.refs_1_) | copy-start | bytes 786436
  19.7 22.4 %collective-permute-start.3 = (f32[256,256]{1,0:T(8,128)}, f32[256,256]{1,0:T(8,128)}, u32[]{:S(2)}, u32[]{:S(2)}) collective-permute-start(f32[256,256]{1,0:T(8,128)} %get-tuple-element.36), channel_id=1, source_target_pairs={{0,1},{1,0},{2,3},{3,2},{4,5},{5,4},{6,7},{7,6},{8,9},{9,8},{10,11... | collective-permute-start | bytes 786440 | tf_op jit(solution)/shard_map/ppermute | solution.py:27
  30.1 34.6 %copy-start.11 = (f32[256,256]{1,0:T(8,128)}, f32[256,256]{1,0:T(8,128)S(1)}, u32[]{:S(2)}) copy-start(f32[256,256]{1,0:T(8,128)S(1)} %get-tuple-element.29.refs_0_) | copy-start | bytes 786436
  30.1 15.1 %collective-permute-start = (f32[256,256]{1,0:T(8,128)}, f32[256,256]{1,0:T(8,128)}, u32[]{:S(2)}, u32[]{:S(2)}) collective-permute-start(f32[256,256]{1,0:T(8,128)} %get-tuple-element.34), channel_id=1, source_target_pairs={{0,1},{1,0},{2,3},{3,2},{4,5},{5,4},{6,7},{7,6},{8,9},{9,8},{10,11... | collective-permute-start | bytes 786440 | tf_op jit(solution)/shard_map/ppermute | solution.py:27
  40.3 25.6 %collective-permute-start.6 = (f32[256,256]{1,0:T(8,128)}, f32[256,256]{1,0:T(8,128)}, u32[]{:S(2)}, u32[]{:S(2)}) collective-permute-start(f32[256,256]{1,0:T(8,128)} %get-tuple-element.38), channel_id=1, source_target_pairs={{0,1},{1,0},{2,3},{3,2},{4,5},{5,4},{6,7},{7,6},{8,9},{9,8},{10,11... | collective-permute-start | bytes 786440 | tf_op jit(solution)/shard_map/ppermute | solution.py:27
  43.8 15.2 %collective-permute-start.4 = (f32[256,256]{1,0:T(8,128)}, f32[256,256]{1,0:T(8,128)}, u32[]{:S(2)}, u32[]{:S(2)}) collective-permute-start(f32[256,256]{1,0:T(8,128)} %add.85), channel_id=1, source_target_pairs={{1,2},{2,1},{5,6},{6,5},{9,10},{10,9},{13,14},{14,13},{17,18},{18,... | collective-permute-start | bytes 786440 | tf_op jit(solution)/shard_map/ppermute | solution.py:27
  47.0 26.9 %copy-start.3 = (bf16[128,7168]{1,0:T(8,128)(2,1)S(1)}, bf16[128,7168]{1,0:T(8,128)(2,1)}, u32[]{:S(2)}) copy-start(bf16[128,7168]{1,0:T(8,128)(2,1)} %p_left.9) | copy-start | bytes 5505028
  47.0 17.7 %collective-permute-start.1 = (f32[256,256]{1,0:T(8,128)}, f32[256,256]{1,0:T(8,128)}, u32[]{:S(2)}, u32[]{:S(2)}) collective-permute-start(f32[256,256]{1,0:T(8,128)} %add.83), channel_id=1, source_target_pairs={{1,2},{2,1},{5,6},{6,5},{9,10},{10,9},{13,14},{14,13},{17,18},{18,... | collective-permute-start | bytes 786440 | tf_op jit(solution)/shard_map/ppermute | solution.py:27
  59.0 46.0 %copy-start.7 = (f32[256,256]{1,0:T(8,128)}, f32[256,256]{1,0:T(8,128)S(1)}, u32[]{:S(2)}) copy-start(f32[256,256]{1,0:T(8,128)S(1)} %get-tuple-element.45.refs_1_) | copy-start | bytes 786436
  60.3 11.6 %collective-permute-start.5 = (f32[256,256]{1,0:T(8,128)S(1)}, f32[256,256]{1,0:T(8,128)S(1)}, u32[]{:S(2)}, u32[]{:S(2)}) collective-permute-start(f32[256,256]{1,0:T(8,128)S(1)} %add_select_fusion.3), channel_id=1, source_target_pairs={{0,1},{1,0},{2,3},{3,2},{4,5},{5,4},{6,7},{7,6},{8,9},{9,8},{10,11... | collective-permute-start | bytes 786440 | tf_op jit(solution)/shard_map/ppermute | solution.py:27
  65.8 17.2 %collective-permute-start.2 = (f32[256,256]{1,0:T(8,128)S(1)}, f32[256,256]{1,0:T(8,128)S(1)}, u32[]{:S(2)}, u32[]{:S(2)}) collective-permute-start(f32[256,256]{1,0:T(8,128)S(1)} %add_select_fusion.4), channel_id=1, source_target_pairs={{0,1},{1,0},{2,3},{3,2},{4,5},{5,4},{6,7},{7,6},{8,9},{9,8},{10,11... | collective-permute-start | bytes 786440 | tf_op jit(solution)/shard_map/ppermute | solution.py:27
  67.0 16.8 %collective-permute-start.7 = (f32[256,256]{1,0:T(8,128)S(1)}, f32[256,256]{1,0:T(8,128)S(1)}, u32[]{:S(2)}, u32[]{:S(2)}) collective-permute-start(f32[256,256]{1,0:T(8,128)S(1)} %add.87), channel_id=1, source_target_pairs={{1,2},{2,1},{5,6},{6,5},{9,10},{10,9},{13,14},{14,13},{17,18},{18,... | collective-permute-start | bytes 786440 | tf_op jit(solution)/shard_map/ppermute | solution.py:27
  73.1 17.3 %collective-permute-start.14 = (f32[256,256]{1,0:T(8,128)S(1)}, f32[256,256]{1,0:T(8,128)S(1)}, u32[]{:S(2)}, u32[]{:S(2)}) collective-permute-start(f32[256,256]{1,0:T(8,128)S(1)} %add.91), channel_id=1, source_target_pairs={{1,2},{2,1},{5,6},{6,5},{9,10},{10,9},{13,14},{14,13},{17,18},{18,... | collective-permute-start | bytes 786440 | tf_op jit(solution)/shard_map/ppermute | solution.py:27
  82.9 44.9 %copy-start.8 = (f32[256,256]{1,0:T(8,128)}, f32[256,256]{1,0:T(8,128)S(1)}, u32[]{:S(2)}) copy-start(f32[256,256]{1,0:T(8,128)S(1)} %get-tuple-element.46.refs_2_) | copy-start | bytes 786436
  83.0 44.9 %copy-start.9 = (f32[256,256]{1,0:T(8,128)}, f32[256,256]{1,0:T(8,128)S(1)}, u32[]{:S(2)}) copy-start(f32[256,256]{1,0:T(8,128)S(1)} %get-tuple-element.47.refs_3_) | copy-start | bytes 786436
  83.0 7.5 %collective-permute-start.9 = (f32[256,256]{1,0:T(8,128)S(1)}, f32[256,256]{1,0:T(8,128)S(1)}, u32[]{:S(2)}, u32[]{:S(2)}) collective-permute-start(f32[256,256]{1,0:T(8,128)S(1)} %add.89), channel_id=1, source_target_pairs={{1,2},{2,1},{5,6},{6,5},{9,10},{10,9},{13,14},{14,13},{17,18},{18,... | collective-permute-start | bytes 786440 | tf_op jit(solution)/shard_map/ppermute | solution.py:27
  83.8 13.8 %collective-permute-start.8 = (f32[256,256]{1,0:T(8,128)S(1)}, f32[256,256]{1,0:T(8,128)S(1)}, u32[]{:S(2)}, u32[]{:S(2)}) collective-permute-start(f32[256,256]{1,0:T(8,128)S(1)} %add_select_fusion.2), channel_id=1, source_target_pairs={{0,1},{1,0},{2,3},{3,2},{4,5},{5,4},{6,7},{7,6},{8,9},{9,8},{10,11... | collective-permute-start | bytes 786440 | tf_op jit(solution)/shard_map/ppermute | solution.py:27
  90.5 11.0 %collective-permute-start.15 = (f32[256,256]{1,0:T(8,128)S(1)}, f32[256,256]{1,0:T(8,128)S(1)}, u32[]{:S(2)}, u32[]{:S(2)}) collective-permute-start(f32[256,256]{1,0:T(8,128)S(1)} %add_select_fusion), channel_id=1, source_target_pairs={{0,1},{1,0},{2,3},{3,2},{4,5},{5,4},{6,7},{7,6},{8,9},{9,8},{10,11... | collective-permute-start | bytes 786440 | tf_op jit(solution)/shard_map/ppermute | solution.py:27
  90.6 13.6 %collective-permute-start.10 = (f32[256,256]{1,0:T(8,128)S(1)}, f32[256,256]{1,0:T(8,128)S(1)}, u32[]{:S(2)}, u32[]{:S(2)}) collective-permute-start(f32[256,256]{1,0:T(8,128)S(1)} %add_select_fusion.1), channel_id=1, source_target_pairs={{0,1},{1,0},{2,3},{3,2},{4,5},{5,4},{6,7},{7,6},{8,9},{9,8},{10,11... | collective-permute-start | bytes 786440 | tf_op jit(solution)/shard_map/ppermute | solution.py:27
  97.7 7.3 %collective-permute-start.16 = (f32[256,256]{1,0:T(8,128)S(1)}, f32[256,256]{1,0:T(8,128)S(1)}, u32[]{:S(2)}, u32[]{:S(2)}) collective-permute-start(f32[256,256]{1,0:T(8,128)S(1)} %add.93), channel_id=1, source_target_pairs={{1,2},{2,1},{5,6},{6,5},{9,10},{10,9},{13,14},{14,13},{17,18},{18,... | collective-permute-start | bytes 786440 | tf_op jit(solution)/shard_map/ppermute | solution.py:27
  101.4 8.9 %collective-permute-start.20 = (f32[256,256]{1,0:T(8,128)S(1)}, f32[256,256]{1,0:T(8,128)S(1)}, u32[]{:S(2)}, u32[]{:S(2)}) collective-permute-start(f32[256,256]{1,0:T(8,128)S(1)} %add.97), channel_id=1, source_target_pairs={{1,2},{2,1},{5,6},{6,5},{9,10},{10,9},{13,14},{14,13},{17,18},{18,... | collective-permute-start | bytes 786440 | tf_op jit(solution)/shard_map/ppermute | solution.py:27
  104.3 9.4 %collective-permute-start.18 = (f32[256,256]{1,0:T(8,128)S(1)}, f32[256,256]{1,0:T(8,128)S(1)}, u32[]{:S(2)}, u32[]{:S(2)}) collective-permute-start(f32[256,256]{1,0:T(8,128)S(1)} %add.95), channel_id=1, source_target_pairs={{1,2},{2,1},{5,6},{6,5},{9,10},{10,9},{13,14},{14,13},{17,18},{18,... | collective-permute-start | bytes 786440 | tf_op jit(solution)/shard_map/ppermute | solution.py:27
  105.0 18.8 %collective-permute-start.17 = (f32[256,256]{1,0:T(8,128)S(1)}, f32[256,256]{1,0:T(8,128)S(1)}, u32[]{:S(2)}, u32[]{:S(2)}) collective-permute-start(f32[256,256]{1,0:T(8,128)S(1)} %add.94), channel_id=1, source_target_pairs={{0,1},{1,0},{2,3},{3,2},{4,5},{5,4},{6,7},{7,6},{8,9},{9,8},{10,11... | collective-permute-start | bytes 786440 | tf_op jit(solution)/shard_map/ppermute | solution.py:27
  110.4 17.4 %collective-permute-start.21 = (f32[256,256]{1,0:T(8,128)S(1)}, f32[256,256]{1,0:T(8,128)S(1)}, u32[]{:S(2)}, u32[]{:S(2)}) collective-permute-start(f32[256,256]{1,0:T(8,128)S(1)} %add.98), channel_id=1, source_target_pairs={{0,1},{1,0},{2,3},{3,2},{4,5},{5,4},{6,7},{7,6},{8,9},{9,8},{10,11... | collective-permute-start | bytes 786440 | tf_op jit(solution)/shard_map/ppermute | solution.py:27
  113.7 14.1 %collective-permute-start.19 = (f32[256,256]{1,0:T(8,128)S(1)}, f32[256,256]{1,0:T(8,128)S(1)}, u32[]{:S(2)}, u32[]{:S(2)}) collective-permute-start(f32[256,256]{1,0:T(8,128)S(1)} %add.96), channel_id=1, source_target_pairs={{0,1},{1,0},{2,3},{3,2},{4,5},{5,4},{6,7},{7,6},{8,9},{9,8},{10,11... | collective-permute-start | bytes 786440 | tf_op jit(solution)/shard_map/ppermute | solution.py:27
  119.6 16.3 %collective-permute-start.11 = (f32[4,32,128]{2,1,0:T(8,128)S(1)}, f32[4,32,128]{2,1,0:T(8,128)S(1)}, u32[]{:S(2)}, u32[]{:S(2)}) collective-permute-start(f32[4,32,128]{2,1,0:T(8,128)S(1)} %get-tuple-element.41), channel_id=1, source_target_pairs={{0,1},{1,0},{2,3},{3,2},{4,5},{5,4},{6,7},{7,6},{8,9},{9,8},{10,11... | collective-permute-start | bytes 196616 | tf_op jit(solution)/shard_map/ppermute | solution.py:27
  119.6 20.9 %collective-permute-start.12 = (f32[4,32,128]{2,1,0:T(8,128)S(1)}, f32[4,32,128]{2,1,0:T(8,128)S(1)}, u32[]{:S(2)}, u32[]{:S(2)}) collective-permute-start(f32[4,32,128]{2,1,0:T(8,128)S(1)} %get-tuple-element.42), channel_id=1, source_target_pairs={{0,2},{3,1},{4,6},{7,5},{8,10},{11,9},{12,14},{15,13},{16,18},{19,... | collective-permute-start | bytes 196616 | tf_op jit(solution)/shard_map/ppermute | solution.py:27
  123.8 16.7 %collective-permute-start.13 = (f32[4,32,128]{2,1,0:T(8,128)S(1)}, f32[4,32,128]{2,1,0:T(8,128)S(1)}, u32[]{:S(2)}, u32[]{:S(2)}) collective-permute-start(f32[4,32,128]{2,1,0:T(8,128)S(1)} %get-tuple-element.43), channel_id=1, source_target_pairs={{0,3},{3,0},{4,7},{7,4},{8,11},{11,8},{12,15},{15,12},{16,19},{19,... | collective-permute-start | bytes 196616 | tf_op jit(solution)/shard_map/ppermute | solution.py:27
  131.7 8.8 %collective-permute-start.22 = (f32[4,32,128]{2,1,0:T(8,128)S(1)}, f32[4,32,128]{2,1,0:T(8,128)S(1)}, u32[]{:S(2)}, u32[]{:S(2)}) collective-permute-start(f32[4,32,128]{2,1,0:T(8,128)S(1)} %get-tuple-element.50), channel_id=1, source_target_pairs={{0,1},{1,0},{2,3},{3,2},{4,5},{5,4},{6,7},{7,6},{8,9},{9,8},{10,11... | collective-permute-start | bytes 196616 | tf_op jit(solution)/shard_map/ppermute | solution.py:27
  131.7 8.9 %collective-permute-start.23 = (f32[4,32,128]{2,1,0:T(8,128)S(1)}, f32[4,32,128]{2,1,0:T(8,128)S(1)}, u32[]{:S(2)}, u32[]{:S(2)}) collective-permute-start(f32[4,32,128]{2,1,0:T(8,128)S(1)} %get-tuple-element.51), channel_id=1, source_target_pairs={{0,2},{3,1},{4,6},{7,5},{8,10},{11,9},{12,14},{15,13},{16,18},{19,... | collective-permute-start | bytes 196616 | tf_op jit(solution)/shard_map/ppermute | solution.py:27
  135.9 8.0 %collective-permute-start.24 = (f32[4,32,128]{2,1,0:T(8,128)S(1)}, f32[4,32,128]{2,1,0:T(8,128)S(1)}, u32[]{:S(2)}, u32[]{:S(2)}) collective-permute-start(f32[4,32,128]{2,1,0:T(8,128)S(1)} %get-tuple-element.52), channel_id=1, source_target_pairs={{0,3},{3,0},{4,7},{7,4},{8,11},{11,8},{12,15},{15,12},{16,19},{19,... | collective-permute-start | bytes 196616 | tf_op jit(solution)/shard_map/ppermute | solution.py:27
  (33 other events, 270.7 us)
Sparse Core Ops, SparseCore 0:
  10.8 60.9 all-gather.1

commit v2 on v0

v2 whole, which is shorter than its diff:
```python
import functools

import jax
import jax.numpy as jnp
from jax import lax
from jax.experimental import pallas as pl
from jax.experimental.pallas import tpu as pltpu
from jax.sharding import PartitionSpec as P

K = 128
LEN = 256
PIECE = 1024
AHEAD = 4
ROWS_BY_ROWS = (((1,), (1,)), ((), ()))
NEAR = [(0, 1), (1, 0), (2, 3), (3, 2)]
SKIP = [(0, 2), (2, 0), (1, 3), (3, 1)]
ACROSS = [(0, 3), (3, 0), (1, 2), (2, 1)]

WHOLE = pl.BlockSpec(memory_space=pltpu.VMEM)
SCALARS = pl.BlockSpec(memory_space=pltpu.SMEM)
OUTSIDE = pl.BlockSpec(memory_space=pltpu.HBM)


def here(x):
    return pltpu.with_memory_space_constraint(x, pltpu.VMEM)


def there(x):
    return pltpu.with_memory_space_constraint(x, pltpu.HBM)


def send(x, pairs, axis="tensor"):
    return lax.ppermute(x, axis, pairs)


def halves(x):
    high = x.astype(jnp.bfloat16)
    return high, (x - high.astype(jnp.float32)).astype(jnp.bfloat16)


def pieces(width):
    return [(lo, min(lo + PIECE, width)) for lo in range(0, width, PIECE)]


def project_kernel(shapes, load, spread, index, left, right, p_left, p_right, *refs):
    moves = []
    if spread:
        queries, refs = refs[0], refs[1:]
        flat, spread_sem = refs[len(shapes)], refs[-1]
        refs = refs[: len(shapes)] + refs[len(shapes) + 1 : -1]
        for r in range(queries.shape[1]):
            moves.append(
                pltpu.make_async_copy(
                    queries.at[:, r, :], flat.at[:, r * K : (r + 1) * K], spread_sem.at[r]
                )
            )
    arrays, (slots, sem, *loaded) = refs[: len(shapes)], refs[len(shapes) :]
    outs = [array.at[i] for array, n in zip(arrays, shapes) for i in range(n)]
    depth = slots.shape[0]
    steps = []
    for first in range(0, len(outs), 2):
        group = range(first, min(first + 2, len(outs)))
        for side, (x, p, row) in enumerate(((left, p_left, 0), (right, p_right, K))):
            for lo, hi in pieces(x.shape[1]):
                slot = len(steps) % depth
                copies = [
                    pltpu.make_async_copy(
                        x.at[pl.ds(pl.multiple_of(index[i] * LEN, LEN), LEN), lo:hi],
                        slots.at[slot, n * LEN : (n + 1) * LEN, : hi - lo],
                        sem.at[slot, n],
                    )
                    for n, i in enumerate(group)
                ]
                if load and first == 0:
                    copies.append(
                        pltpu.make_async_copy(
                            p.at[:, lo:hi], loaded[side].at[:, lo:hi], sem.at[slot, 2]
                        )
                    )
                steps.append((copies, slot, group, loaded[side] if load else p, row, lo, hi))
    for step in steps[: depth - 1]:
        for copy in step[0]:
            copy.start()
    for move in moves:
        move.start()
    for n, (copies, slot, group, p, row, lo, hi) in enumerate(steps):
        for copy in copies:
            copy.wait()
        if n + depth - 1 < len(steps):
            for copy in steps[n + depth - 1][0]:
                copy.start()
        part = lax.dot_general(
            p[:, lo:hi],
            slots[slot, : len(group) * LEN, : hi - lo],
            ROWS_BY_ROWS,
            preferred_element_type=jnp.float32,
        )
        for m, i in enumerate(group):
            if lo == 0:
                outs[i][row : row + K, :] = part[:, m * LEN : (m + 1) * LEN]
            else:
                outs[i][row : row + K, :] += part[:, m * LEN : (m + 1) * LEN]
    for move in moves:
        move.wait()


def project(groups, left, right, p_left, p_right, load=False, after=None, queries=None):
    shapes = [len(group) for group in groups]
    index = jnp.stack([i for group in groups for i in group]).astype(jnp.int32)
    if after is not None:
        index = lax.optimization_barrier((index, after))[0]
    widths = left.shape[1], right.shape[1]
    rows = sum(shapes) * LEN
    place = there if load else here
    scratch = [
        pltpu.VMEM((AHEAD + 1, 2 * LEN, PIECE), left.dtype),
        pltpu.SemaphoreType.DMA((AHEAD + 1, 3)),
    ]
    if load:
        scratch += [pltpu.VMEM((K, w), left.dtype) for w in widths]
    p_spec = OUTSIDE if load else WHOLE
    more_in, more_out = [], []
    if queries is not None:
        more_in = [there(queries)]
        count, per_query, _ = queries.shape
        more_out = [pltpu.VMEM((count, per_query * K), queries.dtype)]
        scratch += [pltpu.SemaphoreType.DMA((per_query,))]
    return pl.pallas_call(
        functools.partial(project_kernel, shapes, load, queries is not None),
        in_specs=[SCALARS, OUTSIDE, OUTSIDE, p_spec, p_spec] + [OUTSIDE] * len(more_in),
        out_specs=[WHOLE] * (len(shapes) + len(more_out)),
        out_shape=[pltpu.VMEM((n, 2 * K, LEN), jnp.float32) for n in shapes] + more_out,
        scratch_shapes=scratch,
        compiler_params=pltpu.CompilerParams(vmem_limit_bytes=16 * 2**20),
        cost_estimate=pl.CostEstimate(
            flops=2 * rows * K * sum(widths), bytes_accessed=2 * rows * sum(widths), transcendentals=0
        ),
    )(index, there(left), there(right), place(p_left), place(p_right), *more_in)


def sketch_kernel(count, width, dest, *refs):
    own, first, second, outs, full = (
        refs[:count],
        refs[count : 2 * count],
        refs[2 * count : 3 * count],
        refs[3 * count : -1],
        refs[-1],
    )
    for i in range(count):
        high, low = halves(own[i][0] + first[i][0] + second[i][...])
        a = jnp.concatenate([high[:K], low[:K]], 0)
        b = jnp.concatenate([high[K:], low[K:]], 0)
        s = lax.dot_general(a, b, ROWS_BY_ROWS, preferred_element_type=jnp.float32)
        full[...] = s[:K, :K] + (s[:K, K:] + s[K:, :K] + s[K:, K:])
        for n, out in enumerate(outs):
            out[i] = full[pl.ds(pl.multiple_of(dest[n] * width, 8), width), :]


def sketches(dest, own, first, second, width):
    count = len(own)
    return pl.pallas_call(
        functools.partial(sketch_kernel, count, width),
        in_specs=[SCALARS] + [WHOLE] * (3 * count),
        out_specs=[WHOLE] * 4,
        out_shape=[pltpu.VMEM((count, width, K), jnp.float32)] * 4,
        scratch_shapes=[pltpu.VMEM((K, K), jnp.float32)],
        cost_estimate=pl.CostEstimate(
            flops=8 * count * LEN * K * K, bytes_accessed=count * 2**19, transcendentals=0
        ),
    )(dest, *own, *first, *second)


def split_kernel(place, mine, other, high, low):
    count, depth = mine.shape
    for n, x in enumerate((mine, other)):
        at = pl.ds(pl.multiple_of((place[0] ^ n) * count, 16), count)
        for lo in range(0, depth, 512):
            h, l = halves(x[:, lo : lo + 512])
            high[at, lo : lo + 512] = h
            low[at, lo : lo + 512] = l


def split(core, mine, other, after=None):
    count, depth = mine.shape
    if after is not None:
        core = lax.optimization_barrier((core, after))[0]
    return pl.pallas_call(
        split_kernel,
        in_specs=[SCALARS, WHOLE, WHOLE],
        out_specs=[WHOLE] * 2,
        out_shape=[pltpu.VMEM((2 * count, depth), jnp.bfloat16)] * 2,
        compiler_params=pltpu.CompilerParams(vmem_limit_bytes=16 * 2**20),
        cost_estimate=pl.CostEstimate(
            flops=8 * count * depth, bytes_accessed=16 * count * depth, transcendentals=0
        ),
    )(core, mine, other)


def score_kernel(pair, place, own, near, skip, across, *refs):
    parts, out, cat = refs[:4], refs[4], refs[5]
    z, chip = place[0], place[1]
    width = own.shape[1]
    count = 4 * pair
    for layer in range(2):
        for r in range(width):
            lanes = slice((layer * width + r) * K, (layer * width + r + 1) * K)
            mine = slice(layer * pair, (layer + 1) * pair)
            cut = [x[mine, r, :] for x in (own, near, skip, across)]
            for b in range(4):
                pick = jnp.where(z == b ^ 2, cut[2], jnp.where(z == 3 - b, cut[3], cut[0]))
                high, low = halves(jnp.where(z == b ^ 1, cut[1], pick))
                cat[b * pair : (b + 1) * pair, lanes] = high.astype(jnp.float32)
                cat[count + b * pair : count + (b + 1) * pair, lanes] = low.astype(jnp.float32)
    s = cat[...].astype(jnp.bfloat16)
    totals = []
    for high, low in (parts[:2], parts[2:]):
        d = lax.dot_general(s, high[...], ROWS_BY_ROWS, preferred_element_type=jnp.float32)
        d += lax.dot_general(s, low[...], ROWS_BY_ROWS, preferred_element_type=jnp.float32)
        totals.append((d[:count] + d[count:]) * (1.0 / (LEN**0.5 * K)))
    mine, other = totals
    out[...] = jnp.concatenate(
        [jnp.where(chip == 0, mine, other), jnp.where(chip == 0, other, mine)], 1
    )


def score(place, cuts, parts, pair):
    queries, depth = parts[0].shape
    return pl.pallas_call(
        functools.partial(score_kernel, pair),
        in_specs=[SCALARS] + [WHOLE] * 8,
        out_specs=WHOLE,
        out_shape=pltpu.VMEM((4 * pair, 2 * queries), jnp.float32),
        scratch_shapes=[pltpu.VMEM((8 * pair, depth), jnp.float32)],
        compiler_params=pltpu.CompilerParams(vmem_limit_bytes=24 * 2**20),
        cost_estimate=pl.CostEstimate(
            flops=64 * queries * depth, bytes_accessed=8 * queries * depth, transcendentals=0
        ),
    )(place, *cuts, *parts)


def line(
    layer_input, up_grad, hidden_input, down_grad, in_up, out_up, in_down, out_down, query_sketch
):
    pair = layer_input.shape[0] // LEN // 4
    width = K // 4
    z = lax.axis_index("tensor").astype(jnp.int32)
    dp = lax.axis_index("dp").astype(jnp.int32)
    up = (layer_input, up_grad, in_up, out_up)
    down = (hidden_input, down_grad, in_down, out_down)

    def of(owner, j):
        return owner * pair + j

    def leaving(j):
        return [of(z ^ 1, j), of(z ^ 2, j)]

    def staying(j):
        return [of(z, j), of(3 - z, j)]

    queries = query_sketch.reshape(query_sketch.shape[0], -1, K)
    by_core = [(0, 1), (1, 0), (2, 3), (3, 2)]
    by_chip = [(0, 2), (2, 0), (1, 3), (3, 1)]
    core = (dp & 1).reshape(1)

    def across(stay, first, after=None):
        if after is not None:
            stay = lax.optimization_barrier((stay, after))[0]
        return stay[1] + first[1]

    (out_0,) = project([leaving(0)], *up, load=True)
    first_0 = send(out_0, NEAR)
    out_1, flat = project([leaving(1)], *up, after=out_0, queries=queries)
    first_1 = send(out_1, NEAR)
    other_core = send(flat, by_core, "dp")
    other_chip = send(flat, by_chip, "dp")
    stay_0, stay_1 = project([staying(0), staying(1)], *up, after=(out_1, first_0))
    sum_0 = across(stay_0, first_0)
    second_0 = send(sum_0, ACROSS)
    sum_1 = across(stay_1, first_1)
    second_1 = send(sum_1, ACROSS)
    out_2, stay_2 = project([leaving(0), staying(0)], *down, after=(sum_0, sum_1))
    first_2 = send(out_2, NEAR)
    out_3, stay_3 = project([leaving(1), staying(1)], *down, after=(out_2, second_0))
    first_3 = send(out_3, NEAR)
    sum_2 = across(stay_2, first_2, (out_3, second_1))
    second_2 = send(sum_2, ACROSS)
    own_chip = split(core, flat, other_core, after=sum_2)
    sum_3 = across(stay_3, first_3, own_chip[0])
    second_3 = send(sum_3, ACROSS)
    other_chip = lax.optimization_barrier((other_chip, sum_3))[0]
    other_both = send(other_chip, by_core, "dp")
    parts = own_chip + split(core, other_chip, other_both, after=second_2)
    stay = [stay_0, stay_1, stay_2, stay_3]
    first = [first_0, first_1, first_2, first_3]
    second = [second_0, second_1, second_2, second_3]

    dest = jnp.stack([z, z ^ 1, z ^ 2, 3 - z])
    own, near, skip, far = sketches(dest, stay, first, second, width)
    cuts = [own, send(near, NEAR), send(skip, SKIP), send(far, ACROSS)]
    partial = score(jnp.stack([z, dp >> 1]), cuts, parts, pair)
    partial = partial + send(partial, NEAR)
    return partial + send(partial, SKIP)


def own_rows(full, width):
    return lax.dynamic_slice_in_dim(full, lax.axis_index("tensor") * width, width, 1)


def layer_sketch(left, right, examples):
    left3 = left.reshape(examples, LEN, left.shape[1])
    right3 = right.reshape(examples, LEN, right.shape[1])
    return jnp.einsum("elr,elc->erc", left3, right3, precision=lax.Precision.HIGHEST) / jnp.sqrt(
        jnp.float32(LEN)
    )


def wide(
    layer_input, up_grad, hidden_input, down_grad, in_up, out_up, in_down, out_down, query_sketch
):
    width = K // lax.axis_size("tensor")
    examples = layer_input.shape[0] // LEN
    pairs = (
        (layer_input, in_up),
        (up_grad, out_up),
        (hidden_input, in_down),
        (down_grad, out_down),
    )
    a_up, b_up, a_down, b_down = lax.psum(
        tuple(jnp.dot(x, p.T, preferred_element_type=jnp.float32) for x, p in pairs), "tensor"
    )
    sketch = jnp.stack(
        [
            layer_sketch(own_rows(a_up, width), b_up, examples),
            layer_sketch(own_rows(a_down, width), b_down, examples),
        ],
        axis=1,
    )
    partial_total = jnp.einsum(
        "elrc,qlrc->qe",
        sketch,
        lax.all_gather(query_sketch, "dp", axis=0, tiled=True),
        precision=lax.Precision.HIGHEST,
    )
    return lax.psum(partial_total, "tensor").T / jnp.float32(K)


def solution(mesh):
    placed = (
        P(("parts", "dp"), "tensor"),
        P(("parts", "dp"), "tensor"),
        P(("parts", "dp"), "tensor"),
        P(("parts", "dp"), "tensor"),
        P(None, "tensor"),
        P(None, "tensor"),
        P(None, "tensor"),
        P(None, "tensor"),
        P(("parts", "dp"), None, "tensor", None),
    )
    return jax.shard_map(
        line if mesh.shape["tensor"] == 4 and mesh.shape["dp"] == 4 else wide,
        mesh=mesh,
        in_specs=placed,
        out_specs=P(("parts", "dp"), None),
        check_vma=False,
    )
```

time: 239 us -> 122 us (0.51)
  waiting for transfers between devices: 154 us -> 37.3 us
  matrix products: 53.9 us -> 0 us
  Pallas kernels: 0 us -> 53.6 us
  starting transfers between devices: 0.23 us -> 23.2 us
  between operations: 14.9 us -> 0.23 us
  blocking collectives: 9.61 us -> 0 us
  other arithmetic: 0.62 us -> 5.62 us
  local copies, waits for them, and re-layouts: 5.4 us -> 2.3 us
    psum x1 -> x0, waiting for transfers between devices: 154 us -> none  [local(): a_down, b_down = lax.psum((a_down, b_down), 'tensor')]
    dot_general x7 -> x0, matrix products: 53.9 us -> none  [the longest x4 41.2 us: project(): return jnp.dot(act, proj.T, preferred_element_type=jnp.float32)]
    pallas_call x0 -> x9, Pallas kernels: none -> 53.6 us  [the longest x5 42.4 us: project(): pl.pallas_call(functools.partial(project_kernel, shapes, load, queries is...]
    ppermute x0 -> x16, waiting for transfers between devices: none -> 37.3 us  [send(): return lax.ppermute(x, axis, pairs)]
    ppermute x0 -> x16, starting transfers between devices: none -> 23.2 us  [send(): return lax.ppermute(x, axis, pairs)]
    psum x1 -> x0, blocking collectives: 9.61 us -> none  [local(): total = lax.psum(partial_total, 'tensor')]
    add x0 -> x6, other arithmetic: none -> 4.56 us  [the longest x4 3.96 us: across(): return stay[1] + first[1]]
  transfers between devices with their start and end apart: 2 -> 16, of which waited for: 1 -> 7; matrix products, arithmetic and copies ran while one was open for 4% -> 4% of each run, Pallas kernels for 0% -> 37%
where the time goes in v2:
time: 122 us
  Pallas kernels  53.6 us (44%)
  waiting for transfers between devices  37.3 us (31%)
  starting transfers between devices  23.2 us (19%)
  other arithmetic  5.62 us (5%)
  local copies, waits for them, and re-layouts  2.3 us (2%)
    pallas_call x5, Pallas kernels, project(): pl.pallas_call(functools.partial(project_kernel, shapes, load, queries is...  42.4 us
    ppermute x16, waiting for transfers between devices, send(): return lax.ppermute(x, axis, pairs)  37.3 us
    ppermute x16, starting transfers between devices, send(): return lax.ppermute(x, axis, pairs)  23.2 us
    pallas_call x2, Pallas kernels, split(): pl.pallas_call(split_kernel, in_specs=[SCALARS, WHOLE, WHOLE], out_specs=...  5.56 us
    add x4, other arithmetic, across(): return stay[1] + first[1]  3.96 us
    pallas_call x1, Pallas kernels, score(): pl.pallas_call(functools.partial(score_kernel, pair), in_specs=[SCALARS]...  2.86 us
    pallas_call x1, Pallas kernels, sketches(): pl.pallas_call(functools.partial(sketch_kernel, count, width), in_specs=[...  2.84 us
  transfers between devices with their start and end apart: 16, of which 7 were waited for; matrix products, arithmetic and copies ran while one was open for 4% of the time, Pallas kernels for 37%

profile of v2, /device:TPU:0, one launch (start us, length us, event | category | flops | bytes accessed | tf_op | source)
XLA Modules:
  0.0 122.2 jit_solution(8245237347390787990)
XLA Ops:
  0.1 6.0 %shard_map.91 = f32[2,256,256]{2,1,0:T(8,128)S(1)} custom-call(s32[2]{0:T(128)S(1)} %pad_add_fusion.3.index, bf16[2048,2048]{1,0:T(8,128)(2,1)} %left.7, bf16[2048,7168]{1,0:T(8,128)(2,1)} %right.7, bf16[128,2048]{1,0:T(8,128)(2,1)} %p_left.7, bf16[128,7168]{1,0:T(8,128)(2,1)} %p_right.7), custom_call_target="tpu_custom_call" | custom-call | flops 1207959552 | bytes 9437184 | tf_op jit(solution)/shard_map/pallas_call | solution.py:128
  6.1 3.1 %collective-permute-start = (f32[2,256,256]{2,1,0:T(8,128)S(1)}, f32[2,256,256]{2,1,0:T(8,128)}, u32[]{:S(2)}, u32[]{:S(2)}) collective-permute-start(f32[2,256,256]{2,1,0:T(8,128)S(1)} %shard_map.91), channel_id=1, source_target_pairs={{0,1},{1,0},{2,3},{3,2},{4,5},{5,4},{6,7},{7,6},{8,9},{9,8},{10,11... | collective-permute-start | bytes 1572872 | tf_op jit(solution)/shard_map/ppermute | solution.py:33
  9.2 8.4 %shard_map.92 = (f32[2,256,256]{2,1,0:T(8,128)}, f32[64,8192]{1,0:T(8,128)}) custom-call(s32[2]{0:T(128)S(1)} %pad_add_fusion.2.index, bf16[2048,2048]{1,0:T(8,128)(2,1)} %left.7, bf16[2048,7168]{1,0:T(8,128)(2,1)} %right.7, bf16[128,2048]{1,0:T(8,128)(2,1)S(1)} %copy-done.2, bf16[128,7168]{1,0:T(8,128)(2,1)S(1)} %copy-done, f32[64,64,128]{2,1,0:T(8,128)} %bitcast.23), custom_call_target="tpu_custom_call" | custom-call | flops 1207959552 | bytes 9437184 | tf_op jit(solution)/shard_map/pallas_call | solution.py:128
  17.8 1.5 %collective-permute-start.12 = (f32[64,8192]{1,0:T(8,128)}, f32[64,8192]{1,0:T(8,128)}, u32[]{:S(2)}, u32[]{:S(2)}) collective-permute-start(f32[64,8192]{1,0:T(8,128)} %get-tuple-element.43.mine), channel_id=1, source_target_pairs={{0,8},{8,0},{4,12},{12,4},{1,9},{9,1},{5,13},{13,5},{2,10},{10,2},... | collective-permute-start | bytes 6291464 | tf_op jit(solution)/shard_map/ppermute | solution.py:33
  19.9 1.3 %collective-permute-done.refs_4_ = f32[2,256,256]{2,1,0:T(8,128)} collective-permute-done((f32[2,256,256]{2,1,0:T(8,128)S(1)}, f32[2,256,256]{2,1,0:T(8,128)}, u32[]{:S(2)}, u32[]{:S(2)}) %collective-permute-start) | collective-permute-done | bytes 524320 | tf_op jit(solution)/shard_map/ppermute | solution.py:33
  21.2 9.2 %shard_map.93 = (f32[2,256,256]{2,1,0:T(8,128)S(1)}, f32[2,256,256]{2,1,0:T(8,128)S(1)}) custom-call(s32[4]{0:T(128)S(1)} %add_add_fusion.index, bf16[2048,2048]{1,0:T(8,128)(2,1)} %left.7, bf16[2048,7168]{1,0:T(8,128)(2,1)} %right.7, bf16[128,2048]{1,0:T(8,128)(2,1)S(1)} %copy-done.2, bf16[128,7168]{1,0:T(8,128)(2,1)S(1)} %copy-done), custom_call_target="tpu_custom_call" | custom-call | flops 2415919104 | bytes 18874368 | tf_op jit(solution)/shard_map/pallas_call | solution.py:128
  30.4 1.2 fusion.3
  31.6 3.8 %collective-permute-start.2 = (f32[256,256]{1,0:T(8,128)S(1)}, f32[256,256]{1,0:T(8,128)S(1)}, u32[]{:S(2)}, u32[]{:S(2)}) collective-permute-start(f32[256,256]{1,0:T(8,128)S(1)} %fusion.3), channel_id=1, source_target_pairs={{0,3},{3,0},{1,2},{2,1},{4,7},{7,4},{5,6},{6,5},{8,11},{11,8},{9,1... | collective-permute-start | bytes 786440 | tf_op jit(solution)/shard_map/ppermute | solution.py:33
  35.4 1.0 fusion.2
  36.4 9.5 %shard_map.94 = (f32[2,256,256]{2,1,0:T(8,128)S(1)}, f32[2,256,256]{2,1,0:T(8,128)S(1)}) custom-call(s32[4]{0:T(128)S(1)} %pad_add_fusion.4.index, bf16[2048,7168]{1,0:T(8,128)(2,1)} %left.9, bf16[2048,2048]{1,0:T(8,128)(2,1)} %right.9, bf16[128,7168]{1,0:T(8,128)(2,1)S(1)} %copy-done.1, bf16[128,2048]{1,0:T(8,128)(2,1)S(1)} %copy-done.3), custom_call_target="tpu_custom_call" | custom-call | flops 2415919104 | bytes 18874368 | tf_op jit(solution)/shard_map/pallas_call | solution.py:128
  46.1 9.3 %shard_map.95 = (f32[2,256,256]{2,1,0:T(8,128)S(1)}, f32[2,256,256]{2,1,0:T(8,128)S(1)}) custom-call(s32[4]{0:T(128)S(1)} %add_add_fusion.1.index, bf16[2048,7168]{1,0:T(8,128)(2,1)} %left.9, bf16[2048,2048]{1,0:T(8,128)(2,1)} %right.9, bf16[128,7168]{1,0:T(8,128)(2,1)S(1)} %copy-done.1, bf16[128,2048]{1,0:T(8,128)(2,1)S(1)} %copy-done.3), custom_call_target="tpu_custom_call" | custom-call | flops 2415919104 | bytes 18874368 | tf_op jit(solution)/shard_map/pallas_call | solution.py:128
  55.5 2.1 %collective-permute-start.4 = (f32[2,256,256]{2,1,0:T(8,128)S(1)}, f32[2,256,256]{2,1,0:T(8,128)}, u32[]{:S(2)}, u32[]{:S(2)}) collective-permute-start(f32[2,256,256]{2,1,0:T(8,128)S(1)} %get-tuple-element.40), channel_id=1, source_target_pairs={{0,1},{1,0},{2,3},{3,2},{4,5},{5,4},{6,7},{7,6},{8,9},{9,8},{10,11... | collective-permute-start | bytes 1572872 | tf_op jit(solution)/shard_map/ppermute | solution.py:33
  57.5 0.7 collective-permute-start.5
  58.3 18.0 %collective-permute-done.5.refs_9_ = f32[256,256]{1,0:T(8,128)S(1)} collective-permute-done((f32[256,256]{1,0:T(8,128)S(1)}, f32[256,256]{1,0:T(8,128)S(1)}, u32[]{:S(2)}, u32[]{:S(2)}) %collective-permute-start.5) | collective-permute-done | bytes 262176 | tf_op jit(solution)/shard_map/ppermute | solution.py:33
  76.3 0.8 fusion.1
  77.2 2.7 %shard_map.96 = (bf16[128,8192]{1,0:T(8,128)(2,1)S(1)}, bf16[128,8192]{1,0:T(8,128)(2,1)S(1)}) custom-call(s32[1]{0:T(128)} %bitcast.17.place, f32[64,8192]{1,0:T(8,128)} %get-tuple-element.43.mine, f32[64,8192]{1,0:T(8,128)} %collective-permute-done.7.other), custom_call_target="tpu_custom_call" | custom-call | flops 4194304 | bytes 8388608 | tf_op jit(solution)/shard_map/pallas_call | solution.py:187
  80.0 1.4 %copy-done.4 = bf16[128,8192]{1,0:T(8,128)(2,1)} copy-done((bf16[128,8192]{1,0:T(8,128)(2,1)}, bf16[128,8192]{1,0:T(8,128)(2,1)S(1)}, u32[]{:S(2)}) %copy-start.4) | copy-done | bytes 2097176
  81.3 1.0 fusion
  82.4 1.3 %collective-permute-start.6 = (f32[256,256]{1,0:T(8,128)}, f32[256,256]{1,0:T(8,128)S(1)}, u32[]{:S(2)}, u32[]{:S(2)}) collective-permute-start(f32[256,256]{1,0:T(8,128)} %fusion.1), channel_id=1, source_target_pairs={{0,3},{3,0},{1,2},{2,1},{4,7},{7,4},{5,6},{6,5},{8,11},{11,8},{9,1... | collective-permute-start | bytes 786440 | tf_op jit(solution)/shard_map/ppermute | solution.py:33
  83.7 2.6 %collective-permute-start.8 = (f32[256,256]{1,0:T(8,128)S(1)}, f32[256,256]{1,0:T(8,128)S(1)}, u32[]{:S(2)}, u32[]{:S(2)}) collective-permute-start(f32[256,256]{1,0:T(8,128)S(1)} %fusion), channel_id=1, source_target_pairs={{0,3},{3,0},{1,2},{2,1},{4,7},{7,4},{5,6},{6,5},{8,11},{11,8},{9,1... | collective-permute-start | bytes 786440 | tf_op jit(solution)/shard_map/ppermute | solution.py:33
  86.9 6.7 %collective-permute-done.6.refs_10_ = f32[256,256]{1,0:T(8,128)S(1)} collective-permute-done((f32[256,256]{1,0:T(8,128)}, f32[256,256]{1,0:T(8,128)S(1)}, u32[]{:S(2)}, u32[]{:S(2)}) %collective-permute-start.6) | collective-permute-done | bytes 262176 | tf_op jit(solution)/shard_map/ppermute | solution.py:33
  93.6 5.2 %collective-permute-done.8.refs_11_ = f32[256,256]{1,0:T(8,128)S(1)} collective-permute-done((f32[256,256]{1,0:T(8,128)S(1)}, f32[256,256]{1,0:T(8,128)S(1)}, u32[]{:S(2)}, u32[]{:S(2)}) %collective-permute-start.8) | collective-permute-done | bytes 262176 | tf_op jit(solution)/shard_map/ppermute | solution.py:33
  99.5 2.8 %shard_map.97 = (f32[4,32,128]{2,1,0:T(8,128)S(1)}, f32[4,32,128]{2,1,0:T(8,128)S(1)}, f32[4,32,128]{2,1,0:T(8,128)S(1)}, f32[4,32,128]{2,1,0:T(8,128)S(1)}) custom-call(s32[4]{0:T(128)} %pad_add_fusion.1.dest, f32[2,256,256]{2,1,0:T(8,128)} %copy-done.6, f32[2,256,256]{2,1,0:T(8,128)} %copy-done.7, f32[2,256,256]{2,1,0:T(8,128)} %copy-done.8, ...), custom_call_target="tpu_custom_call" | custom-call | flops 134217728 | bytes 2097152 | tf_op jit(solution)/shard_map/pallas_call | solution.py:161
  102.4 1.8 %collective-permute-start.10 = (f32[4,32,128]{2,1,0:T(8,128)S(1)}, f32[4,32,128]{2,1,0:T(8,128)S(1)}, u32[]{:S(2)}, u32[]{:S(2)}) collective-permute-start(f32[4,32,128]{2,1,0:T(8,128)S(1)} %get-tuple-element.48), channel_id=1, source_target_pairs={{0,2},{2,0},{1,3},{3,1},{4,6},{6,4},{5,7},{7,5},{8,10},{10,8},{9,1... | collective-permute-start | bytes 196616 | tf_op jit(solution)/shard_map/ppermute | solution.py:33
  104.3 2.5 %collective-permute-start.11 = (f32[4,32,128]{2,1,0:T(8,128)S(1)}, f32[4,32,128]{2,1,0:T(8,128)S(1)}, u32[]{:S(2)}, u32[]{:S(2)}) collective-permute-start(f32[4,32,128]{2,1,0:T(8,128)S(1)} %get-tuple-element.49), channel_id=1, source_target_pairs={{0,3},{3,0},{1,2},{2,1},{4,7},{7,4},{5,6},{6,5},{8,11},{11,8},{9,1... | collective-permute-start | bytes 196616 | tf_op jit(solution)/shard_map/ppermute | solution.py:33
  106.9 2.9 %shard_map.98 = (bf16[128,8192]{1,0:T(8,128)(2,1)S(1)}, bf16[128,8192]{1,0:T(8,128)(2,1)S(1)}) custom-call(s32[1]{0:T(128)} %bitcast.17.place, f32[64,8192]{1,0:T(8,128)} %collective-permute-done.12.mine, f32[64,8192]{1,0:T(8,128)} %collective-permute-done.13.other), custom_call_target="tpu_custom_call" | custom-call | flops 4194304 | bytes 8388608 | tf_op jit(solution)/shard_map/pallas_call | solution.py:187
  109.8 0.8 collective-permute-done.10.skip
  110.5 2.9 %shard_map.99 = f32[8,256]{1,0:T(8,128)S(1)} custom-call(s32[2]{0:T(128)S(1)} %pad_add_fusion.place, f32[4,32,128]{2,1,0:T(8,128)S(1)} %get-tuple-element.46.own, f32[4,32,128]{2,1,0:T(8,128)S(1)} %collective-permute-done.9.near, f32[4,32,128]{2,1,0:T(8,128)S(1)} %collective-permute-done.10.skip, f32[4,32,128]{2,1,0:T(8,128)S(1)} %collective-permute-done.11.across, ...), custom_call_target="tpu_custom_call" | custom-call | flops 67108864 | bytes 8388608 | tf_op jit(solution)/shard_map/pallas_call | solution.py:228
  113.4 1.3 %collective-permute-start.14 = (f32[8,256]{1,0:T(8,128)S(1)}, f32[8,256]{1,0:T(8,128)S(1)}, u32[]{:S(2)}, u32[]{:S(2)}) collective-permute-start(f32[8,256]{1,0:T(8,128)S(1)} %shard_map.99), channel_id=1, source_target_pairs={{0,1},{1,0},{2,3},{3,2},{4,5},{5,4},{6,7},{7,6},{8,9},{9,8},{10,11... | collective-permute-start | bytes 24584 | tf_op jit(solution)/shard_map/ppermute | solution.py:33
  114.7 2.4 %collective-permute-done.14 = f32[8,256]{1,0:T(8,128)S(1)} collective-permute-done((f32[8,256]{1,0:T(8,128)S(1)}, f32[8,256]{1,0:T(8,128)S(1)}, u32[]{:S(2)}, u32[]{:S(2)}) %collective-permute-start.14) | collective-permute-done | bytes 8224 | tf_op jit(solution)/shard_map/ppermute | solution.py:33
  117.1 1.6 %collective-permute-start.15 = (f32[8,256]{1,0:T(8,128)S(1)}, f32[8,256]{1,0:T(8,128)S(1)}, u32[]{:S(2)}, u32[]{:S(2)}) collective-permute-start(f32[8,256]{1,0:T(8,128)S(1)} %add.58), channel_id=1, source_target_pairs={{0,2},{2,0},{1,3},{3,1},{4,6},{6,4},{5,7},{7,5},{8,10},{10,8},{9,1... | collective-permute-start | bytes 24584 | tf_op jit(solution)/shard_map/ppermute | solution.py:33
  118.7 2.9 %collective-permute-done.15 = f32[8,256]{1,0:T(8,128)S(1)} collective-permute-done((f32[8,256]{1,0:T(8,128)S(1)}, f32[8,256]{1,0:T(8,128)S(1)}, u32[]{:S(2)}, u32[]{:S(2)}) %collective-permute-start.15) | collective-permute-done | bytes 8224 | tf_op jit(solution)/shard_map/ppermute | solution.py:33
  (52 shorter events, 3.4 us)
Async XLA Ops:
  0.1 9.2 %copy-start = (bf16[128,7168]{1,0:T(8,128)(2,1)S(1)}, bf16[128,7168]{1,0:T(8,128)(2,1)}, u32[]{:S(2)}) copy-start(bf16[128,7168]{1,0:T(8,128)(2,1)} %p_right.7) | copy-start | bytes 5505028
  0.1 9.2 %copy-start.2 = (bf16[128,2048]{1,0:T(8,128)(2,1)S(1)}, bf16[128,2048]{1,0:T(8,128)(2,1)}, u32[]{:S(2)}) copy-start(bf16[128,2048]{1,0:T(8,128)(2,1)} %p_left.7) | copy-start | bytes 1572868
  6.1 15.1 %collective-permute-start = (f32[2,256,256]{2,1,0:T(8,128)S(1)}, f32[2,256,256]{2,1,0:T(8,128)}, u32[]{:S(2)}, u32[]{:S(2)}) collective-permute-start(f32[2,256,256]{2,1,0:T(8,128)S(1)} %shard_map.91), channel_id=1, source_target_pairs={{0,1},{1,0},{2,3},{3,2},{4,5},{5,4},{6,7},{7,6},{8,9},{9,8},{10,11... | collective-permute-start | bytes 1572872 | tf_op jit(solution)/shard_map/ppermute | solution.py:33
  17.7 59.6 %collective-permute-start.7 = (f32[64,8192]{1,0:T(8,128)}, f32[64,8192]{1,0:T(8,128)}, u32[]{:S(2)}, u32[]{:S(2)}) collective-permute-start(f32[64,8192]{1,0:T(8,128)} %get-tuple-element.43.mine), channel_id=1, source_target_pairs={{0,4},{4,0},{8,12},{12,8},{1,5},{5,1},{9,13},{13,9},{2,6},{6,2},{1... | collective-permute-start | bytes 6291464 | tf_op jit(solution)/shard_map/ppermute | solution.py:33
  17.8 64.6 %collective-permute-start.12 = (f32[64,8192]{1,0:T(8,128)}, f32[64,8192]{1,0:T(8,128)}, u32[]{:S(2)}, u32[]{:S(2)}) collective-permute-start(f32[64,8192]{1,0:T(8,128)} %get-tuple-element.43.mine), channel_id=1, source_target_pairs={{0,8},{8,0},{4,12},{12,4},{1,9},{9,1},{5,13},{13,5},{2,10},{10,2},... | collective-permute-start | bytes 6291464 | tf_op jit(solution)/shard_map/ppermute | solution.py:33
  19.3 16.1 %collective-permute-start.1 = (f32[2,256,256]{2,1,0:T(8,128)}, f32[2,256,256]{2,1,0:T(8,128)}, u32[]{:S(2)}, u32[]{:S(2)}) collective-permute-start(f32[2,256,256]{2,1,0:T(8,128)} %get-tuple-element.31), channel_id=1, source_target_pairs={{0,1},{1,0},{2,3},{3,2},{4,5},{5,4},{6,7},{7,6},{8,9},{9,8},{10,11... | collective-permute-start | bytes 1572872 | tf_op jit(solution)/shard_map/ppermute | solution.py:33
  19.9 16.5 %copy-start.3 = (bf16[128,2048]{1,0:T(8,128)(2,1)S(1)}, bf16[128,2048]{1,0:T(8,128)(2,1)}, u32[]{:S(2)}) copy-start(bf16[128,2048]{1,0:T(8,128)(2,1)} %p_right.9) | copy-start | bytes 1572868
  21.2 15.3 %copy-start.1 = (bf16[128,7168]{1,0:T(8,128)(2,1)S(1)}, bf16[128,7168]{1,0:T(8,128)(2,1)}, u32[]{:S(2)}) copy-start(bf16[128,7168]{1,0:T(8,128)(2,1)} %p_left.9) | copy-start | bytes 5505028
  30.4 15.6 %copy-start.6 = (f32[2,256,256]{2,1,0:T(8,128)}, f32[2,256,256]{2,1,0:T(8,128)S(1)}, u32[]{:S(2)}) copy-start(f32[2,256,256]{2,1,0:T(8,128)S(1)} %get-tuple-element.33.refs_0_) | copy-start | bytes 1572868
  30.4 15.6 %copy-start.7 = (f32[2,256,256]{2,1,0:T(8,128)}, f32[2,256,256]{2,1,0:T(8,128)S(1)}, u32[]{:S(2)}) copy-start(f32[2,256,256]{2,1,0:T(8,128)S(1)} %get-tuple-element.34.refs_1_) | copy-start | bytes 1572868
  31.6 14.5 %collective-permute-start.2 = (f32[256,256]{1,0:T(8,128)S(1)}, f32[256,256]{1,0:T(8,128)S(1)}, u32[]{:S(2)}, u32[]{:S(2)}) collective-permute-start(f32[256,256]{1,0:T(8,128)S(1)} %fusion.3), channel_id=1, source_target_pairs={{0,3},{3,0},{1,2},{2,1},{4,7},{7,4},{5,6},{6,5},{8,11},{11,8},{9,1... | collective-permute-start | bytes 786440 | tf_op jit(solution)/shard_map/ppermute | solution.py:33
  46.0 30.3 %copy-start.8 = (f32[2,256,256]{2,1,0:T(8,128)}, f32[2,256,256]{2,1,0:T(8,128)S(1)}, u32[]{:S(2)}) copy-start(f32[2,256,256]{2,1,0:T(8,128)S(1)} %get-tuple-element.41.refs_2_) | copy-start | bytes 1572868
  46.0 30.3 %collective-permute-start.3 = (f32[2,256,256]{2,1,0:T(8,128)S(1)}, f32[2,256,256]{2,1,0:T(8,128)S(1)}, u32[]{:S(2)}, u32[]{:S(2)}) collective-permute-start(f32[2,256,256]{2,1,0:T(8,128)S(1)} %get-tuple-element.37), channel_id=1, source_target_pairs={{0,1},{1,0},{2,3},{3,2},{4,5},{5,4},{6,7},{7,6},{8,9},{9,8},{10,11... | collective-permute-start | bytes 1572872 | tf_op jit(solution)/shard_map/ppermute | solution.py:33
  46.1 9.3 %copy-start.11 = (f32[256,256]{1,0:T(8,128)}, f32[256,256]{1,0:T(8,128)S(1)}, u32[]{:S(2)}) copy-start(f32[256,256]{1,0:T(8,128)S(1)} %collective-permute-done.2.refs_8_) | copy-start | bytes 786436
  55.5 25.9 %copy-start.9 = (f32[2,256,256]{2,1,0:T(8,128)}, f32[2,256,256]{2,1,0:T(8,128)S(1)}, u32[]{:S(2)}) copy-start(f32[2,256,256]{2,1,0:T(8,128)S(1)} %get-tuple-element.45.refs_3_) | copy-start | bytes 1572868
  55.5 25.9 %collective-permute-start.4 = (f32[2,256,256]{2,1,0:T(8,128)S(1)}, f32[2,256,256]{2,1,0:T(8,128)}, u32[]{:S(2)}, u32[]{:S(2)}) collective-permute-start(f32[2,256,256]{2,1,0:T(8,128)S(1)} %get-tuple-element.40), channel_id=1, source_target_pairs={{0,1},{1,0},{2,3},{3,2},{4,5},{5,4},{6,7},{7,6},{8,9},{9,8},{10,11... | collective-permute-start | bytes 1572872 | tf_op jit(solution)/shard_map/ppermute | solution.py:33
  57.5 18.7 %collective-permute-start.5 = (f32[256,256]{1,0:T(8,128)S(1)}, f32[256,256]{1,0:T(8,128)S(1)}, u32[]{:S(2)}, u32[]{:S(2)}) collective-permute-start(f32[256,256]{1,0:T(8,128)S(1)} %fusion.2), channel_id=1, source_target_pairs={{0,3},{3,0},{1,2},{2,1},{4,7},{7,4},{5,6},{6,5},{8,11},{11,8},{9,1... | collective-permute-start | bytes 786440 | tf_op jit(solution)/shard_map/ppermute | solution.py:33
  76.2 0.8 copy-start.12
  76.3 1.0 copy-start.10
  80.0 1.4 %copy-start.4 = (bf16[128,8192]{1,0:T(8,128)(2,1)}, bf16[128,8192]{1,0:T(8,128)(2,1)S(1)}, u32[]{:S(2)}) copy-start(bf16[128,8192]{1,0:T(8,128)(2,1)S(1)} %get-tuple-element.50.refs_1_) | copy-start | bytes 6291460
  82.3 24.5 %collective-permute-start.13 = (f32[64,8192]{1,0:T(8,128)}, f32[64,8192]{1,0:T(8,128)}, u32[]{:S(2)}, u32[]{:S(2)}) collective-permute-start(f32[64,8192]{1,0:T(8,128)} %collective-permute-done.12.mine), channel_id=1, source_target_pairs={{0,4},{4,0},{8,12},{12,8},{1,5},{5,1},{9,13},{13,9},{2,6},{6,2},{1... | collective-permute-start | bytes 6291464 | tf_op jit(solution)/shard_map/ppermute | solution.py:33
  82.4 11.2 %collective-permute-start.6 = (f32[256,256]{1,0:T(8,128)}, f32[256,256]{1,0:T(8,128)S(1)}, u32[]{:S(2)}, u32[]{:S(2)}) collective-permute-start(f32[256,256]{1,0:T(8,128)} %fusion.1), channel_id=1, source_target_pairs={{0,3},{3,0},{1,2},{2,1},{4,7},{7,4},{5,6},{6,5},{8,11},{11,8},{9,1... | collective-permute-start | bytes 786440 | tf_op jit(solution)/shard_map/ppermute | solution.py:33
  83.7 15.1 %collective-permute-start.8 = (f32[256,256]{1,0:T(8,128)S(1)}, f32[256,256]{1,0:T(8,128)S(1)}, u32[]{:S(2)}, u32[]{:S(2)}) collective-permute-start(f32[256,256]{1,0:T(8,128)S(1)} %fusion), channel_id=1, source_target_pairs={{0,3},{3,0},{1,2},{2,1},{4,7},{7,4},{5,6},{6,5},{8,11},{11,8},{9,1... | collective-permute-start | bytes 786440 | tf_op jit(solution)/shard_map/ppermute | solution.py:33
  93.6 5.2 %copy-start.13 = (f32[256,256]{1,0:T(8,128)}, f32[256,256]{1,0:T(8,128)S(1)}, u32[]{:S(2)}) copy-start(f32[256,256]{1,0:T(8,128)S(1)} %collective-permute-done.6.refs_10_) | copy-start | bytes 786436
  98.8 0.7 copy-start.14
  102.4 7.4 %collective-permute-start.9 = (f32[4,32,128]{2,1,0:T(8,128)S(1)}, f32[4,32,128]{2,1,0:T(8,128)S(1)}, u32[]{:S(2)}, u32[]{:S(2)}) collective-permute-start(f32[4,32,128]{2,1,0:T(8,128)S(1)} %get-tuple-element.47), channel_id=1, source_target_pairs={{0,1},{1,0},{2,3},{3,2},{4,5},{5,4},{6,7},{7,6},{8,9},{9,8},{10,11... | collective-permute-start | bytes 196616 | tf_op jit(solution)/shard_map/ppermute | solution.py:33
  102.4 8.1 %collective-permute-start.10 = (f32[4,32,128]{2,1,0:T(8,128)S(1)}, f32[4,32,128]{2,1,0:T(8,128)S(1)}, u32[]{:S(2)}, u32[]{:S(2)}) collective-permute-start(f32[4,32,128]{2,1,0:T(8,128)S(1)} %get-tuple-element.48), channel_id=1, source_target_pairs={{0,2},{2,0},{1,3},{3,1},{4,6},{6,4},{5,7},{7,5},{8,10},{10,8},{9,1... | collective-permute-start | bytes 196616 | tf_op jit(solution)/shard_map/ppermute | solution.py:33
  104.3 6.2 %collective-permute-start.11 = (f32[4,32,128]{2,1,0:T(8,128)S(1)}, f32[4,32,128]{2,1,0:T(8,128)S(1)}, u32[]{:S(2)}, u32[]{:S(2)}) collective-permute-start(f32[4,32,128]{2,1,0:T(8,128)S(1)} %get-tuple-element.49), channel_id=1, source_target_pairs={{0,3},{3,0},{1,2},{2,1},{4,7},{7,4},{5,6},{6,5},{8,11},{11,8},{9,1... | collective-permute-start | bytes 196616 | tf_op jit(solution)/shard_map/ppermute | solution.py:33
  106.9 3.6 %copy-start.5 = (bf16[128,8192]{1,0:T(8,128)(2,1)S(1)}, bf16[128,8192]{1,0:T(8,128)(2,1)}, u32[]{:S(2)}) copy-start(bf16[128,8192]{1,0:T(8,128)(2,1)} %copy-done.4) | copy-start | bytes 6291460
  113.4 3.7 %collective-permute-start.14 = (f32[8,256]{1,0:T(8,128)S(1)}, f32[8,256]{1,0:T(8,128)S(1)}, u32[]{:S(2)}, u32[]{:S(2)}) collective-permute-start(f32[8,256]{1,0:T(8,128)S(1)} %shard_map.99), channel_id=1, source_target_pairs={{0,1},{1,0},{2,3},{3,2},{4,5},{5,4},{6,7},{7,6},{8,9},{9,8},{10,11... | collective-permute-start | bytes 24584 | tf_op jit(solution)/shard_map/ppermute | solution.py:33
  117.1 4.5 %collective-permute-start.15 = (f32[8,256]{1,0:T(8,128)S(1)}, f32[8,256]{1,0:T(8,128)S(1)}, u32[]{:S(2)}, u32[]{:S(2)}) collective-permute-start(f32[8,256]{1,0:T(8,128)S(1)} %add.58), channel_id=1, source_target_pairs={{0,2},{2,0},{1,3},{3,1},{4,6},{6,4},{5,7},{7,5},{8,10},{10,8},{9,1... | collective-permute-start | bytes 24584 | tf_op jit(solution)/shard_map/ppermute | solution.py:33

commit v3 on v2

--- a/solution.py
+++ b/solution.py
@@ -42,48 +42,53 @@
     return [(lo, min(lo + PIECE, width)) for lo in range(0, width, PIECE)]
 
 
-def project_kernel(shapes, load, spread, index, left, right, p_left, p_right, *refs):
+def project_kernel(jobs, load, spread, index, *refs):
+    operands, refs = refs[:8], refs[8:]
     moves = []
     if spread:
         queries, refs = refs[0], refs[1:]
-        flat, spread_sem = refs[len(shapes)], refs[-1]
-        refs = refs[: len(shapes)] + refs[len(shapes) + 1 : -1]
+        flat, spread_sem = refs[len(jobs)], refs[-1]
+        refs = refs[: len(jobs)] + refs[len(jobs) + 1 : -1]
         for r in range(queries.shape[1]):
             moves.append(
                 pltpu.make_async_copy(
                     queries.at[:, r, :], flat.at[:, r * K : (r + 1) * K], spread_sem.at[r]
                 )
             )
-    arrays, (slots, sem, *loaded) = refs[: len(shapes)], refs[len(shapes) :]
-    outs = [array.at[i] for array, n in zip(arrays, shapes) for i in range(n)]
+    arrays, (slots, sem, *loaded) = refs[: len(jobs)], refs[len(jobs) :]
     depth = slots.shape[0]
     steps = []
-    for first in range(0, len(outs), 2):
-        group = range(first, min(first + 2, len(outs)))
-        for side, (x, p, row) in enumerate(((left, p_left, 0), (right, p_right, K))):
-            for lo, hi in pieces(x.shape[1]):
-                slot = len(steps) % depth
-                copies = [
-                    pltpu.make_async_copy(
-                        x.at[pl.ds(pl.multiple_of(index[i] * LEN, LEN), LEN), lo:hi],
-                        slots.at[slot, n * LEN : (n + 1) * LEN, : hi - lo],
-                        sem.at[slot, n],
-                    )
-                    for n, i in enumerate(group)
-                ]
-                if load and first == 0:
-                    copies.append(
+    number = 0
+    for array, (layer, count) in zip(arrays, jobs):
+        left, right, p_left, p_right = operands[4 * layer : 4 * layer + 4]
+        for first in range(0, count, 2):
+            group = range(first, min(first + 2, count))
+            for side, (x, p, row) in enumerate(((left, p_left, 0), (right, p_right, K))):
+                for lo, hi in pieces(x.shape[1]):
+                    slot = len(steps) % depth
+                    copies = [
                         pltpu.make_async_copy(
-                            p.at[:, lo:hi], loaded[side].at[:, lo:hi], sem.at[slot, 2]
+                            x.at[pl.ds(pl.multiple_of(index[number + i] * LEN, LEN), LEN), lo:hi],
+                            slots.at[slot, n * LEN : (n + 1) * LEN, : hi - lo],
+                            sem.at[slot, n],
                         )
-                    )
-                steps.append((copies, slot, group, loaded[side] if load else p, row, lo, hi))
+                        for n, i in enumerate(group)
+                    ]
+                    if load and first == 0:
+                        copies.append(
+                            pltpu.make_async_copy(
+                                p.at[:, lo:hi], loaded[side].at[:, lo:hi], sem.at[slot, 2]
+                            )
+                        )
+                    outs = [array.at[i] for i in group]
+                    steps.append((copies, slot, outs, loaded[side] if load else p, row, lo, hi))
+        number += count
     for step in steps[: depth - 1]:
         for copy in step[0]:
             copy.start()
     for move in moves:
         move.start()
-    for n, (copies, slot, group, p, row, lo, hi) in enumerate(steps):
+    for n, (copies, slot, outs, p, row, lo, hi) in enumerate(steps):
         for copy in copies:
             copy.wait()
         if n + depth - 1 < len(steps):
@@ -91,51 +96,64 @@
                 copy.start()
         part = lax.dot_general(
             p[:, lo:hi],
-            slots[slot, : len(group) * LEN, : hi - lo],
+            slots[slot, : len(outs) * LEN, : hi - lo],
             ROWS_BY_ROWS,
             preferred_element_type=jnp.float32,
         )
-        for m, i in enumerate(group):
+        for m, out in enumerate(outs):
             if lo == 0:
-                outs[i][row : row + K, :] = part[:, m * LEN : (m + 1) * LEN]
+                out[row : row + K, :] = part[:, m * LEN : (m + 1) * LEN]
             else:
-                outs[i][row : row + K, :] += part[:, m * LEN : (m + 1) * LEN]
+                out[row : row + K, :] += part[:, m * LEN : (m + 1) * LEN]
     for move in moves:
         move.wait()
 
 
-def project(groups, left, right, p_left, p_right, load=False, after=None, queries=None):
-    shapes = [len(group) for group in groups]
-    index = jnp.stack([i for group in groups for i in group]).astype(jnp.int32)
+def project(layers, jobs, load=False, after=None, queries=None):
+    index = jnp.stack([i for _, group in jobs for i in group]).astype(jnp.int32)
     if after is not None:
         index = lax.optimization_barrier((index, after))[0]
-    widths = left.shape[1], right.shape[1]
-    rows = sum(shapes) * LEN
-    place = there if load else here
+    jobs = [(layer, len(group)) for layer, group in jobs]
+    dtype = layers[0][0].dtype
     scratch = [
-        pltpu.VMEM((AHEAD + 1, 2 * LEN, PIECE), left.dtype),
+        pltpu.VMEM((AHEAD + 1, 2 * LEN, PIECE), dtype),
         pltpu.SemaphoreType.DMA((AHEAD + 1, 3)),
     ]
     if load:
-        scratch += [pltpu.VMEM((K, w), left.dtype) for w in widths]
-    p_spec = OUTSIDE if load else WHOLE
-    more_in, more_out = [], []
+        scratch += [pltpu.VMEM(p.shape, dtype) for p in layers[jobs[0][0]][2:]]
+    place = there if load else here
+    operands, specs = [], []
+    for layer, (left, right, p_left, p_right) in enumerate(layers):
+        used = layer in [job[0] for job in jobs]
+        operands += [there(left), there(right)]
+        operands += [place(p) if used else there(p) for p in (p_left, p_right)]
+        specs += [OUTSIDE, OUTSIDE] + [OUTSIDE if load or not used else WHOLE] * 2
+    extra = []
     if queries is not None:
-        more_in = [there(queries)]
+        operands.append(there(queries))
+        specs.append(OUTSIDE)
         count, per_query, _ = queries.shape
-        more_out = [pltpu.VMEM((count, per_query * K), queries.dtype)]
-        scratch += [pltpu.SemaphoreType.DMA((per_query,))]
+        extra = [pltpu.VMEM((count, per_query * K), queries.dtype)]
+        scratch.append(pltpu.SemaphoreType.DMA((per_query,)))
     return pl.pallas_call(
-        functools.partial(project_kernel, shapes, load, queries is not None),
-        in_specs=[SCALARS, OUTSIDE, OUTSIDE, p_spec, p_spec] + [OUTSIDE] * len(more_in),
-        out_specs=[WHOLE] * (len(shapes) + len(more_out)),
-        out_shape=[pltpu.VMEM((n, 2 * K, LEN), jnp.float32) for n in shapes] + more_out,
+        functools.partial(project_kernel, jobs, load, queries is not None),
+        in_specs=[SCALARS] + specs,
+        out_specs=[WHOLE] * (len(jobs) + len(extra)),
+        out_shape=[pltpu.VMEM((n, 2 * K, LEN), jnp.float32) for _, n in jobs] + extra,
         scratch_shapes=scratch,
         compiler_params=pltpu.CompilerParams(vmem_limit_bytes=16 * 2**20),
         cost_estimate=pl.CostEstimate(
-            flops=2 * rows * K * sum(widths), bytes_accessed=2 * rows * sum(widths), transcendentals=0
+            flops=sum(
+                2 * n * LEN * K * (layers[layer][0].shape[1] + layers[layer][1].shape[1])
+                for layer, n in jobs
+            ),
+            bytes_accessed=sum(
+                2 * n * LEN * (layers[layer][0].shape[1] + layers[layer][1].shape[1])
+                for layer, n in jobs
+            ),
+            transcendentals=0,
         ),
-    )(index, there(left), there(right), place(p_left), place(p_right), *more_in)
+    )(index, *operands)
 
 
 def sketch_kernel(count, width, dest, *refs):
@@ -245,17 +263,19 @@
     width = K // 4
     z = lax.axis_index("tensor").astype(jnp.int32)
     dp = lax.axis_index("dp").astype(jnp.int32)
-    up = (layer_input, up_grad, in_up, out_up)
-    down = (hidden_input, down_grad, in_down, out_down)
+    layers = (
+        (layer_input, up_grad, in_up, out_up),
+        (hidden_input, down_grad, in_down, out_down),
+    )
 
     def of(owner, j):
         return owner * pair + j
 
-    def leaving(j):
-        return [of(z ^ 1, j), of(z ^ 2, j)]
-
-    def staying(j):
-        return [of(z, j), of(3 - z, j)]
+    def leaving(k):
+        return k // pair, [of(z ^ 1, k % pair), of(z ^ 2, k % pair)]
+
+    def staying(k):
+        return k // pair, [of(z, k % pair), of(3 - z, k % pair)]
 
     queries = query_sketch.reshape(query_sketch.shape[0], -1, K)
     by_core = [(0, 1), (1, 0), (2, 3), (3, 2)]
@@ -267,32 +287,32 @@
             stay = lax.optimization_barrier((stay, after))[0]
         return stay[1] + first[1]
 
-    (out_0,) = project([leaving(0)], *up, load=True)
-    first_0 = send(out_0, NEAR)
-    out_1, flat = project([leaving(1)], *up, after=out_0, queries=queries)
-    first_1 = send(out_1, NEAR)
-    other_core = send(flat, by_core, "dp")
-    other_chip = send(flat, by_chip, "dp")
-    stay_0, stay_1 = project([staying(0), staying(1)], *up, after=(out_1, first_0))
-    sum_0 = across(stay_0, first_0)
-    second_0 = send(sum_0, ACROSS)
-    sum_1 = across(stay_1, first_1)
-    second_1 = send(sum_1, ACROSS)
-    out_2, stay_2 = project([leaving(0), staying(0)], *down, after=(sum_0, sum_1))
-    first_2 = send(out_2, NEAR)
-    out_3, stay_3 = project([leaving(1), staying(1)], *down, after=(out_2, second_0))
-    first_3 = send(out_3, NEAR)
-    sum_2 = across(stay_2, first_2, (out_3, second_1))
-    second_2 = send(sum_2, ACROSS)
-    own_chip = split(core, flat, other_core, after=sum_2)
-    sum_3 = across(stay_3, first_3, own_chip[0])
-    second_3 = send(sum_3, ACROSS)
-    other_chip = lax.optimization_barrier((other_chip, sum_3))[0]
+    chunks = 2 * pair
+    stay, first, second = [], [], []
+    (out,) = project(layers, [leaving(0)], load=True)
+    first.append(send(out, NEAR))
+    order = out
+    for k in range(chunks):
+        if k == 0:
+            out, kept, flat = project(layers, [leaving(1), staying(0)], after=order, queries=queries)
+            other_core = send(flat, by_core, "dp")
+            other_chip = send(flat, by_chip, "dp")
+        elif k < chunks - 1:
+            out, kept = project(layers, [leaving(k + 1), staying(k)], after=order)
+        else:
+            (kept,) = project(layers, [staying(k)], after=order)
+        stay.append(kept)
+        if k < chunks - 1:
+            first.append(send(out, NEAR))
+            order = (out,) + tuple(second[-1:])
+        else:
+            own_chip = split(core, flat, other_core, after=kept)
+            order = (own_chip[0],) + tuple(second[-1:])
+        order = across(kept, first[k], order)
+        second.append(send(order, ACROSS))
+    other_chip = lax.optimization_barrier((other_chip, order))[0]
     other_both = send(other_chip, by_core, "dp")
-    parts = own_chip + split(core, other_chip, other_both, after=second_2)
-    stay = [stay_0, stay_1, stay_2, stay_3]
-    first = [first_0, first_1, first_2, first_3]
-    second = [second_0, second_1, second_2, second_3]
+    parts = own_chip + split(core, other_chip, other_both)
 
     dest = jnp.stack([z, z ^ 1, z ^ 2, 3 - z])
     own, near, skip, far = sketches(dest, stay, first, second, width)

time: 122 us -> 115 us (0.943)
  starting transfers between devices: 23.2 us -> 16.6 us
  waiting for transfers between devices: 37.3 us -> 32.3 us
  local copies, waits for them, and re-layouts: 2.3 us -> 5.76 us
    ppermute x16, starting transfers between devices: 23.2 us -> 16.6 us  [send(): return lax.ppermute(x, axis, pairs)]
    ppermute x16, waiting for transfers between devices: 37.3 us -> 32.3 us  [send(): return lax.ppermute(x, axis, pairs)]
    unnamed x30 -> x36, local copies, waits for them, and re-layouts: 2.3 us -> 5.76 us
  transfers between devices with their start and end apart: 16 -> 16, of which waited for: 7 -> 7; matrix products, arithmetic and copies ran while one was open for 4% -> 4% of each run, Pallas kernels for 37% -> 39%
where the time goes in v3:
time: 115 us
  Pallas kernels  54.1 us (47%)
  waiting for transfers between devices  32.3 us (28%)
  starting transfers between devices  16.6 us (14%)
  local copies, waits for them, and re-layouts  5.76 us (5%)
  other arithmetic  5.48 us (5%)
    pallas_call x5, Pallas kernels, project(): pl.pallas_call(functools.partial(project_kernel, jobs, load, queries is n...  43.3 us
    ppermute x16, waiting for transfers between devices, send(): return lax.ppermute(x, axis, pairs)  32.3 us
    ppermute x16, starting transfers between devices, send(): return lax.ppermute(x, axis, pairs)  16.6 us
    unnamed x36, local copies, waits for them, and re-layouts  5.76 us
    pallas_call x2, Pallas kernels, split(): pl.pallas_call(split_kernel, in_specs=[SCALARS, WHOLE, WHOLE], out_specs=...  5.11 us
    add x4, other arithmetic, across(): return stay[1] + first[1]  3.84 us
    pallas_call x1, Pallas kernels, score(): pl.pallas_call(functools.partial(score_kernel, pair), in_specs=[SCALARS]...  2.86 us
    pallas_call x1, Pallas kernels, sketches(): pl.pallas_call(functools.partial(sketch_kernel, count, width), in_specs=[...  2.84 us
  transfers between devices with their start and end apart: 16, of which 7 were waited for; matrix products, arithmetic and copies ran while one was open for 4% of the time, Pallas kernels for 39%

profile of v3, /device:TPU:0, one launch (start us, length us, event | category | flops | bytes accessed | tf_op | source)
XLA Modules:
  0.0 114.5 jit_solution(17982503566122691266)
XLA Ops:
  0.1 6.8 %shard_map.91 = f32[2,256,256]{2,1,0:T(8,128)} custom-call(s32[2]{0:T(128)S(1)} %pad_add_fusion.3.index, bf16[2048,2048]{1,0:T(8,128)(2,1)} %refs_0_.9, bf16[2048,7168]{1,0:T(8,128)(2,1)} %refs_1_.9, bf16[128,2048]{1,0:T(8,128)(2,1)} %refs_2_.9, bf16[128,7168]{1,0:T(8,128)(2,1)} %refs_3_.9, bf16[2048,7168]{1,0:T(8,128)(2,1)} %refs_4_.9, ...), custom_call_target="tpu_custom_call" | custom-call | flops 1207959552 | bytes 9437184 | tf_op jit(solution)/shard_map/pallas_call | solution.py:138
  6.9 3.1 %collective-permute-start = (f32[2,256,256]{2,1,0:T(8,128)}, f32[2,256,256]{2,1,0:T(8,128)}, u32[]{:S(2)}, u32[]{:S(2)}) collective-permute-start(f32[2,256,256]{2,1,0:T(8,128)} %shard_map.91), channel_id=1, source_target_pairs={{0,1},{1,0},{2,3},{3,2},{4,5},{5,4},{6,7},{7,6},{8,9},{9,8},{10,11... | collective-permute-start | bytes 1572872 | tf_op jit(solution)/shard_map/ppermute | solution.py:33
  10.0 12.1 %shard_map.92 = (f32[2,256,256]{2,1,0:T(8,128)}, f32[2,256,256]{2,1,0:T(8,128)S(1)}, f32[64,8192]{1,0:T(8,128)}) custom-call(s32[4]{0:T(128)S(1)} %pad_add_fusion.2.index, bf16[2048,2048]{1,0:T(8,128)(2,1)} %refs_0_.9, bf16[2048,7168]{1,0:T(8,128)(2,1)} %refs_1_.9, bf16[128,2048]{1,0:T(8,128)(2,1)S(1)} %copy-done.4, bf16[128,7168]{1,0:T(8,128)(2,1)S(1)} %copy-done, ...), custom_call_target="tpu_custom_call" | custom-call | flops 2415919104 | bytes 18874368 | tf_op jit(solution)/shard_map/pallas_call | solution.py:138
  22.2 1.6 %collective-permute-start.12 = (f32[64,8192]{1,0:T(8,128)}, f32[64,8192]{1,0:T(8,128)}, u32[]{:S(2)}, u32[]{:S(2)}) collective-permute-start(f32[64,8192]{1,0:T(8,128)} %get-tuple-element.44.mine), channel_id=1, source_target_pairs={{0,8},{8,0},{4,12},{12,4},{1,9},{9,1},{5,13},{13,5},{2,10},{10,2},... | collective-permute-start | bytes 6291464 | tf_op jit(solution)/shard_map/ppermute | solution.py:33
  24.2 1.0 fusion.3
  25.2 3.7 %collective-permute-start.1 = (f32[256,256]{1,0:T(8,128)S(1)}, f32[256,256]{1,0:T(8,128)S(1)}, u32[]{:S(2)}, u32[]{:S(2)}) collective-permute-start(f32[256,256]{1,0:T(8,128)S(1)} %fusion.3), channel_id=1, source_target_pairs={{0,3},{3,0},{1,2},{2,1},{4,7},{7,4},{5,6},{6,5},{8,11},{11,8},{9,1... | collective-permute-start | bytes 786440 | tf_op jit(solution)/shard_map/ppermute | solution.py:33
  28.9 1.5 %copy-done.1 = bf16[128,7168]{1,0:T(8,128)(2,1)S(1)} copy-done((bf16[128,7168]{1,0:T(8,128)(2,1)S(1)}, bf16[128,7168]{1,0:T(8,128)(2,1)}, u32[]{:S(2)}) %copy-start.1) | copy-done | bytes 1835032
  30.4 9.2 %shard_map.93 = (f32[2,256,256]{2,1,0:T(8,128)S(1)}, f32[2,256,256]{2,1,0:T(8,128)S(1)}) custom-call(s32[4]{0:T(128)S(1)} %pad_add_fusion.4.index, bf16[2048,2048]{1,0:T(8,128)(2,1)} %refs_0_.9, bf16[2048,7168]{1,0:T(8,128)(2,1)} %refs_1_.9, bf16[128,2048]{1,0:T(8,128)(2,1)S(1)} %copy-done.4, bf16[128,7168]{1,0:T(8,128)(2,1)S(1)} %copy-done, ...), custom_call_target="tpu_custom_call" | custom-call | flops 2415919104 | bytes 18874368 | tf_op jit(solution)/shard_map/pallas_call | solution.py:138
  39.7 6.6 %collective-permute-done.1.refs_8_ = f32[256,256]{1,0:T(8,128)S(1)} collective-permute-done((f32[256,256]{1,0:T(8,128)S(1)}, f32[256,256]{1,0:T(8,128)S(1)}, u32[]{:S(2)}, u32[]{:S(2)}) %collective-permute-start.1) | collective-permute-done | bytes 262176 | tf_op jit(solution)/shard_map/ppermute | solution.py:33
  46.4 1.1 fusion.2
  47.8 9.8 %shard_map.94 = (f32[2,256,256]{2,1,0:T(8,128)}, f32[2,256,256]{2,1,0:T(8,128)S(1)}) custom-call(s32[4]{0:T(128)S(1)} %pad_add_fusion.2.index, bf16[2048,2048]{1,0:T(8,128)(2,1)} %refs_0_.9, bf16[2048,7168]{1,0:T(8,128)(2,1)} %refs_1_.9, bf16[128,2048]{1,0:T(8,128)(2,1)} %refs_2_.9, bf16[128,7168]{1,0:T(8,128)(2,1)} %refs_3_.9, bf16[2048,7168]{1,0:T(8,128)(2,1)} %refs_4_.9, ...), custom_call_target="tpu_custom_call" | custom-call | flops 2415919104 | bytes 18874368 | tf_op jit(solution)/shard_map/pallas_call | solution.py:138
  57.6 5.6 %collective-permute-done.3.refs_9_ = f32[256,256]{1,0:T(8,128)S(1)} collective-permute-done((f32[256,256]{1,0:T(8,128)S(1)}, f32[256,256]{1,0:T(8,128)S(1)}, u32[]{:S(2)}, u32[]{:S(2)}) %collective-permute-start.3) | collective-permute-done | bytes 262176 | tf_op jit(solution)/shard_map/ppermute | solution.py:33
  63.2 0.7 copy-done.16
  63.9 0.8 fusion.1
  65.0 5.5 %shard_map.95.refs_3_ = f32[2,256,256]{2,1,0:T(8,128)S(1)} custom-call(s32[2]{0:T(128)S(1)} %pad_add_fusion.5.index, bf16[2048,2048]{1,0:T(8,128)(2,1)} %refs_0_.9, bf16[2048,7168]{1,0:T(8,128)(2,1)} %refs_1_.9, bf16[128,2048]{1,0:T(8,128)(2,1)} %refs_2_.9, bf16[128,7168]{1,0:T(8,128)(2,1)} %refs_3_.9, bf16[2048,7168]{1,0:T(8,128)(2,1)} %refs_4_.9, ...), custom_call_target="tpu_custom_call" | custom-call | flops 1207959552 | bytes 9437184 | tf_op jit(solution)/shard_map/pallas_call | solution.py:138
  70.6 2.9 %shard_map.96 = (bf16[128,8192]{1,0:T(8,128)(2,1)S(1)}, bf16[128,8192]{1,0:T(8,128)(2,1)S(1)}) custom-call(s32[1]{0:T(128)} %bitcast.17.place, f32[64,8192]{1,0:T(8,128)} %get-tuple-element.44.mine, f32[64,8192]{1,0:T(8,128)} %collective-permute-done.7.other), custom_call_target="tpu_custom_call" | custom-call | flops 4194304 | bytes 8388608 | tf_op jit(solution)/shard_map/pallas_call | solution.py:205
  73.5 1.4 %copy-done.7 = bf16[128,8192]{1,0:T(8,128)(2,1)} copy-done((bf16[128,8192]{1,0:T(8,128)(2,1)}, bf16[128,8192]{1,0:T(8,128)(2,1)S(1)}, u32[]{:S(2)}) %copy-start.7) | copy-done | bytes 2097176
  74.9 1.4 %copy-done.9 = bf16[128,8192]{1,0:T(8,128)(2,1)} copy-done((bf16[128,8192]{1,0:T(8,128)(2,1)}, bf16[128,8192]{1,0:T(8,128)(2,1)S(1)}, u32[]{:S(2)}) %copy-start.9) | copy-done | bytes 2097176
  76.3 3.2 %collective-permute-done.6.refs_10_ = f32[256,256]{1,0:T(8,128)} collective-permute-done((f32[256,256]{1,0:T(8,128)}, f32[256,256]{1,0:T(8,128)}, u32[]{:S(2)}, u32[]{:S(2)}) %collective-permute-start.6) | collective-permute-done | bytes 262176 | tf_op jit(solution)/shard_map/ppermute | solution.py:33
  79.5 1.0 fusion
  81.7 9.4 %collective-permute-done.8.refs_11_ = f32[256,256]{1,0:T(8,128)S(1)} collective-permute-done((f32[256,256]{1,0:T(8,128)S(1)}, f32[256,256]{1,0:T(8,128)S(1)}, u32[]{:S(2)}, u32[]{:S(2)}) %collective-permute-start.8) | collective-permute-done | bytes 262176 | tf_op jit(solution)/shard_map/ppermute | solution.py:33
  91.1 0.7 copy-done.17
  91.8 2.8 %shard_map.97 = (f32[4,32,128]{2,1,0:T(8,128)S(1)}, f32[4,32,128]{2,1,0:T(8,128)S(1)}, f32[4,32,128]{2,1,0:T(8,128)S(1)}, f32[4,32,128]{2,1,0:T(8,128)S(1)}) custom-call(s32[4]{0:T(128)} %pad_add_fusion.1.dest, f32[2,256,256]{2,1,0:T(8,128)} %copy-done.11, f32[2,256,256]{2,1,0:T(8,128)} %copy-done.12, f32[2,256,256]{2,1,0:T(8,128)} %copy-done.13, ...), custom_call_target="tpu_custom_call" | custom-call | flops 134217728 | bytes 2097152 | tf_op jit(solution)/shard_map/pallas_call | solution.py:179
  94.7 1.0 collective-permute-start.10
  95.7 3.4 %collective-permute-start.11 = (f32[4,32,128]{2,1,0:T(8,128)S(1)}, f32[4,32,128]{2,1,0:T(8,128)S(1)}, u32[]{:S(2)}, u32[]{:S(2)}) collective-permute-start(f32[4,32,128]{2,1,0:T(8,128)S(1)} %get-tuple-element.50), channel_id=1, source_target_pairs={{0,3},{3,0},{1,2},{2,1},{4,7},{7,4},{5,6},{6,5},{8,11},{11,8},{9,1... | collective-permute-start | bytes 196616 | tf_op jit(solution)/shard_map/ppermute | solution.py:33
  99.2 2.2 %shard_map.98 = (bf16[128,8192]{1,0:T(8,128)(2,1)S(1)}, bf16[128,8192]{1,0:T(8,128)(2,1)S(1)}) custom-call(s32[1]{0:T(128)} %bitcast.17.place, f32[64,8192]{1,0:T(8,128)} %collective-permute-done.12.mine, f32[64,8192]{1,0:T(8,128)S(1)} %collective-permute-done.13.other), custom_call_target="tpu_custom_call" | custom-call | flops 4194304 | bytes 8388608 | tf_op jit(solution)/shard_map/pallas_call | solution.py:205
  101.4 1.4 %collective-permute-done.10.skip = f32[4,32,128]{2,1,0:T(8,128)S(1)} collective-permute-done((f32[4,32,128]{2,1,0:T(8,128)S(1)}, f32[4,32,128]{2,1,0:T(8,128)S(1)}, u32[]{:S(2)}, u32[]{:S(2)}) %collective-permute-start.10) | collective-permute-done | bytes 65568 | tf_op jit(solution)/shard_map/ppermute | solution.py:33
  102.8 2.9 %shard_map.99 = f32[8,256]{1,0:T(8,128)S(1)} custom-call(s32[2]{0:T(128)S(1)} %pad_add_fusion.place, f32[4,32,128]{2,1,0:T(8,128)S(1)} %get-tuple-element.47.own, f32[4,32,128]{2,1,0:T(8,128)S(1)} %collective-permute-done.9.near, f32[4,32,128]{2,1,0:T(8,128)S(1)} %collective-permute-done.10.skip, f32[4,32,128]{2,1,0:T(8,128)S(1)} %collective-permute-done.11.across, ...), custom_call_target="tpu_custom_call" | custom-call | flops 67108864 | bytes 8388608 | tf_op jit(solution)/shard_map/pallas_call | solution.py:246
  105.7 1.3 %collective-permute-start.14 = (f32[8,256]{1,0:T(8,128)S(1)}, f32[8,256]{1,0:T(8,128)S(1)}, u32[]{:S(2)}, u32[]{:S(2)}) collective-permute-start(f32[8,256]{1,0:T(8,128)S(1)} %shard_map.99), channel_id=1, source_target_pairs={{0,1},{1,0},{2,3},{3,2},{4,5},{5,4},{6,7},{7,6},{8,9},{9,8},{10,11... | collective-permute-start | bytes 24584 | tf_op jit(solution)/shard_map/ppermute | solution.py:33
  107.0 2.4 %collective-permute-done.14 = f32[8,256]{1,0:T(8,128)S(1)} collective-permute-done((f32[8,256]{1,0:T(8,128)S(1)}, f32[8,256]{1,0:T(8,128)S(1)}, u32[]{:S(2)}, u32[]{:S(2)}) %collective-permute-start.14) | collective-permute-done | bytes 8224 | tf_op jit(solution)/shard_map/ppermute | solution.py:33
  109.4 0.8 collective-permute-start.15
  110.2 3.7 %collective-permute-done.15 = f32[8,256]{1,0:T(8,128)S(1)} collective-permute-done((f32[8,256]{1,0:T(8,128)S(1)}, f32[8,256]{1,0:T(8,128)S(1)}, u32[]{:S(2)}, u32[]{:S(2)}) %collective-permute-start.15) | collective-permute-done | bytes 8224 | tf_op jit(solution)/shard_map/ppermute | solution.py:33
  (57 shorter events, 3.5 us)
Async XLA Ops:
  0.1 10.0 %copy-start = (bf16[128,7168]{1,0:T(8,128)(2,1)S(1)}, bf16[128,7168]{1,0:T(8,128)(2,1)}, u32[]{:S(2)}) copy-start(bf16[128,7168]{1,0:T(8,128)(2,1)} %refs_3_.9) | copy-start | bytes 5505028
  0.1 10.0 %copy-start.4 = (bf16[128,2048]{1,0:T(8,128)(2,1)S(1)}, bf16[128,2048]{1,0:T(8,128)(2,1)}, u32[]{:S(2)}) copy-start(bf16[128,2048]{1,0:T(8,128)(2,1)} %refs_2_.9) | copy-start | bytes 1572868
  6.9 17.3 %collective-permute-start = (f32[2,256,256]{2,1,0:T(8,128)}, f32[2,256,256]{2,1,0:T(8,128)}, u32[]{:S(2)}, u32[]{:S(2)}) collective-permute-start(f32[2,256,256]{2,1,0:T(8,128)} %shard_map.91), channel_id=1, source_target_pairs={{0,1},{1,0},{2,3},{3,2},{4,5},{5,4},{6,7},{7,6},{8,9},{9,8},{10,11... | collective-permute-start | bytes 1572872 | tf_op jit(solution)/shard_map/ppermute | solution.py:33
  10.0 18.9 %copy-start.5 = (bf16[128,2048]{1,0:T(8,128)(2,1)S(1)}, bf16[128,2048]{1,0:T(8,128)(2,1)}, u32[]{:S(2)}) copy-start(bf16[128,2048]{1,0:T(8,128)(2,1)} %refs_7_.9) | copy-start | bytes 1572868
  22.1 17.5 %copy-start.11 = (f32[2,256,256]{2,1,0:T(8,128)}, f32[2,256,256]{2,1,0:T(8,128)S(1)}, u32[]{:S(2)}) copy-start(f32[2,256,256]{2,1,0:T(8,128)S(1)} %get-tuple-element.33.refs_0_) | copy-start | bytes 1572868
  22.1 48.5 %collective-permute-start.7 = (f32[64,8192]{1,0:T(8,128)}, f32[64,8192]{1,0:T(8,128)}, u32[]{:S(2)}, u32[]{:S(2)}) collective-permute-start(f32[64,8192]{1,0:T(8,128)} %get-tuple-element.44.mine), channel_id=1, source_target_pairs={{0,4},{4,0},{8,12},{12,8},{1,5},{5,1},{9,13},{13,9},{2,6},{6,2},{1... | collective-permute-start | bytes 6291464 | tf_op jit(solution)/shard_map/ppermute | solution.py:33
  22.2 58.3 %collective-permute-start.12 = (f32[64,8192]{1,0:T(8,128)}, f32[64,8192]{1,0:T(8,128)}, u32[]{:S(2)}, u32[]{:S(2)}) collective-permute-start(f32[64,8192]{1,0:T(8,128)} %get-tuple-element.44.mine), channel_id=1, source_target_pairs={{0,8},{8,0},{4,12},{12,4},{1,9},{9,1},{5,13},{13,5},{2,10},{10,2},... | collective-permute-start | bytes 6291464 | tf_op jit(solution)/shard_map/ppermute | solution.py:33
  23.7 22.6 %collective-permute-start.2 = (f32[2,256,256]{2,1,0:T(8,128)}, f32[2,256,256]{2,1,0:T(8,128)}, u32[]{:S(2)}, u32[]{:S(2)}) collective-permute-start(f32[2,256,256]{2,1,0:T(8,128)} %get-tuple-element.32), channel_id=1, source_target_pairs={{0,1},{1,0},{2,3},{3,2},{4,5},{5,4},{6,7},{7,6},{8,9},{9,8},{10,11... | collective-permute-start | bytes 1572872 | tf_op jit(solution)/shard_map/ppermute | solution.py:33
  25.2 21.2 %collective-permute-start.1 = (f32[256,256]{1,0:T(8,128)S(1)}, f32[256,256]{1,0:T(8,128)S(1)}, u32[]{:S(2)}, u32[]{:S(2)}) collective-permute-start(f32[256,256]{1,0:T(8,128)S(1)} %fusion.3), channel_id=1, source_target_pairs={{0,3},{3,0},{1,2},{2,1},{4,7},{7,4},{5,6},{6,5},{8,11},{11,8},{9,1... | collective-permute-start | bytes 786440 | tf_op jit(solution)/shard_map/ppermute | solution.py:33
  28.9 1.5 %copy-start.1 = (bf16[128,7168]{1,0:T(8,128)(2,1)S(1)}, bf16[128,7168]{1,0:T(8,128)(2,1)}, u32[]{:S(2)}) copy-start(bf16[128,7168]{1,0:T(8,128)(2,1)} %refs_6_.9) | copy-start | bytes 5505028
  30.4 17.3 %copy-start.2 = (bf16[128,7168]{1,0:T(8,128)(2,1)S(1)}, bf16[128,7168]{1,0:T(8,128)(2,1)}, u32[]{:S(2)}) copy-start(bf16[128,7168]{1,0:T(8,128)(2,1)} %refs_6_.9) | copy-start | bytes 5505028
  39.7 6.7 %copy-start.12 = (f32[2,256,256]{2,1,0:T(8,128)}, f32[2,256,256]{2,1,0:T(8,128)S(1)}, u32[]{:S(2)}) copy-start(f32[2,256,256]{2,1,0:T(8,128)S(1)} %get-tuple-element.37.refs_1_) | copy-start | bytes 1572868
  39.7 23.6 %collective-permute-start.4 = (f32[2,256,256]{2,1,0:T(8,128)S(1)}, f32[2,256,256]{2,1,0:T(8,128)S(1)}, u32[]{:S(2)}, u32[]{:S(2)}) collective-permute-start(f32[2,256,256]{2,1,0:T(8,128)S(1)} %get-tuple-element.36), channel_id=1, source_target_pairs={{0,1},{1,0},{2,3},{3,2},{4,5},{5,4},{6,7},{7,6},{8,9},{9,8},{10,11... | collective-permute-start | bytes 1572872 | tf_op jit(solution)/shard_map/ppermute | solution.py:33
  46.4 1.1 copy-start.15
  47.5 17.5 %copy-start.3 = (bf16[128,7168]{1,0:T(8,128)(2,1)S(1)}, bf16[128,7168]{1,0:T(8,128)(2,1)}, u32[]{:S(2)}) copy-start(bf16[128,7168]{1,0:T(8,128)(2,1)} %refs_6_.9) | copy-start | bytes 5505028
  47.5 15.7 %collective-permute-start.3 = (f32[256,256]{1,0:T(8,128)S(1)}, f32[256,256]{1,0:T(8,128)S(1)}, u32[]{:S(2)}, u32[]{:S(2)}) collective-permute-start(f32[256,256]{1,0:T(8,128)S(1)} %fusion.2), channel_id=1, source_target_pairs={{0,3},{3,0},{1,2},{2,1},{4,7},{7,4},{5,6},{6,5},{8,11},{11,8},{9,1... | collective-permute-start | bytes 786440 | tf_op jit(solution)/shard_map/ppermute | solution.py:33
  57.6 13.0 %copy-start.13 = (f32[2,256,256]{2,1,0:T(8,128)}, f32[2,256,256]{2,1,0:T(8,128)S(1)}, u32[]{:S(2)}) copy-start(f32[2,256,256]{2,1,0:T(8,128)S(1)} %get-tuple-element.41.refs_2_) | copy-start | bytes 1572868
  57.6 21.9 %collective-permute-start.5 = (f32[2,256,256]{2,1,0:T(8,128)}, f32[2,256,256]{2,1,0:T(8,128)}, u32[]{:S(2)}, u32[]{:S(2)}) collective-permute-start(f32[2,256,256]{2,1,0:T(8,128)} %get-tuple-element.40), channel_id=1, source_target_pairs={{0,1},{1,0},{2,3},{3,2},{4,5},{5,4},{6,7},{7,6},{8,9},{9,8},{10,11... | collective-permute-start | bytes 1572872 | tf_op jit(solution)/shard_map/ppermute | solution.py:33
  63.9 1.0 copy-start.14
  64.7 14.7 %collective-permute-start.6 = (f32[256,256]{1,0:T(8,128)}, f32[256,256]{1,0:T(8,128)}, u32[]{:S(2)}, u32[]{:S(2)}) collective-permute-start(f32[256,256]{1,0:T(8,128)} %fusion.1), channel_id=1, source_target_pairs={{0,3},{3,0},{1,2},{2,1},{4,7},{7,4},{5,6},{6,5},{8,11},{11,8},{9,1... | collective-permute-start | bytes 786440 | tf_op jit(solution)/shard_map/ppermute | solution.py:33
  70.6 8.9 %copy-start.6 = (f32[2,256,256]{2,1,0:T(8,128)}, f32[2,256,256]{2,1,0:T(8,128)S(1)}, u32[]{:S(2)}) copy-start(f32[2,256,256]{2,1,0:T(8,128)S(1)} %shard_map.95.refs_3_) | copy-start | bytes 1572868
  73.5 1.4 %copy-start.7 = (bf16[128,8192]{1,0:T(8,128)(2,1)}, bf16[128,8192]{1,0:T(8,128)(2,1)S(1)}, u32[]{:S(2)}) copy-start(bf16[128,8192]{1,0:T(8,128)(2,1)S(1)} %get-tuple-element.45.refs_0_) | copy-start | bytes 6291460
  74.9 1.4 %copy-start.9 = (bf16[128,8192]{1,0:T(8,128)(2,1)}, bf16[128,8192]{1,0:T(8,128)(2,1)S(1)}, u32[]{:S(2)}) copy-start(bf16[128,8192]{1,0:T(8,128)(2,1)S(1)} %get-tuple-element.51.refs_1_) | copy-start | bytes 6291460
  80.5 18.7 %collective-permute-start.13 = (f32[64,8192]{1,0:T(8,128)}, f32[64,8192]{1,0:T(8,128)S(1)}, u32[]{:S(2)}, u32[]{:S(2)}) collective-permute-start(f32[64,8192]{1,0:T(8,128)} %collective-permute-done.12.mine), channel_id=1, source_target_pairs={{0,4},{4,0},{8,12},{12,8},{1,5},{5,1},{9,13},{13,9},{2,6},{6,2},{1... | collective-permute-start | bytes 6291464 | tf_op jit(solution)/shard_map/ppermute | solution.py:33
  80.5 10.5 %collective-permute-start.8 = (f32[256,256]{1,0:T(8,128)S(1)}, f32[256,256]{1,0:T(8,128)S(1)}, u32[]{:S(2)}, u32[]{:S(2)}) collective-permute-start(f32[256,256]{1,0:T(8,128)S(1)} %fusion), channel_id=1, source_target_pairs={{0,3},{3,0},{1,2},{2,1},{4,7},{7,4},{5,6},{6,5},{8,11},{11,8},{9,1... | collective-permute-start | bytes 786440 | tf_op jit(solution)/shard_map/ppermute | solution.py:33
  94.6 6.8 %collective-permute-start.9 = (f32[4,32,128]{2,1,0:T(8,128)S(1)}, f32[4,32,128]{2,1,0:T(8,128)S(1)}, u32[]{:S(2)}, u32[]{:S(2)}) collective-permute-start(f32[4,32,128]{2,1,0:T(8,128)S(1)} %get-tuple-element.48), channel_id=1, source_target_pairs={{0,1},{1,0},{2,3},{3,2},{4,5},{5,4},{6,7},{7,6},{8,9},{9,8},{10,11... | collective-permute-start | bytes 196616 | tf_op jit(solution)/shard_map/ppermute | solution.py:33
  94.7 8.1 %collective-permute-start.10 = (f32[4,32,128]{2,1,0:T(8,128)S(1)}, f32[4,32,128]{2,1,0:T(8,128)S(1)}, u32[]{:S(2)}, u32[]{:S(2)}) collective-permute-start(f32[4,32,128]{2,1,0:T(8,128)S(1)} %get-tuple-element.49), channel_id=1, source_target_pairs={{0,2},{2,0},{1,3},{3,1},{4,6},{6,4},{5,7},{7,5},{8,10},{10,8},{9,1... | collective-permute-start | bytes 196616 | tf_op jit(solution)/shard_map/ppermute | solution.py:33
  95.7 7.2 %collective-permute-start.11 = (f32[4,32,128]{2,1,0:T(8,128)S(1)}, f32[4,32,128]{2,1,0:T(8,128)S(1)}, u32[]{:S(2)}, u32[]{:S(2)}) collective-permute-start(f32[4,32,128]{2,1,0:T(8,128)S(1)} %get-tuple-element.50), channel_id=1, source_target_pairs={{0,3},{3,0},{1,2},{2,1},{4,7},{7,4},{5,6},{6,5},{8,11},{11,8},{9,1... | collective-permute-start | bytes 196616 | tf_op jit(solution)/shard_map/ppermute | solution.py:33
  99.2 3.7 %copy-start.8 = (bf16[128,8192]{1,0:T(8,128)(2,1)S(1)}, bf16[128,8192]{1,0:T(8,128)(2,1)}, u32[]{:S(2)}) copy-start(bf16[128,8192]{1,0:T(8,128)(2,1)} %copy-done.7) | copy-start | bytes 6291460
  99.2 3.7 %copy-start.10 = (bf16[128,8192]{1,0:T(8,128)(2,1)S(1)}, bf16[128,8192]{1,0:T(8,128)(2,1)}, u32[]{:S(2)}) copy-start(bf16[128,8192]{1,0:T(8,128)(2,1)} %copy-done.9) | copy-start | bytes 6291460
  105.7 3.7 %collective-permute-start.14 = (f32[8,256]{1,0:T(8,128)S(1)}, f32[8,256]{1,0:T(8,128)S(1)}, u32[]{:S(2)}, u32[]{:S(2)}) collective-permute-start(f32[8,256]{1,0:T(8,128)S(1)} %shard_map.99), channel_id=1, source_target_pairs={{0,1},{1,0},{2,3},{3,2},{4,5},{5,4},{6,7},{7,6},{8,9},{9,8},{10,11... | collective-permute-start | bytes 24584 | tf_op jit(solution)/shard_map/ppermute | solution.py:33
  109.4 4.5 %collective-permute-start.15 = (f32[8,256]{1,0:T(8,128)S(1)}, f32[8,256]{1,0:T(8,128)S(1)}, u32[]{:S(2)}, u32[]{:S(2)}) collective-permute-start(f32[8,256]{1,0:T(8,128)S(1)} %add.58), channel_id=1, source_target_pairs={{0,2},{2,0},{1,3},{3,1},{4,6},{6,4},{5,7},{7,5},{8,10},{10,8},{9,1... | collective-permute-start | bytes 24584 | tf_op jit(solution)/shard_map/ppermute | solution.py:33
  (2 other events, 1.4 us)

commit v4 on v3

--- a/solution.py
+++ b/solution.py
@@ -42,19 +42,8 @@
     return [(lo, min(lo + PIECE, width)) for lo in range(0, width, PIECE)]
 
 
-def project_kernel(jobs, load, spread, index, *refs):
+def project_kernel(jobs, load, index, *refs):
     operands, refs = refs[:8], refs[8:]
-    moves = []
-    if spread:
-        queries, refs = refs[0], refs[1:]
-        flat, spread_sem = refs[len(jobs)], refs[-1]
-        refs = refs[: len(jobs)] + refs[len(jobs) + 1 : -1]
-        for r in range(queries.shape[1]):
-            moves.append(
-                pltpu.make_async_copy(
-                    queries.at[:, r, :], flat.at[:, r * K : (r + 1) * K], spread_sem.at[r]
-                )
-            )
     arrays, (slots, sem, *loaded) = refs[: len(jobs)], refs[len(jobs) :]
     depth = slots.shape[0]
     steps = []
@@ -86,8 +75,6 @@
     for step in steps[: depth - 1]:
         for copy in step[0]:
             copy.start()
-    for move in moves:
-        move.start()
     for n, (copies, slot, outs, p, row, lo, hi) in enumerate(steps):
         for copy in copies:
             copy.wait()
@@ -105,11 +92,9 @@
                 out[row : row + K, :] = part[:, m * LEN : (m + 1) * LEN]
             else:
                 out[row : row + K, :] += part[:, m * LEN : (m + 1) * LEN]
-    for move in moves:
-        move.wait()
-
-
-def project(layers, jobs, load=False, after=None, queries=None):
+
+
+def project(layers, jobs, load=False, after=None):
     index = jnp.stack([i for _, group in jobs for i in group]).astype(jnp.int32)
     if after is not None:
         index = lax.optimization_barrier((index, after))[0]
@@ -128,20 +113,13 @@
         operands += [there(left), there(right)]
         operands += [place(p) if used else there(p) for p in (p_left, p_right)]
         specs += [OUTSIDE, OUTSIDE] + [OUTSIDE if load or not used else WHOLE] * 2
-    extra = []
-    if queries is not None:
-        operands.append(there(queries))
-        specs.append(OUTSIDE)
-        count, per_query, _ = queries.shape
-        extra = [pltpu.VMEM((count, per_query * K), queries.dtype)]
-        scratch.append(pltpu.SemaphoreType.DMA((per_query,)))
     return pl.pallas_call(
-        functools.partial(project_kernel, jobs, load, queries is not None),
+        functools.partial(project_kernel, jobs, load),
         in_specs=[SCALARS] + specs,
-        out_specs=[WHOLE] * (len(jobs) + len(extra)),
-        out_shape=[pltpu.VMEM((n, 2 * K, LEN), jnp.float32) for _, n in jobs] + extra,
+        out_specs=[WHOLE] * len(jobs),
+        out_shape=[pltpu.VMEM((n, 2 * K, LEN), jnp.float32) for _, n in jobs],
         scratch_shapes=scratch,
-        compiler_params=pltpu.CompilerParams(vmem_limit_bytes=16 * 2**20),
+        compiler_params=pltpu.CompilerParams(vmem_limit_bytes=12 * 2**20),
         cost_estimate=pl.CostEstimate(
             flops=sum(
                 2 * n * LEN * K * (layers[layer][0].shape[1] + layers[layer][1].shape[1])
@@ -156,14 +134,17 @@
     )(index, *operands)
 
 
-def sketch_kernel(count, width, dest, *refs):
-    own, first, second, outs, full = (
+def sketch_kernel(count, width, before, dest, *refs):
+    own, first, second, made, outs, full = (
         refs[:count],
         refs[count : 2 * count],
         refs[2 * count : 3 * count],
-        refs[3 * count : -1],
+        refs[3 * count : -5],
+        refs[-5:-1],
         refs[-1],
     )
+    for earlier, out in zip(made, outs):
+        out[:before] = earlier[...]
     for i in range(count):
         high, low = halves(own[i][0] + first[i][0] + second[i][...])
         a = jnp.concatenate([high[:K], low[:K]], 0)
@@ -171,89 +152,111 @@
         s = lax.dot_general(a, b, ROWS_BY_ROWS, preferred_element_type=jnp.float32)
         full[...] = s[:K, :K] + (s[:K, K:] + s[K:, :K] + s[K:, K:])
         for n, out in enumerate(outs):
-            out[i] = full[pl.ds(pl.multiple_of(dest[n] * width, 8), width), :]
-
-
-def sketches(dest, own, first, second, width):
+            out[before + i] = full[pl.ds(pl.multiple_of(dest[n] * width, 8), width), :]
+
+
+def sketches(dest, own, first, second, width, made=()):
     count = len(own)
+    before = made[0].shape[0] if made else 0
+    total = before + count
     return pl.pallas_call(
-        functools.partial(sketch_kernel, count, width),
-        in_specs=[SCALARS] + [WHOLE] * (3 * count),
+        functools.partial(sketch_kernel, count, width, before),
+        in_specs=[SCALARS] + [WHOLE] * (3 * count + len(made)),
         out_specs=[WHOLE] * 4,
-        out_shape=[pltpu.VMEM((count, width, K), jnp.float32)] * 4,
+        out_shape=[pltpu.VMEM((total, width, K), jnp.float32)] * 4,
         scratch_shapes=[pltpu.VMEM((K, K), jnp.float32)],
+        compiler_params=pltpu.CompilerParams(vmem_limit_bytes=8 * 2**20),
         cost_estimate=pl.CostEstimate(
             flops=8 * count * LEN * K * K, bytes_accessed=count * 2**19, transcendentals=0
         ),
-    )(dest, *own, *first, *second)
-
-
-def split_kernel(place, mine, other, high, low):
-    count, depth = mine.shape
-    for n, x in enumerate((mine, other)):
+    )(dest, *own, *first, *second, *made)
+
+
+def split_kernel(place, mine, other, high, low, flat, sem):
+    count, rows, _ = mine.shape
+    moves = [
+        [
+            pltpu.make_async_copy(x.at[:, r, :], flat.at[n, :, r * K : (r + 1) * K], sem.at[n, r])
+            for r in range(rows)
+        ]
+        for n, x in enumerate((mine, other))
+    ]
+    for move in moves[0] + moves[1]:
+        move.start()
+    step = 4
+    for n in range(2):
         at = pl.ds(pl.multiple_of((place[0] ^ n) * count, 16), count)
-        for lo in range(0, depth, 512):
-            h, l = halves(x[:, lo : lo + 512])
-            high[at, lo : lo + 512] = h
-            low[at, lo : lo + 512] = l
+        for r in range(0, rows, step):
+            for move in moves[n][r : r + step]:
+                move.wait()
+            lanes = slice(r * K, (r + step) * K)
+            h, l = halves(flat[n, :, lanes])
+            high[at, lanes] = h
+            low[at, lanes] = l
 
 
 def split(core, mine, other, after=None):
-    count, depth = mine.shape
+    count, rows, _ = mine.shape
     if after is not None:
         core = lax.optimization_barrier((core, after))[0]
     return pl.pallas_call(
         split_kernel,
-        in_specs=[SCALARS, WHOLE, WHOLE],
+        in_specs=[SCALARS, OUTSIDE, OUTSIDE],
         out_specs=[WHOLE] * 2,
-        out_shape=[pltpu.VMEM((2 * count, depth), jnp.bfloat16)] * 2,
-        compiler_params=pltpu.CompilerParams(vmem_limit_bytes=16 * 2**20),
+        out_shape=[pltpu.VMEM((2 * count, rows * K), jnp.bfloat16)] * 2,
+        scratch_shapes=[
+            pltpu.VMEM((2, count, rows * K), jnp.float32),
+            pltpu.SemaphoreType.DMA((2, rows)),
+        ],
+        compiler_params=pltpu.CompilerParams(vmem_limit_bytes=8 * 2**20),
         cost_estimate=pl.CostEstimate(
-            flops=8 * count * depth, bytes_accessed=16 * count * depth, transcendentals=0
+            flops=8 * count * rows * K, bytes_accessed=16 * count * rows * K, transcendentals=0
         ),
-    )(core, mine, other)
-
-
-def score_kernel(pair, place, own, near, skip, across, *refs):
-    parts, out, cat = refs[:4], refs[4], refs[5]
-    z, chip = place[0], place[1]
-    width = own.shape[1]
+    )(core, there(mine), there(other))
+
+
+def score_kernel(chunks, pair, chip, dest, *refs):
+    cuts, parts, base, out, cat = refs[:4], refs[4:8], refs[8:-2], refs[-2], refs[-1]
+    width = cuts[0].shape[1]
     count = 4 * pair
-    for layer in range(2):
-        for r in range(width):
-            lanes = slice((layer * width + r) * K, (layer * width + r + 1) * K)
-            mine = slice(layer * pair, (layer + 1) * pair)
-            cut = [x[mine, r, :] for x in (own, near, skip, across)]
-            for b in range(4):
-                pick = jnp.where(z == b ^ 2, cut[2], jnp.where(z == 3 - b, cut[3], cut[0]))
-                high, low = halves(jnp.where(z == b ^ 1, cut[1], pick))
-                cat[b * pair : (b + 1) * pair, lanes] = high.astype(jnp.float32)
-                cat[count + b * pair : count + (b + 1) * pair, lanes] = low.astype(jnp.float32)
-    s = cat[...].astype(jnp.bfloat16)
+    used = sorted({k // pair for k in chunks})
+    depth = width * K
+    cat[...] = jnp.zeros_like(cat)
+    for i, k in enumerate(chunks):
+        layer, j = divmod(k, pair)
+        rows = slice(used.index(layer) * width, (used.index(layer) + 1) * width)
+        for n, cut in enumerate(cuts):
+            high, low = halves(cut[i])
+            cat[dest[n] * pair + j, rows, :] = high.astype(jnp.float32)
+            cat[count + dest[n] * pair + j, rows, :] = low.astype(jnp.float32)
+    s = jnp.concatenate([cat[:, r, :] for r in range(cat.shape[1])], 1).astype(jnp.bfloat16)
+    lanes = slice(used[0] * depth, (used[-1] + 1) * depth)
     totals = []
     for high, low in (parts[:2], parts[2:]):
-        d = lax.dot_general(s, high[...], ROWS_BY_ROWS, preferred_element_type=jnp.float32)
-        d += lax.dot_general(s, low[...], ROWS_BY_ROWS, preferred_element_type=jnp.float32)
+        d = lax.dot_general(s, high[:, lanes], ROWS_BY_ROWS, preferred_element_type=jnp.float32)
+        d += lax.dot_general(s, low[:, lanes], ROWS_BY_ROWS, preferred_element_type=jnp.float32)
         totals.append((d[:count] + d[count:]) * (1.0 / (LEN**0.5 * K)))
     mine, other = totals
-    out[...] = jnp.concatenate(
-        [jnp.where(chip == 0, mine, other), jnp.where(chip == 0, other, mine)], 1
-    )
-
-
-def score(place, cuts, parts, pair):
-    queries, depth = parts[0].shape
+    first = chip[0] == 0
+    total = jnp.concatenate([jnp.where(first, mine, other), jnp.where(first, other, mine)], 1)
+    out[...] = total + base[0][...] if base else total
+
+
+def score(chip, dest, cuts, parts, chunks, pair, base=None):
+    queries, _ = parts[0].shape
+    rows = len({k // pair for k in chunks}) * cuts[0].shape[1]
+    more = [] if base is None else [base]
     return pl.pallas_call(
-        functools.partial(score_kernel, pair),
-        in_specs=[SCALARS] + [WHOLE] * 8,
+        functools.partial(score_kernel, chunks, pair),
+        in_specs=[SCALARS, SCALARS] + [WHOLE] * (8 + len(more)),
         out_specs=WHOLE,
         out_shape=pltpu.VMEM((4 * pair, 2 * queries), jnp.float32),
-        scratch_shapes=[pltpu.VMEM((8 * pair, depth), jnp.float32)],
-        compiler_params=pltpu.CompilerParams(vmem_limit_bytes=24 * 2**20),
+        scratch_shapes=[pltpu.VMEM((8 * pair, rows, K), jnp.float32)],
+        compiler_params=pltpu.CompilerParams(vmem_limit_bytes=8 * 2**20),
         cost_estimate=pl.CostEstimate(
-            flops=64 * queries * depth, bytes_accessed=8 * queries * depth, transcendentals=0
+            flops=64 * queries * rows * K, bytes_accessed=8 * queries * rows * K, transcendentals=0
         ),
-    )(place, *cuts, *parts)
+    )(chip, dest, *cuts, *parts, *more)
 
 
 def line(
@@ -288,36 +291,40 @@
         return stay[1] + first[1]
 
     chunks = 2 * pair
+    chip = (dp >> 1).reshape(1)
+    dest = jnp.stack([z, z ^ 1, z ^ 2, 3 - z])
     stay, first, second = [], [], []
     (out,) = project(layers, [leaving(0)], load=True)
     first.append(send(out, NEAR))
     order = out
+    queries = lax.optimization_barrier((queries, out))[0]
+    other_core = send(queries, by_core, "dp")
+    other_chip = send(queries, by_chip, "dp")
     for k in range(chunks):
-        if k == 0:
-            out, kept, flat = project(layers, [leaving(1), staying(0)], after=order, queries=queries)
-            other_core = send(flat, by_core, "dp")
-            other_chip = send(flat, by_chip, "dp")
-        elif k < chunks - 1:
+        if k < chunks - 1:
             out, kept = project(layers, [leaving(k + 1), staying(k)], after=order)
+            first.append(send(out, NEAR))
+            order = (out,)
         else:
             (kept,) = project(layers, [staying(k)], after=order)
+            parts = split(core, queries, other_core, after=kept)
+            order = (parts[0],)
         stay.append(kept)
-        if k < chunks - 1:
-            first.append(send(out, NEAR))
-            order = (out,) + tuple(second[-1:])
-        else:
-            own_chip = split(core, flat, other_core, after=kept)
-            order = (own_chip[0],) + tuple(second[-1:])
-        order = across(kept, first[k], order)
+        order = across(kept, first[k], order + tuple(second[-1:]))
         second.append(send(order, ACROSS))
     other_chip = lax.optimization_barrier((other_chip, order))[0]
-    other_both = send(other_chip, by_core, "dp")
-    parts = own_chip + split(core, other_chip, other_both)
-
-    dest = jnp.stack([z, z ^ 1, z ^ 2, 3 - z])
-    own, near, skip, far = sketches(dest, stay, first, second, width)
+    parts += split(core, other_chip, send(other_chip, by_core, "dp"))
+    few = list(range(chunks - 1))
+    made = sketches(
+        lax.optimization_barrier((dest, order))[0],
+        [stay[k] for k in few],
+        [first[k] for k in few],
+        [second[k] for k in few],
+        width,
+    )
+    own, near, skip, far = sketches(dest, stay[-1:], first[-1:], second[-1:], width, made=made)
     cuts = [own, send(near, NEAR), send(skip, SKIP), send(far, ACROSS)]
-    partial = score(jnp.stack([z, dp >> 1]), cuts, parts, pair)
+    partial = score(chip, dest, cuts, parts, list(range(chunks)), pair)
     partial = partial + send(partial, NEAR)
     return partial + send(partial, SKIP)
 

time: 115 us -> 111 us (0.965)
  waiting for transfers between devices: 32.3 us -> 27.7 us
  starting transfers between devices: 16.6 us -> 17.8 us
    ppermute x16, waiting for transfers between devices: 32.3 us -> 27.7 us  [send(): return lax.ppermute(x, axis, pairs)]
    ppermute x16, starting transfers between devices: 16.6 us -> 17.8 us  [send(): return lax.ppermute(x, axis, pairs)]
    unnamed x36 -> x40, local copies, waits for them, and re-layouts: 5.76 us -> 5.87 us
    pallas_call x9 -> x10, Pallas kernels: 54.1 us -> 54.1 us  [the longest x5 40.5 us: project(): pl.pallas_call(functools.partial(project_kernel, jobs, load), in_specs=[S...]
  transfers between devices with their start and end apart: 16 -> 16, of which waited for: 7 -> 6; matrix products, arithmetic and copies ran while one was open for 4% -> 4% of each run, Pallas kernels for 39% -> 40%
where the time goes in v4:
time: 111 us
  Pallas kernels  54.1 us (49%)
  waiting for transfers between devices  27.7 us (25%)
  starting transfers between devices  17.8 us (16%)
  local copies, waits for them, and re-layouts  5.87 us (5%)
  other arithmetic  4.81 us (4%)
    pallas_call x5, Pallas kernels, project(): pl.pallas_call(functools.partial(project_kernel, jobs, load), in_specs=[S...  40.5 us
    ppermute x16, waiting for transfers between devices, send(): return lax.ppermute(x, axis, pairs)  27.7 us
    ppermute x16, starting transfers between devices, send(): return lax.ppermute(x, axis, pairs)  17.8 us
    pallas_call x2, Pallas kernels, split(): pl.pallas_call(split_kernel, in_specs=[SCALARS, OUTSIDE, OUTSIDE], out_sp...  7.96 us
    unnamed x40, local copies, waits for them, and re-layouts  5.87 us
    add x4, other arithmetic, across(): return stay[1] + first[1]  3.83 us
    pallas_call x1, Pallas kernels, score(): pl.pallas_call(functools.partial(score_kernel, chunks, pair), in_specs=[S...  2.84 us
    pallas_call x2, Pallas kernels, sketches(): pl.pallas_call(functools.partial(sketch_kernel, count, width, before), in...  2.79 us
  transfers between devices with their start and end apart: 16, of which 6 were waited for; matrix products, arithmetic and copies ran while one was open for 4% of the time, Pallas kernels for 40%

profile of v4, /device:TPU:0, one launch (start us, length us, event | category | flops | bytes accessed | tf_op | source)
XLA Modules:
  0.0 110.6 jit_solution(12494880631690758116)
XLA Ops:
  0.1 6.8 %shard_map.91 = f32[2,256,256]{2,1,0:T(8,128)} custom-call(s32[2]{0:T(128)S(1)} %pad_add_fusion.4.index, bf16[2048,2048]{1,0:T(8,128)(2,1)} %refs_0_.9, bf16[2048,7168]{1,0:T(8,128)(2,1)} %refs_1_.9, bf16[128,2048]{1,0:T(8,128)(2,1)} %refs_2_.9, bf16[128,7168]{1,0:T(8,128)(2,1)} %refs_3_.9, bf16[2048,7168]{1,0:T(8,128)(2,1)} %refs_4_.9, ...), custom_call_target="tpu_custom_call" | custom-call | flops 1207959552 | bytes 9437184 | tf_op jit(solution)/shard_map/pallas_call | solution.py:116
  6.9 3.1 %collective-permute-start = (f32[2,256,256]{2,1,0:T(8,128)}, f32[2,256,256]{2,1,0:T(8,128)S(1)}, u32[]{:S(2)}, u32[]{:S(2)}) collective-permute-start(f32[2,256,256]{2,1,0:T(8,128)} %shard_map.91), channel_id=1, source_target_pairs={{0,1},{1,0},{2,3},{3,2},{4,5},{5,4},{6,7},{7,6},{8,9},{9,8},{10,11... | collective-permute-start | bytes 1572872 | tf_op jit(solution)/shard_map/ppermute | solution.py:33
  9.9 1.5 %collective-permute-start.12 = (f32[64,64,128]{2,1,0:T(8,128)}, f32[64,64,128]{2,1,0:T(8,128)}, u32[]{:S(2)}, u32[]{:S(2)}) collective-permute-start(f32[64,64,128]{2,1,0:T(8,128)} %bitcast.17.mine), channel_id=1, source_target_pairs={{0,8},{8,0},{4,12},{12,4},{1,9},{9,1},{5,13},{13,5},{2,10},{10,2},... | collective-permute-start | bytes 6291464 | tf_op jit(solution)/shard_map/ppermute | solution.py:33
  11.5 9.5 %shard_map.92 = (f32[2,256,256]{2,1,0:T(8,128)}, f32[2,256,256]{2,1,0:T(8,128)S(1)}) custom-call(s32[4]{0:T(128)S(1)} %pad_add_fusion.2.index, bf16[2048,2048]{1,0:T(8,128)(2,1)} %refs_0_.9, bf16[2048,7168]{1,0:T(8,128)(2,1)} %refs_1_.9, bf16[128,2048]{1,0:T(8,128)(2,1)S(1)} %copy-done.4, bf16[128,7168]{1,0:T(8,128)(2,1)S(1)} %copy-done, ...), custom_call_target="tpu_custom_call" | custom-call | flops 2415919104 | bytes 18874368 | tf_op jit(solution)/shard_map/pallas_call | solution.py:116
  21.0 0.8 copy-done.10
  22.2 1.0 fusion.3
  23.2 3.7 %collective-permute-start.1 = (f32[256,256]{1,0:T(8,128)S(1)}, f32[256,256]{1,0:T(8,128)S(1)}, u32[]{:S(2)}, u32[]{:S(2)}) collective-permute-start(f32[256,256]{1,0:T(8,128)S(1)} %fusion.3), channel_id=1, source_target_pairs={{0,3},{3,0},{1,2},{2,1},{4,7},{7,4},{5,6},{6,5},{8,11},{11,8},{9,1... | collective-permute-start | bytes 786440 | tf_op jit(solution)/shard_map/ppermute | solution.py:33
  27.0 1.5 %copy-done.1 = bf16[128,7168]{1,0:T(8,128)(2,1)S(1)} copy-done((bf16[128,7168]{1,0:T(8,128)(2,1)S(1)}, bf16[128,7168]{1,0:T(8,128)(2,1)}, u32[]{:S(2)}) %copy-start.1) | copy-done | bytes 1835032
  28.5 9.2 %shard_map.93 = (f32[2,256,256]{2,1,0:T(8,128)S(1)}, f32[2,256,256]{2,1,0:T(8,128)S(1)}) custom-call(s32[4]{0:T(128)S(1)} %pad_add_fusion.3.index, bf16[2048,2048]{1,0:T(8,128)(2,1)} %refs_0_.9, bf16[2048,7168]{1,0:T(8,128)(2,1)} %refs_1_.9, bf16[128,2048]{1,0:T(8,128)(2,1)S(1)} %copy-done.4, bf16[128,7168]{1,0:T(8,128)(2,1)S(1)} %copy-done, ...), custom_call_target="tpu_custom_call" | custom-call | flops 2415919104 | bytes 18874368 | tf_op jit(solution)/shard_map/pallas_call | solution.py:116
  37.8 6.7 %collective-permute-done.1.refs_6_ = f32[256,256]{1,0:T(8,128)S(1)} collective-permute-done((f32[256,256]{1,0:T(8,128)S(1)}, f32[256,256]{1,0:T(8,128)S(1)}, u32[]{:S(2)}, u32[]{:S(2)}) %collective-permute-start.1) | collective-permute-done | bytes 262176 | tf_op jit(solution)/shard_map/ppermute | solution.py:33
  44.4 1.1 fusion.2
  45.8 9.6 %shard_map.94 = (f32[2,256,256]{2,1,0:T(8,128)}, f32[2,256,256]{2,1,0:T(8,128)S(1)}) custom-call(s32[4]{0:T(128)S(1)} %pad_add_fusion.2.index, bf16[2048,2048]{1,0:T(8,128)(2,1)} %refs_0_.9, bf16[2048,7168]{1,0:T(8,128)(2,1)} %refs_1_.9, bf16[128,2048]{1,0:T(8,128)(2,1)} %refs_2_.9, bf16[128,7168]{1,0:T(8,128)(2,1)} %refs_3_.9, bf16[2048,7168]{1,0:T(8,128)(2,1)} %refs_4_.9, ...), custom_call_target="tpu_custom_call" | custom-call | flops 2415919104 | bytes 18874368 | tf_op jit(solution)/shard_map/pallas_call | solution.py:116
  55.5 5.7 %collective-permute-done.3.refs_7_ = f32[256,256]{1,0:T(8,128)S(1)} collective-permute-done((f32[256,256]{1,0:T(8,128)S(1)}, f32[256,256]{1,0:T(8,128)S(1)}, u32[]{:S(2)}, u32[]{:S(2)}) %collective-permute-start.3) | collective-permute-done | bytes 262176 | tf_op jit(solution)/shard_map/ppermute | solution.py:33
  62.1 0.8 copy-done.14
  63.2 5.5 %shard_map.95.refs_0_ = f32[2,256,256]{2,1,0:T(8,128)S(1)} custom-call(s32[2]{0:T(128)S(1)} %pad_add_fusion.1.index, bf16[2048,2048]{1,0:T(8,128)(2,1)} %refs_0_.9, bf16[2048,7168]{1,0:T(8,128)(2,1)} %refs_1_.9, bf16[128,2048]{1,0:T(8,128)(2,1)} %refs_2_.9, bf16[128,7168]{1,0:T(8,128)(2,1)} %refs_3_.9, bf16[2048,7168]{1,0:T(8,128)(2,1)} %refs_4_.9, ...), custom_call_target="tpu_custom_call" | custom-call | flops 1207959552 | bytes 9437184 | tf_op jit(solution)/shard_map/pallas_call | solution.py:116
  68.7 4.0 %shard_map.96 = (bf16[128,8192]{1,0:T(8,128)(2,1)S(1)}, bf16[128,8192]{1,0:T(8,128)(2,1)S(1)}) custom-call(s32[1]{0:T(128)} %bitcast.16.place, f32[64,64,128]{2,1,0:T(8,128)} %bitcast.17.mine, f32[64,64,128]{2,1,0:T(8,128)} %collective-permute-done.6.other), custom_call_target="tpu_custom_call" | custom-call | flops 4194304 | bytes 8388608 | tf_op jit(solution)/shard_map/pallas_call | solution.py:202
  72.7 1.3 %copy-done.6 = bf16[128,8192]{1,0:T(8,128)(2,1)} copy-done((bf16[128,8192]{1,0:T(8,128)(2,1)}, bf16[128,8192]{1,0:T(8,128)(2,1)S(1)}, u32[]{:S(2)}) %copy-start.6) | copy-done | bytes 2097176
  74.1 1.4 %copy-done.8 = bf16[128,8192]{1,0:T(8,128)(2,1)} copy-done((bf16[128,8192]{1,0:T(8,128)(2,1)}, bf16[128,8192]{1,0:T(8,128)(2,1)S(1)}, u32[]{:S(2)}) %copy-start.8) | copy-done | bytes 2097176
  75.4 2.1 %collective-permute-done.7.refs_8_ = f32[256,256]{1,0:T(8,128)} collective-permute-done((f32[256,256]{1,0:T(8,128)}, f32[256,256]{1,0:T(8,128)}, u32[]{:S(2)}, u32[]{:S(2)}) %collective-permute-start.7) | collective-permute-done | bytes 262176 | tf_op jit(solution)/shard_map/ppermute | solution.py:33
  77.5 1.0 fusion
  78.6 1.6 %collective-permute-start.8 = (f32[256,256]{1,0:T(8,128)S(1)}, f32[256,256]{1,0:T(8,128)S(1)}, u32[]{:S(2)}, u32[]{:S(2)}) collective-permute-start(f32[256,256]{1,0:T(8,128)S(1)} %fusion), channel_id=1, source_target_pairs={{0,3},{3,0},{1,2},{2,1},{4,7},{7,4},{5,6},{6,5},{8,11},{11,8},{9,1... | collective-permute-start | bytes 786440 | tf_op jit(solution)/shard_map/ppermute | solution.py:33
  80.3 1.5 %shard_map.97 = (f32[3,32,128]{2,1,0:T(8,128)S(1)}, f32[3,32,128]{2,1,0:T(8,128)S(1)}, f32[3,32,128]{2,1,0:T(8,128)S(1)}, f32[3,32,128]{2,1,0:T(8,128)S(1)}) custom-call(s32[4]{0:T(128)S(1)} %pad_add_fusion.dest, f32[2,256,256]{2,1,0:T(8,128)S(1)} %copy-done.11, f32[2,256,256]{2,1,0:T(8,128)S(1)} %copy-done.13, f32[2,256,256]{2,1,0:T(8,128)S(1)} %copy-done.15, ...), custom_call_target="tpu_custom_call" | custom-call | flops 100663296 | bytes 1572864 | tf_op jit(solution)/shard_map/pallas_call | solution.py:162
  81.8 7.3 %collective-permute-done.8.refs_2_ = f32[256,256]{1,0:T(8,128)S(1)} collective-permute-done((f32[256,256]{1,0:T(8,128)S(1)}, f32[256,256]{1,0:T(8,128)S(1)}, u32[]{:S(2)}, u32[]{:S(2)}) %collective-permute-start.8) | collective-permute-done | bytes 262176 | tf_op jit(solution)/shard_map/ppermute | solution.py:33
  89.1 1.3 %shard_map.98 = (f32[4,32,128]{2,1,0:T(8,128)S(1)}, f32[4,32,128]{2,1,0:T(8,128)S(1)}, f32[4,32,128]{2,1,0:T(8,128)S(1)}, f32[4,32,128]{2,1,0:T(8,128)S(1)}) custom-call(s32[4]{0:T(128)S(1)} %pad_add_fusion.dest, f32[2,256,256]{2,1,0:T(8,128)S(1)} %shard_map.95.refs_0_, f32[2,256,256]{2,1,0:T(8,128)} %collective-permute-done.5.refs_1_, ...), custom_call_target="tpu_custom_call" | custom-call | flops 33554432 | bytes 524288 | tf_op jit(solution)/shard_map/pallas_call | solution.py:162
  90.5 2.1 %collective-permute-start.10 = (f32[4,32,128]{2,1,0:T(8,128)S(1)}, f32[4,32,128]{2,1,0:T(8,128)S(1)}, u32[]{:S(2)}, u32[]{:S(2)}) collective-permute-start(f32[4,32,128]{2,1,0:T(8,128)S(1)} %get-tuple-element.59), channel_id=1, source_target_pairs={{0,2},{2,0},{1,3},{3,1},{4,6},{6,4},{5,7},{7,5},{8,10},{10,8},{9,1... | collective-permute-start | bytes 196616 | tf_op jit(solution)/shard_map/ppermute | solution.py:33
  92.6 2.3 %collective-permute-start.11 = (f32[4,32,128]{2,1,0:T(8,128)S(1)}, f32[4,32,128]{2,1,0:T(8,128)S(1)}, u32[]{:S(2)}, u32[]{:S(2)}) collective-permute-start(f32[4,32,128]{2,1,0:T(8,128)S(1)} %get-tuple-element.60), channel_id=1, source_target_pairs={{0,3},{3,0},{1,2},{2,1},{4,7},{7,4},{5,6},{6,5},{8,11},{11,8},{9,1... | collective-permute-start | bytes 196616 | tf_op jit(solution)/shard_map/ppermute | solution.py:33
  94.9 4.0 %shard_map.99 = (bf16[128,8192]{1,0:T(8,128)(2,1)S(1)}, bf16[128,8192]{1,0:T(8,128)(2,1)S(1)}) custom-call(s32[1]{0:T(128)} %bitcast.16.place, f32[64,64,128]{2,1,0:T(8,128)} %collective-permute-done.12.mine, f32[64,64,128]{2,1,0:T(8,128)} %collective-permute-done.13.other), custom_call_target="tpu_custom_call" | custom-call | flops 4194304 | bytes 8388608 | tf_op jit(solution)/shard_map/pallas_call | solution.py:202
  99.0 2.8 %shard_map.100 = f32[8,256]{1,0:T(8,128)S(1)} custom-call(s32[1]{0:T(128)} %bitcast.chip, s32[4]{0:T(128)S(1)} %pad_add_fusion.dest, f32[4,32,128]{2,1,0:T(8,128)S(1)} %get-tuple-element.57.refs_0_, f32[4,32,128]{2,1,0:T(8,128)S(1)} %collective-permute-done.9.refs_1_, f32[4,32,128]{2,1,0:T(8,128)S(1)} %collective-permute-done.10.refs_2_, ...), custom_call_target="tpu_custom_call" | custom-call | flops 67108864 | bytes 8388608 | tf_op jit(solution)/shard_map/pallas_call | solution.py:249
  101.8 1.0 collective-permute-start.14
  102.8 2.7 %collective-permute-done.14 = f32[8,256]{1,0:T(8,128)S(1)} collective-permute-done((f32[8,256]{1,0:T(8,128)S(1)}, f32[8,256]{1,0:T(8,128)S(1)}, u32[]{:S(2)}, u32[]{:S(2)}) %collective-permute-start.14) | collective-permute-done | bytes 8224 | tf_op jit(solution)/shard_map/ppermute | solution.py:33
  105.5 1.4 %collective-permute-start.15 = (f32[8,256]{1,0:T(8,128)S(1)}, f32[8,256]{1,0:T(8,128)S(1)}, u32[]{:S(2)}, u32[]{:S(2)}) collective-permute-start(f32[8,256]{1,0:T(8,128)S(1)} %add.58), channel_id=1, source_target_pairs={{0,2},{2,0},{1,3},{3,1},{4,6},{6,4},{5,7},{7,5},{8,10},{10,8},{9,1... | collective-permute-start | bytes 24584 | tf_op jit(solution)/shard_map/ppermute | solution.py:33
  106.9 3.1 %collective-permute-done.15 = f32[8,256]{1,0:T(8,128)S(1)} collective-permute-done((f32[8,256]{1,0:T(8,128)S(1)}, f32[8,256]{1,0:T(8,128)S(1)}, u32[]{:S(2)}, u32[]{:S(2)}) %collective-permute-start.15) | collective-permute-done | bytes 8224 | tf_op jit(solution)/shard_map/ppermute | solution.py:33
  (61 shorter events, 3.1 us)
Async XLA Ops:
  0.1 11.4 %copy-start = (bf16[128,7168]{1,0:T(8,128)(2,1)S(1)}, bf16[128,7168]{1,0:T(8,128)(2,1)}, u32[]{:S(2)}) copy-start(bf16[128,7168]{1,0:T(8,128)(2,1)} %refs_3_.9) | copy-start | bytes 5505028
  0.1 11.4 %copy-start.4 = (bf16[128,2048]{1,0:T(8,128)(2,1)S(1)}, bf16[128,2048]{1,0:T(8,128)(2,1)}, u32[]{:S(2)}) copy-start(bf16[128,2048]{1,0:T(8,128)(2,1)} %refs_2_.9) | copy-start | bytes 1572868
  6.9 15.4 %collective-permute-start = (f32[2,256,256]{2,1,0:T(8,128)}, f32[2,256,256]{2,1,0:T(8,128)S(1)}, u32[]{:S(2)}, u32[]{:S(2)}) collective-permute-start(f32[2,256,256]{2,1,0:T(8,128)} %shard_map.91), channel_id=1, source_target_pairs={{0,1},{1,0},{2,3},{3,2},{4,5},{5,4},{6,7},{7,6},{8,9},{9,8},{10,11... | collective-permute-start | bytes 1572872 | tf_op jit(solution)/shard_map/ppermute | solution.py:33
  9.9 58.8 %collective-permute-start.6 = (f32[64,64,128]{2,1,0:T(8,128)}, f32[64,64,128]{2,1,0:T(8,128)}, u32[]{:S(2)}, u32[]{:S(2)}) collective-permute-start(f32[64,64,128]{2,1,0:T(8,128)} %bitcast.17.mine), channel_id=1, source_target_pairs={{0,4},{4,0},{8,12},{12,8},{1,5},{5,1},{9,13},{13,9},{2,6},{6,2},{1... | collective-permute-start | bytes 6291464 | tf_op jit(solution)/shard_map/ppermute | solution.py:33
  9.9 68.6 %collective-permute-start.12 = (f32[64,64,128]{2,1,0:T(8,128)}, f32[64,64,128]{2,1,0:T(8,128)}, u32[]{:S(2)}, u32[]{:S(2)}) collective-permute-start(f32[64,64,128]{2,1,0:T(8,128)} %bitcast.17.mine), channel_id=1, source_target_pairs={{0,8},{8,0},{4,12},{12,4},{1,9},{9,1},{5,13},{13,5},{2,10},{10,2},... | collective-permute-start | bytes 6291464 | tf_op jit(solution)/shard_map/ppermute | solution.py:33
  11.5 15.5 %copy-start.5 = (bf16[128,2048]{1,0:T(8,128)(2,1)S(1)}, bf16[128,2048]{1,0:T(8,128)(2,1)}, u32[]{:S(2)}) copy-start(bf16[128,2048]{1,0:T(8,128)(2,1)} %refs_7_.9) | copy-start | bytes 1572868
  21.8 22.6 %collective-permute-start.2 = (f32[2,256,256]{2,1,0:T(8,128)}, f32[2,256,256]{2,1,0:T(8,128)}, u32[]{:S(2)}, u32[]{:S(2)}) collective-permute-start(f32[2,256,256]{2,1,0:T(8,128)} %get-tuple-element.37), channel_id=1, source_target_pairs={{0,1},{1,0},{2,3},{3,2},{4,5},{5,4},{6,7},{7,6},{8,9},{9,8},{10,11... | collective-permute-start | bytes 1572872 | tf_op jit(solution)/shard_map/ppermute | solution.py:33
  23.2 21.2 %collective-permute-start.1 = (f32[256,256]{1,0:T(8,128)S(1)}, f32[256,256]{1,0:T(8,128)S(1)}, u32[]{:S(2)}, u32[]{:S(2)}) collective-permute-start(f32[256,256]{1,0:T(8,128)S(1)} %fusion.3), channel_id=1, source_target_pairs={{0,3},{3,0},{1,2},{2,1},{4,7},{7,4},{5,6},{6,5},{8,11},{11,8},{9,1... | collective-permute-start | bytes 786440 | tf_op jit(solution)/shard_map/ppermute | solution.py:33
  27.0 1.5 %copy-start.1 = (bf16[128,7168]{1,0:T(8,128)(2,1)S(1)}, bf16[128,7168]{1,0:T(8,128)(2,1)}, u32[]{:S(2)}) copy-start(bf16[128,7168]{1,0:T(8,128)(2,1)} %refs_6_.9) | copy-start | bytes 5505028
  28.5 17.3 %copy-start.2 = (bf16[128,7168]{1,0:T(8,128)(2,1)S(1)}, bf16[128,7168]{1,0:T(8,128)(2,1)}, u32[]{:S(2)}) copy-start(bf16[128,7168]{1,0:T(8,128)(2,1)} %refs_6_.9) | copy-start | bytes 5505028
  37.7 17.8 %copy-start.12 = (f32[2,256,256]{2,1,0:T(8,128)}, f32[2,256,256]{2,1,0:T(8,128)S(1)}, u32[]{:S(2)}) copy-start(f32[2,256,256]{2,1,0:T(8,128)S(1)} %get-tuple-element.42.refs_1_) | copy-start | bytes 1572868
  37.7 23.6 %collective-permute-start.4 = (f32[2,256,256]{2,1,0:T(8,128)S(1)}, f32[2,256,256]{2,1,0:T(8,128)S(1)}, u32[]{:S(2)}, u32[]{:S(2)}) collective-permute-start(f32[2,256,256]{2,1,0:T(8,128)S(1)} %get-tuple-element.41), channel_id=1, source_target_pairs={{0,1},{1,0},{2,3},{3,2},{4,5},{5,4},{6,7},{7,6},{8,9},{9,8},{10,11... | collective-permute-start | bytes 1572872 | tf_op jit(solution)/shard_map/ppermute | solution.py:33
  44.4 11.0 %copy-start.16 = (f32[256,256]{1,0:T(8,128)}, f32[256,256]{1,0:T(8,128)S(1)}, u32[]{:S(2)}) copy-start(f32[256,256]{1,0:T(8,128)S(1)} %collective-permute-done.1.refs_6_) | copy-start | bytes 786436
  45.5 17.6 %copy-start.3 = (bf16[128,7168]{1,0:T(8,128)(2,1)S(1)}, bf16[128,7168]{1,0:T(8,128)(2,1)}, u32[]{:S(2)}) copy-start(bf16[128,7168]{1,0:T(8,128)(2,1)} %refs_6_.9) | copy-start | bytes 5505028
  45.5 15.7 %collective-permute-start.3 = (f32[256,256]{1,0:T(8,128)S(1)}, f32[256,256]{1,0:T(8,128)S(1)}, u32[]{:S(2)}, u32[]{:S(2)}) collective-permute-start(f32[256,256]{1,0:T(8,128)S(1)} %fusion.2), channel_id=1, source_target_pairs={{0,3},{3,0},{1,2},{2,1},{4,7},{7,4},{5,6},{6,5},{8,11},{11,8},{9,1... | collective-permute-start | bytes 786440 | tf_op jit(solution)/shard_map/ppermute | solution.py:33
  55.5 22.1 %collective-permute-start.5 = (f32[2,256,256]{2,1,0:T(8,128)}, f32[2,256,256]{2,1,0:T(8,128)}, u32[]{:S(2)}, u32[]{:S(2)}) collective-permute-start(f32[2,256,256]{2,1,0:T(8,128)} %get-tuple-element.45), channel_id=1, source_target_pairs={{0,1},{1,0},{2,3},{3,2},{4,5},{5,4},{6,7},{7,6},{8,9},{9,8},{10,11... | collective-permute-start | bytes 1572872 | tf_op jit(solution)/shard_map/ppermute | solution.py:33
  62.9 14.7 %collective-permute-start.7 = (f32[256,256]{1,0:T(8,128)}, f32[256,256]{1,0:T(8,128)}, u32[]{:S(2)}, u32[]{:S(2)}) collective-permute-start(f32[256,256]{1,0:T(8,128)} %fusion.1), channel_id=1, source_target_pairs={{0,3},{3,0},{1,2},{2,1},{4,7},{7,4},{5,6},{6,5},{8,11},{11,8},{9,1... | collective-permute-start | bytes 786440 | tf_op jit(solution)/shard_map/ppermute | solution.py:33
  68.7 11.6 %copy-start.11 = (f32[2,256,256]{2,1,0:T(8,128)S(1)}, f32[2,256,256]{2,1,0:T(8,128)}, u32[]{:S(2)}) copy-start(f32[2,256,256]{2,1,0:T(8,128)} %copy-done.10) | copy-start | bytes 1572868
  68.7 11.6 %copy-start.13 = (f32[2,256,256]{2,1,0:T(8,128)S(1)}, f32[2,256,256]{2,1,0:T(8,128)}, u32[]{:S(2)}) copy-start(f32[2,256,256]{2,1,0:T(8,128)} %copy-done.12) | copy-start | bytes 1572868
  68.7 11.6 %copy-start.15 = (f32[2,256,256]{2,1,0:T(8,128)S(1)}, f32[2,256,256]{2,1,0:T(8,128)}, u32[]{:S(2)}) copy-start(f32[2,256,256]{2,1,0:T(8,128)} %copy-done.14) | copy-start | bytes 1572868
  68.7 11.6 %copy-start.17 = (f32[256,256]{1,0:T(8,128)S(1)}, f32[256,256]{1,0:T(8,128)}, u32[]{:S(2)}) copy-start(f32[256,256]{1,0:T(8,128)} %copy-done.16) | copy-start | bytes 786436
  68.7 11.6 %copy-start.19 = (f32[256,256]{1,0:T(8,128)S(1)}, f32[256,256]{1,0:T(8,128)}, u32[]{:S(2)}) copy-start(f32[256,256]{1,0:T(8,128)} %copy-done.18) | copy-start | bytes 786436
  74.1 1.4 %copy-start.8 = (bf16[128,8192]{1,0:T(8,128)(2,1)}, bf16[128,8192]{1,0:T(8,128)(2,1)S(1)}, u32[]{:S(2)}) copy-start(bf16[128,8192]{1,0:T(8,128)(2,1)S(1)} %get-tuple-element.61.refs_5_) | copy-start | bytes 6291460
  78.5 16.4 %collective-permute-start.13 = (f32[64,64,128]{2,1,0:T(8,128)}, f32[64,64,128]{2,1,0:T(8,128)}, u32[]{:S(2)}, u32[]{:S(2)}) collective-permute-start(f32[64,64,128]{2,1,0:T(8,128)} %collective-permute-done.12.mine), channel_id=1, source_target_pairs={{0,4},{4,0},{8,12},{12,8},{1,5},{5,1},{9,13},{13,9},{2,6},{6,2},{1... | collective-permute-start | bytes 6291464 | tf_op jit(solution)/shard_map/ppermute | solution.py:33
  78.6 10.5 %collective-permute-start.8 = (f32[256,256]{1,0:T(8,128)S(1)}, f32[256,256]{1,0:T(8,128)S(1)}, u32[]{:S(2)}, u32[]{:S(2)}) collective-permute-start(f32[256,256]{1,0:T(8,128)S(1)} %fusion), channel_id=1, source_target_pairs={{0,3},{3,0},{1,2},{2,1},{4,7},{7,4},{5,6},{6,5},{8,11},{11,8},{9,1... | collective-permute-start | bytes 786440 | tf_op jit(solution)/shard_map/ppermute | solution.py:33
  90.4 8.5 %collective-permute-start.9 = (f32[4,32,128]{2,1,0:T(8,128)S(1)}, f32[4,32,128]{2,1,0:T(8,128)S(1)}, u32[]{:S(2)}, u32[]{:S(2)}) collective-permute-start(f32[4,32,128]{2,1,0:T(8,128)S(1)} %get-tuple-element.58), channel_id=1, source_target_pairs={{0,1},{1,0},{2,3},{3,2},{4,5},{5,4},{6,7},{7,6},{8,9},{9,8},{10,11... | collective-permute-start | bytes 196616 | tf_op jit(solution)/shard_map/ppermute | solution.py:33
  90.5 8.4 %collective-permute-start.10 = (f32[4,32,128]{2,1,0:T(8,128)S(1)}, f32[4,32,128]{2,1,0:T(8,128)S(1)}, u32[]{:S(2)}, u32[]{:S(2)}) collective-permute-start(f32[4,32,128]{2,1,0:T(8,128)S(1)} %get-tuple-element.59), channel_id=1, source_target_pairs={{0,2},{2,0},{1,3},{3,1},{4,6},{6,4},{5,7},{7,5},{8,10},{10,8},{9,1... | collective-permute-start | bytes 196616 | tf_op jit(solution)/shard_map/ppermute | solution.py:33
  92.6 6.3 %collective-permute-start.11 = (f32[4,32,128]{2,1,0:T(8,128)S(1)}, f32[4,32,128]{2,1,0:T(8,128)S(1)}, u32[]{:S(2)}, u32[]{:S(2)}) collective-permute-start(f32[4,32,128]{2,1,0:T(8,128)S(1)} %get-tuple-element.60), channel_id=1, source_target_pairs={{0,3},{3,0},{1,2},{2,1},{4,7},{7,4},{5,6},{6,5},{8,11},{11,8},{9,1... | collective-permute-start | bytes 196616 | tf_op jit(solution)/shard_map/ppermute | solution.py:33
  94.9 4.0 %copy-start.7 = (bf16[128,8192]{1,0:T(8,128)(2,1)S(1)}, bf16[128,8192]{1,0:T(8,128)(2,1)}, u32[]{:S(2)}) copy-start(bf16[128,8192]{1,0:T(8,128)(2,1)} %copy-done.6) | copy-start | bytes 6291460
  94.9 4.1 %copy-start.9 = (bf16[128,8192]{1,0:T(8,128)(2,1)S(1)}, bf16[128,8192]{1,0:T(8,128)(2,1)}, u32[]{:S(2)}) copy-start(bf16[128,8192]{1,0:T(8,128)(2,1)} %copy-done.8) | copy-start | bytes 6291460
  101.8 3.7 %collective-permute-start.14 = (f32[8,256]{1,0:T(8,128)S(1)}, f32[8,256]{1,0:T(8,128)S(1)}, u32[]{:S(2)}, u32[]{:S(2)}) collective-permute-start(f32[8,256]{1,0:T(8,128)S(1)} %shard_map.100), channel_id=1, source_target_pairs={{0,1},{1,0},{2,3},{3,2},{4,5},{5,4},{6,7},{7,6},{8,9},{9,8},{10,11... | collective-permute-start | bytes 24584 | tf_op jit(solution)/shard_map/ppermute | solution.py:33
  105.5 4.5 %collective-permute-start.15 = (f32[8,256]{1,0:T(8,128)S(1)}, f32[8,256]{1,0:T(8,128)S(1)}, u32[]{:S(2)}, u32[]{:S(2)}) collective-permute-start(f32[8,256]{1,0:T(8,128)S(1)} %add.58), channel_id=1, source_target_pairs={{0,2},{2,0},{1,3},{3,1},{4,6},{6,4},{5,7},{7,5},{8,10},{10,8},{9,1... | collective-permute-start | bytes 24584 | tf_op jit(solution)/shard_map/ppermute | solution.py:33
  (4 other events, 3.7 us)

commit v5 on v4

--- a/solution.py
+++ b/solution.py
@@ -134,17 +134,14 @@
     )(index, *operands)
 
 
-def sketch_kernel(count, width, before, dest, *refs):
-    own, first, second, made, outs, full = (
+def sketch_kernel(count, width, dest, *refs):
+    own, first, second, outs, full = (
         refs[:count],
         refs[count : 2 * count],
         refs[2 * count : 3 * count],
-        refs[3 * count : -5],
         refs[-5:-1],
         refs[-1],
     )
-    for earlier, out in zip(made, outs):
-        out[:before] = earlier[...]
     for i in range(count):
         high, low = halves(own[i][0] + first[i][0] + second[i][...])
         a = jnp.concatenate([high[:K], low[:K]], 0)
@@ -152,24 +149,22 @@
         s = lax.dot_general(a, b, ROWS_BY_ROWS, preferred_element_type=jnp.float32)
         full[...] = s[:K, :K] + (s[:K, K:] + s[K:, :K] + s[K:, K:])
         for n, out in enumerate(outs):
-            out[before + i] = full[pl.ds(pl.multiple_of(dest[n] * width, 8), width), :]
-
-
-def sketches(dest, own, first, second, width, made=()):
+            out[i] = full[pl.ds(pl.multiple_of(dest[n] * width, 8), width), :]
+
+
+def sketches(dest, own, first, second, width):
     count = len(own)
-    before = made[0].shape[0] if made else 0
-    total = before + count
     return pl.pallas_call(
-        functools.partial(sketch_kernel, count, width, before),
-        in_specs=[SCALARS] + [WHOLE] * (3 * count + len(made)),
+        functools.partial(sketch_kernel, count, width),
+        in_specs=[SCALARS] + [WHOLE] * (3 * count),
         out_specs=[WHOLE] * 4,
-        out_shape=[pltpu.VMEM((total, width, K), jnp.float32)] * 4,
+        out_shape=[pltpu.VMEM((count, width, K), jnp.float32)] * 4,
         scratch_shapes=[pltpu.VMEM((K, K), jnp.float32)],
         compiler_params=pltpu.CompilerParams(vmem_limit_bytes=8 * 2**20),
         cost_estimate=pl.CostEstimate(
             flops=8 * count * LEN * K * K, bytes_accessed=count * 2**19, transcendentals=0
         ),
-    )(dest, *own, *first, *second, *made)
+    )(dest, *own, *first, *second)
 
 
 def split_kernel(place, mine, other, high, low, flat, sem):
@@ -216,47 +211,43 @@
 
 
 def score_kernel(chunks, pair, chip, dest, *refs):
-    cuts, parts, base, out, cat = refs[:4], refs[4:8], refs[8:-2], refs[-2], refs[-1]
-    width = cuts[0].shape[1]
+    sets = [refs[4 * n : 4 * n + 4] for n in range(len(chunks))]
+    parts, out, cat = refs[-6:-2], refs[-2], refs[-1]
+    width = sets[0][0].shape[1]
     count = 4 * pair
-    used = sorted({k // pair for k in chunks})
-    depth = width * K
-    cat[...] = jnp.zeros_like(cat)
-    for i, k in enumerate(chunks):
-        layer, j = divmod(k, pair)
-        rows = slice(used.index(layer) * width, (used.index(layer) + 1) * width)
-        for n, cut in enumerate(cuts):
-            high, low = halves(cut[i])
-            cat[dest[n] * pair + j, rows, :] = high.astype(jnp.float32)
-            cat[count + dest[n] * pair + j, rows, :] = low.astype(jnp.float32)
+    for few, cuts in zip(chunks, sets):
+        for i, k in enumerate(few):
+            layer, j = divmod(k, pair)
+            rows = slice(layer * width, (layer + 1) * width)
+            for n, cut in enumerate(cuts):
+                high, low = halves(cut[i])
+                cat[dest[n] * pair + j, rows, :] = high.astype(jnp.float32)
+                cat[count + dest[n] * pair + j, rows, :] = low.astype(jnp.float32)
     s = jnp.concatenate([cat[:, r, :] for r in range(cat.shape[1])], 1).astype(jnp.bfloat16)
-    lanes = slice(used[0] * depth, (used[-1] + 1) * depth)
     totals = []
     for high, low in (parts[:2], parts[2:]):
-        d = lax.dot_general(s, high[:, lanes], ROWS_BY_ROWS, preferred_element_type=jnp.float32)
-        d += lax.dot_general(s, low[:, lanes], ROWS_BY_ROWS, preferred_element_type=jnp.float32)
+        d = lax.dot_general(s, high[...], ROWS_BY_ROWS, preferred_element_type=jnp.float32)
+        d += lax.dot_general(s, low[...], ROWS_BY_ROWS, preferred_element_type=jnp.float32)
         totals.append((d[:count] + d[count:]) * (1.0 / (LEN**0.5 * K)))
     mine, other = totals
     first = chip[0] == 0
     total = jnp.concatenate([jnp.where(first, mine, other), jnp.where(first, other, mine)], 1)
-    out[...] = total + base[0][...] if base else total
-
-
-def score(chip, dest, cuts, parts, chunks, pair, base=None):
-    queries, _ = parts[0].shape
-    rows = len({k // pair for k in chunks}) * cuts[0].shape[1]
-    more = [] if base is None else [base]
+    out[...] = total
+
+
+def score(chip, dest, sets, parts, chunks, pair):
+    queries, depth = parts[0].shape
     return pl.pallas_call(
         functools.partial(score_kernel, chunks, pair),
-        in_specs=[SCALARS, SCALARS] + [WHOLE] * (8 + len(more)),
+        in_specs=[SCALARS, SCALARS] + [WHOLE] * (4 * len(sets) + 4),
         out_specs=WHOLE,
         out_shape=pltpu.VMEM((4 * pair, 2 * queries), jnp.float32),
-        scratch_shapes=[pltpu.VMEM((8 * pair, rows, K), jnp.float32)],
+        scratch_shapes=[pltpu.VMEM((8 * pair, depth // K, K), jnp.float32)],
         compiler_params=pltpu.CompilerParams(vmem_limit_bytes=8 * 2**20),
         cost_estimate=pl.CostEstimate(
-            flops=64 * queries * rows * K, bytes_accessed=8 * queries * rows * K, transcendentals=0
+            flops=64 * queries * depth, bytes_accessed=8 * queries * depth, transcendentals=0
         ),
-    )(chip, dest, *cuts, *parts, *more)
+    )(chip, dest, *[cut for cuts in sets for cut in cuts], *parts)
 
 
 def line(
@@ -314,17 +305,17 @@
         second.append(send(order, ACROSS))
     other_chip = lax.optimization_barrier((other_chip, order))[0]
     parts += split(core, other_chip, send(other_chip, by_core, "dp"))
-    few = list(range(chunks - 1))
-    made = sketches(
-        lax.optimization_barrier((dest, order))[0],
-        [stay[k] for k in few],
-        [first[k] for k in few],
-        [second[k] for k in few],
-        width,
-    )
-    own, near, skip, far = sketches(dest, stay[-1:], first[-1:], second[-1:], width, made=made)
-    cuts = [own, send(near, NEAR), send(skip, SKIP), send(far, ACROSS)]
-    partial = score(chip, dest, cuts, parts, list(range(chunks)), pair)
+    few, last = list(range(chunks - 1)), [chunks - 1]
+
+    def cuts_of(these, to):
+        own, near, skip, far = sketches(
+            to, [stay[k] for k in these], [first[k] for k in these], [second[k] for k in these], width
+        )
+        return [own, send(near, NEAR), send(skip, SKIP), send(far, ACROSS)]
+
+    early = cuts_of(few, lax.optimization_barrier((dest, order))[0])
+    late = cuts_of(last, dest)
+    partial = score(chip, dest, [early, late], parts, [few, last], pair)
     partial = partial + send(partial, NEAR)
     return partial + send(partial, SKIP)
 

time: 111 us -> 110 us (level)
  starting transfers between devices: 17.8 us -> 20.6 us
  waiting for transfers between devices: 27.7 us -> 25.4 us
    ppermute x16 -> x19, starting transfers between devices: 17.8 us -> 20.6 us  [send(): return lax.ppermute(x, axis, pairs)]
    ppermute x16 -> x19, waiting for transfers between devices: 27.7 us -> 25.4 us  [send(): return lax.ppermute(x, axis, pairs)]
    unnamed x40 -> x46, local copies, waits for them, and re-layouts: 5.87 us -> 5.9 us
  transfers between devices with their start and end apart: 16 -> 19, of which waited for: 6 -> 7; matrix products, arithmetic and copies ran while one was open for 4% -> 3% of each run, Pallas kernels for 40% -> 40%
where the time goes in v5:
time: 110 us
  Pallas kernels  53.7 us (49%)
  waiting for transfers between devices  25.4 us (23%)
  starting transfers between devices  20.6 us (19%)
  local copies, waits for them, and re-layouts  5.9 us (5%)
  other arithmetic  3.89 us (4%)
    pallas_call x5, Pallas kernels, project(): pl.pallas_call(functools.partial(project_kernel, jobs, load), in_specs=[S...  40.6 us
    ppermute x19, waiting for transfers between devices, send(): return lax.ppermute(x, axis, pairs)  25.4 us
    ppermute x19, starting transfers between devices, send(): return lax.ppermute(x, axis, pairs)  20.6 us
    pallas_call x2, Pallas kernels, split(): pl.pallas_call(split_kernel, in_specs=[SCALARS, OUTSIDE, OUTSIDE], out_sp...  7.97 us
    unnamed x46, local copies, waits for them, and re-layouts  5.9 us
    add x4, other arithmetic, across(): return stay[1] + first[1]  2.91 us
    pallas_call x1, Pallas kernels, score(): pl.pallas_call(functools.partial(score_kernel, chunks, pair), in_specs=[S...  2.83 us
    pallas_call x2, Pallas kernels, sketches(): pl.pallas_call(functools.partial(sketch_kernel, count, width), in_specs=[...  2.26 us
  transfers between devices with their start and end apart: 19, of which 7 were waited for; matrix products, arithmetic and copies ran while one was open for 3% of the time, Pallas kernels for 40%

profile of v5, /device:TPU:0, one launch (start us, length us, event | category | flops | bytes accessed | tf_op | source)
XLA Modules:
  0.0 109.8 jit_solution(11921855225917845493)
XLA Ops:
  0.1 6.8 %shard_map.91 = f32[2,256,256]{2,1,0:T(8,128)} custom-call(s32[2]{0:T(128)S(1)} %pad_add_fusion.4.index, bf16[2048,2048]{1,0:T(8,128)(2,1)} %refs_0_.9, bf16[2048,7168]{1,0:T(8,128)(2,1)} %refs_1_.9, bf16[128,2048]{1,0:T(8,128)(2,1)} %refs_2_.9, bf16[128,7168]{1,0:T(8,128)(2,1)} %refs_3_.9, bf16[2048,7168]{1,0:T(8,128)(2,1)} %refs_4_.9, ...), custom_call_target="tpu_custom_call" | custom-call | flops 1207959552 | bytes 9437184 | tf_op jit(solution)/shard_map/pallas_call | solution.py:116
  6.9 3.1 %collective-permute-start = (f32[2,256,256]{2,1,0:T(8,128)}, f32[2,256,256]{2,1,0:T(8,128)S(1)}, u32[]{:S(2)}, u32[]{:S(2)}) collective-permute-start(f32[2,256,256]{2,1,0:T(8,128)} %shard_map.91), channel_id=1, source_target_pairs={{0,1},{1,0},{2,3},{3,2},{4,5},{5,4},{6,7},{7,6},{8,9},{9,8},{10,11... | collective-permute-start | bytes 1572872 | tf_op jit(solution)/shard_map/ppermute | solution.py:33
  10.0 1.5 %collective-permute-start.15 = (f32[64,64,128]{2,1,0:T(8,128)}, f32[64,64,128]{2,1,0:T(8,128)}, u32[]{:S(2)}, u32[]{:S(2)}) collective-permute-start(f32[64,64,128]{2,1,0:T(8,128)} %bitcast.17.mine), channel_id=1, source_target_pairs={{0,8},{8,0},{4,12},{12,4},{1,9},{9,1},{5,13},{13,5},{2,10},{10,2},... | collective-permute-start | bytes 6291464 | tf_op jit(solution)/shard_map/ppermute | solution.py:33
  11.5 9.5 %shard_map.92 = (f32[2,256,256]{2,1,0:T(8,128)}, f32[2,256,256]{2,1,0:T(8,128)S(1)}) custom-call(s32[4]{0:T(128)S(1)} %pad_add_fusion.2.index, bf16[2048,2048]{1,0:T(8,128)(2,1)} %refs_0_.9, bf16[2048,7168]{1,0:T(8,128)(2,1)} %refs_1_.9, bf16[128,2048]{1,0:T(8,128)(2,1)S(1)} %copy-done.4, bf16[128,7168]{1,0:T(8,128)(2,1)S(1)} %copy-done, ...), custom_call_target="tpu_custom_call" | custom-call | flops 2415919104 | bytes 18874368 | tf_op jit(solution)/shard_map/pallas_call | solution.py:116
  21.1 0.8 copy-done.10
  22.3 1.0 fusion.3
  23.3 3.7 %collective-permute-start.1 = (f32[256,256]{1,0:T(8,128)S(1)}, f32[256,256]{1,0:T(8,128)S(1)}, u32[]{:S(2)}, u32[]{:S(2)}) collective-permute-start(f32[256,256]{1,0:T(8,128)S(1)} %fusion.3), channel_id=1, source_target_pairs={{0,3},{3,0},{1,2},{2,1},{4,7},{7,4},{5,6},{6,5},{8,11},{11,8},{9,1... | collective-permute-start | bytes 786440 | tf_op jit(solution)/shard_map/ppermute | solution.py:33
  27.0 1.5 %copy-done.1 = bf16[128,7168]{1,0:T(8,128)(2,1)S(1)} copy-done((bf16[128,7168]{1,0:T(8,128)(2,1)S(1)}, bf16[128,7168]{1,0:T(8,128)(2,1)}, u32[]{:S(2)}) %copy-start.1) | copy-done | bytes 1835032
  28.5 9.2 %shard_map.93 = (f32[2,256,256]{2,1,0:T(8,128)S(1)}, f32[2,256,256]{2,1,0:T(8,128)S(1)}) custom-call(s32[4]{0:T(128)S(1)} %pad_add_fusion.3.index, bf16[2048,2048]{1,0:T(8,128)(2,1)} %refs_0_.9, bf16[2048,7168]{1,0:T(8,128)(2,1)} %refs_1_.9, bf16[128,2048]{1,0:T(8,128)(2,1)S(1)} %copy-done.4, bf16[128,7168]{1,0:T(8,128)(2,1)S(1)} %copy-done, ...), custom_call_target="tpu_custom_call" | custom-call | flops 2415919104 | bytes 18874368 | tf_op jit(solution)/shard_map/pallas_call | solution.py:116
  37.8 6.7 %collective-permute-done.1.refs_6_ = f32[256,256]{1,0:T(8,128)S(1)} collective-permute-done((f32[256,256]{1,0:T(8,128)S(1)}, f32[256,256]{1,0:T(8,128)S(1)}, u32[]{:S(2)}, u32[]{:S(2)}) %collective-permute-start.1) | collective-permute-done | bytes 262176 | tf_op jit(solution)/shard_map/ppermute | solution.py:33
  44.5 1.1 fusion.2
  45.8 9.6 %shard_map.94 = (f32[2,256,256]{2,1,0:T(8,128)}, f32[2,256,256]{2,1,0:T(8,128)S(1)}) custom-call(s32[4]{0:T(128)S(1)} %pad_add_fusion.2.index, bf16[2048,2048]{1,0:T(8,128)(2,1)} %refs_0_.9, bf16[2048,7168]{1,0:T(8,128)(2,1)} %refs_1_.9, bf16[128,2048]{1,0:T(8,128)(2,1)} %refs_2_.9, bf16[128,7168]{1,0:T(8,128)(2,1)} %refs_3_.9, bf16[2048,7168]{1,0:T(8,128)(2,1)} %refs_4_.9, ...), custom_call_target="tpu_custom_call" | custom-call | flops 2415919104 | bytes 18874368 | tf_op jit(solution)/shard_map/pallas_call | solution.py:116
  55.6 5.7 %collective-permute-done.3.refs_7_ = f32[256,256]{1,0:T(8,128)S(1)} collective-permute-done((f32[256,256]{1,0:T(8,128)S(1)}, f32[256,256]{1,0:T(8,128)S(1)}, u32[]{:S(2)}, u32[]{:S(2)}) %collective-permute-start.3) | collective-permute-done | bytes 262176 | tf_op jit(solution)/shard_map/ppermute | solution.py:33
  61.3 0.8 fusion.1
  62.1 0.8 copy-done.14
  63.3 5.5 %shard_map.95.refs_0_ = f32[2,256,256]{2,1,0:T(8,128)S(1)} custom-call(s32[2]{0:T(128)S(1)} %pad_add_fusion.1.index, bf16[2048,2048]{1,0:T(8,128)(2,1)} %refs_0_.9, bf16[2048,7168]{1,0:T(8,128)(2,1)} %refs_1_.9, bf16[128,2048]{1,0:T(8,128)(2,1)} %refs_2_.9, bf16[128,7168]{1,0:T(8,128)(2,1)} %refs_3_.9, bf16[2048,7168]{1,0:T(8,128)(2,1)} %refs_4_.9, ...), custom_call_target="tpu_custom_call" | custom-call | flops 1207959552 | bytes 9437184 | tf_op jit(solution)/shard_map/pallas_call | solution.py:116
  68.9 4.0 %shard_map.96 = (bf16[128,8192]{1,0:T(8,128)(2,1)S(1)}, bf16[128,8192]{1,0:T(8,128)(2,1)S(1)}) custom-call(s32[1]{0:T(128)} %bitcast.16.place, f32[64,64,128]{2,1,0:T(8,128)} %bitcast.17.mine, f32[64,64,128]{2,1,0:T(8,128)} %collective-permute-done.5.other), custom_call_target="tpu_custom_call" | custom-call | flops 4194304 | bytes 8388608 | tf_op jit(solution)/shard_map/pallas_call | solution.py:197
  72.9 1.3 %copy-done.6 = bf16[128,8192]{1,0:T(8,128)(2,1)} copy-done((bf16[128,8192]{1,0:T(8,128)(2,1)}, bf16[128,8192]{1,0:T(8,128)(2,1)S(1)}, u32[]{:S(2)}) %copy-start.6) | copy-done | bytes 2097176
  74.2 1.4 %copy-done.8 = bf16[128,8192]{1,0:T(8,128)(2,1)} copy-done((bf16[128,8192]{1,0:T(8,128)(2,1)}, bf16[128,8192]{1,0:T(8,128)(2,1)S(1)}, u32[]{:S(2)}) %copy-start.8) | copy-done | bytes 2097176
  75.6 2.0 %collective-permute-done.6.refs_8_ = f32[256,256]{1,0:T(8,128)} collective-permute-done((f32[256,256]{1,0:T(8,128)}, f32[256,256]{1,0:T(8,128)}, u32[]{:S(2)}, u32[]{:S(2)}) %collective-permute-start.6) | collective-permute-done | bytes 262176 | tf_op jit(solution)/shard_map/ppermute | solution.py:33
  77.7 1.6 %collective-permute-start.11 = (f32[256,256]{1,0:T(8,128)S(1)}, f32[256,256]{1,0:T(8,128)S(1)}, u32[]{:S(2)}, u32[]{:S(2)}) collective-permute-start(f32[256,256]{1,0:T(8,128)S(1)} %fusion), channel_id=1, source_target_pairs={{0,3},{3,0},{1,2},{2,1},{4,7},{7,4},{5,6},{6,5},{8,11},{11,8},{9,1... | collective-permute-start | bytes 786440 | tf_op jit(solution)/shard_map/ppermute | solution.py:33
  79.5 1.5 %shard_map.97 = (f32[3,32,128]{2,1,0:T(8,128)S(1)}, f32[3,32,128]{2,1,0:T(8,128)S(1)}, f32[3,32,128]{2,1,0:T(8,128)S(1)}, f32[3,32,128]{2,1,0:T(8,128)S(1)}) custom-call(s32[4]{0:T(128)S(1)} %pad_add_fusion.dest, f32[2,256,256]{2,1,0:T(8,128)S(1)} %copy-done.11, f32[2,256,256]{2,1,0:T(8,128)S(1)} %copy-done.13, f32[2,256,256]{2,1,0:T(8,128)S(1)} %copy-done.17, ...), custom_call_target="tpu_custom_call" | custom-call | flops 100663296 | bytes 1572864 | tf_op jit(solution)/shard_map/pallas_call | solution.py:157
  81.0 2.8 %collective-permute-start.9 = (f32[3,32,128]{2,1,0:T(8,128)S(1)}, f32[3,32,128]{2,1,0:T(8,128)S(1)}, u32[]{:S(2)}, u32[]{:S(2)}) collective-permute-start(f32[3,32,128]{2,1,0:T(8,128)S(1)} %get-tuple-element.55), channel_id=1, source_target_pairs={{0,2},{2,0},{1,3},{3,1},{4,6},{6,4},{5,7},{7,5},{8,10},{10,8},{9,1... | collective-permute-start | bytes 147464 | tf_op jit(solution)/shard_map/ppermute | solution.py:33
  83.9 1.6 %collective-permute-start.10 = (f32[3,32,128]{2,1,0:T(8,128)S(1)}, f32[3,32,128]{2,1,0:T(8,128)S(1)}, u32[]{:S(2)}, u32[]{:S(2)}) collective-permute-start(f32[3,32,128]{2,1,0:T(8,128)S(1)} %get-tuple-element.56), channel_id=1, source_target_pairs={{0,3},{3,0},{1,2},{2,1},{4,7},{7,4},{5,6},{6,5},{8,11},{11,8},{9,1... | collective-permute-start | bytes 147464 | tf_op jit(solution)/shard_map/ppermute | solution.py:33
  85.4 3.4 %collective-permute-done.11.refs_2_ = f32[256,256]{1,0:T(8,128)S(1)} collective-permute-done((f32[256,256]{1,0:T(8,128)S(1)}, f32[256,256]{1,0:T(8,128)S(1)}, u32[]{:S(2)}, u32[]{:S(2)}) %collective-permute-start.11) | collective-permute-done | bytes 262176 | tf_op jit(solution)/shard_map/ppermute | solution.py:33
  88.8 0.8 shard_map.98
  90.2 1.6 %collective-permute-start.13 = (f32[1,32,128]{2,1,0:T(8,128)S(1)}, f32[1,32,128]{2,1,0:T(8,128)S(1)}, u32[]{:S(2)}, u32[]{:S(2)}) collective-permute-start(f32[1,32,128]{2,1,0:T(8,128)S(1)} %get-tuple-element.59), channel_id=1, source_target_pairs={{0,2},{2,0},{1,3},{3,1},{4,6},{6,4},{5,7},{7,5},{8,10},{10,8},{9,1... | collective-permute-start | bytes 49160 | tf_op jit(solution)/shard_map/ppermute | solution.py:33
  91.8 2.2 %collective-permute-start.14 = (f32[1,32,128]{2,1,0:T(8,128)S(1)}, f32[1,32,128]{2,1,0:T(8,128)S(1)}, u32[]{:S(2)}, u32[]{:S(2)}) collective-permute-start(f32[1,32,128]{2,1,0:T(8,128)S(1)} %get-tuple-element.60), channel_id=1, source_target_pairs={{0,3},{3,0},{1,2},{2,1},{4,7},{7,4},{5,6},{6,5},{8,11},{11,8},{9,1... | collective-permute-start | bytes 49160 | tf_op jit(solution)/shard_map/ppermute | solution.py:33
  94.1 4.0 %shard_map.99 = (bf16[128,8192]{1,0:T(8,128)(2,1)S(1)}, bf16[128,8192]{1,0:T(8,128)(2,1)S(1)}) custom-call(s32[1]{0:T(128)} %bitcast.16.place, f32[64,64,128]{2,1,0:T(8,128)} %collective-permute-done.15.mine, f32[64,64,128]{2,1,0:T(8,128)} %copy-done.22), custom_call_target="tpu_custom_call" | custom-call | flops 4194304 | bytes 8388608 | tf_op jit(solution)/shard_map/pallas_call | solution.py:197
  98.1 2.8 %shard_map.100 = f32[8,256]{1,0:T(8,128)S(1)} custom-call(s32[1]{0:T(128)} %bitcast.chip, s32[4]{0:T(128)S(1)} %pad_add_fusion.dest, f32[3,32,128]{2,1,0:T(8,128)S(1)} %get-tuple-element.53.refs_0_, f32[3,32,128]{2,1,0:T(8,128)S(1)} %collective-permute-done.8.refs_1_, f32[3,32,128]{2,1,0:T(8,128)S(1)} %collective-permute-done.9.refs_2_, ...), custom_call_target="tpu_custom_call" | custom-call | flops 67108864 | bytes 8388608 | tf_op jit(solution)/shard_map/pallas_call | solution.py:240
  101.2 3.5 %collective-permute-done.17 = f32[8,256]{1,0:T(8,128)S(1)} collective-permute-done((f32[8,256]{1,0:T(8,128)S(1)}, f32[8,256]{1,0:T(8,128)S(1)}, u32[]{:S(2)}, u32[]{:S(2)}) %collective-permute-start.17) | collective-permute-done | bytes 8224 | tf_op jit(solution)/shard_map/ppermute | solution.py:33
  105.1 4.0 %collective-permute-done.18 = f32[8,256]{1,0:T(8,128)S(1)} collective-permute-done((f32[8,256]{1,0:T(8,128)S(1)}, f32[8,256]{1,0:T(8,128)S(1)}, u32[]{:S(2)}, u32[]{:S(2)}) %collective-permute-start.18) | collective-permute-done | bytes 8224 | tf_op jit(solution)/shard_map/ppermute | solution.py:33
  (73 shorter events, 3.7 us)
Async XLA Ops:
  0.1 11.4 %copy-start = (bf16[128,7168]{1,0:T(8,128)(2,1)S(1)}, bf16[128,7168]{1,0:T(8,128)(2,1)}, u32[]{:S(2)}) copy-start(bf16[128,7168]{1,0:T(8,128)(2,1)} %refs_3_.9) | copy-start | bytes 5505028
  0.1 11.4 %copy-start.4 = (bf16[128,2048]{1,0:T(8,128)(2,1)S(1)}, bf16[128,2048]{1,0:T(8,128)(2,1)}, u32[]{:S(2)}) copy-start(bf16[128,2048]{1,0:T(8,128)(2,1)} %refs_2_.9) | copy-start | bytes 1572868
  6.9 15.4 %collective-permute-start = (f32[2,256,256]{2,1,0:T(8,128)}, f32[2,256,256]{2,1,0:T(8,128)S(1)}, u32[]{:S(2)}, u32[]{:S(2)}) collective-permute-start(f32[2,256,256]{2,1,0:T(8,128)} %shard_map.91), channel_id=1, source_target_pairs={{0,1},{1,0},{2,3},{3,2},{4,5},{5,4},{6,7},{7,6},{8,9},{9,8},{10,11... | collective-permute-start | bytes 1572872 | tf_op jit(solution)/shard_map/ppermute | solution.py:33
  10.0 58.9 %collective-permute-start.5 = (f32[64,64,128]{2,1,0:T(8,128)}, f32[64,64,128]{2,1,0:T(8,128)}, u32[]{:S(2)}, u32[]{:S(2)}) collective-permute-start(f32[64,64,128]{2,1,0:T(8,128)} %bitcast.17.mine), channel_id=1, source_target_pairs={{0,4},{4,0},{8,12},{12,8},{1,5},{5,1},{9,13},{13,9},{2,6},{6,2},{1... | collective-permute-start | bytes 6291464 | tf_op jit(solution)/shard_map/ppermute | solution.py:33
  10.0 67.7 %collective-permute-start.15 = (f32[64,64,128]{2,1,0:T(8,128)}, f32[64,64,128]{2,1,0:T(8,128)}, u32[]{:S(2)}, u32[]{:S(2)}) collective-permute-start(f32[64,64,128]{2,1,0:T(8,128)} %bitcast.17.mine), channel_id=1, source_target_pairs={{0,8},{8,0},{4,12},{12,4},{1,9},{9,1},{5,13},{13,5},{2,10},{10,2},... | collective-permute-start | bytes 6291464 | tf_op jit(solution)/shard_map/ppermute | solution.py:33
  11.5 15.5 %copy-start.5 = (bf16[128,2048]{1,0:T(8,128)(2,1)S(1)}, bf16[128,2048]{1,0:T(8,128)(2,1)}, u32[]{:S(2)}) copy-start(bf16[128,2048]{1,0:T(8,128)(2,1)} %refs_7_.9) | copy-start | bytes 1572868
  21.9 22.6 %collective-permute-start.2 = (f32[2,256,256]{2,1,0:T(8,128)}, f32[2,256,256]{2,1,0:T(8,128)}, u32[]{:S(2)}, u32[]{:S(2)}) collective-permute-start(f32[2,256,256]{2,1,0:T(8,128)} %get-tuple-element.37), channel_id=1, source_target_pairs={{0,1},{1,0},{2,3},{3,2},{4,5},{5,4},{6,7},{7,6},{8,9},{9,8},{10,11... | collective-permute-start | bytes 1572872 | tf_op jit(solution)/shard_map/ppermute | solution.py:33
  23.3 21.2 %collective-permute-start.1 = (f32[256,256]{1,0:T(8,128)S(1)}, f32[256,256]{1,0:T(8,128)S(1)}, u32[]{:S(2)}, u32[]{:S(2)}) collective-permute-start(f32[256,256]{1,0:T(8,128)S(1)} %fusion.3), channel_id=1, source_target_pairs={{0,3},{3,0},{1,2},{2,1},{4,7},{7,4},{5,6},{6,5},{8,11},{11,8},{9,1... | collective-permute-start | bytes 786440 | tf_op jit(solution)/shard_map/ppermute | solution.py:33
  28.5 17.3 %copy-start.2 = (bf16[128,7168]{1,0:T(8,128)(2,1)S(1)}, bf16[128,7168]{1,0:T(8,128)(2,1)}, u32[]{:S(2)}) copy-start(bf16[128,7168]{1,0:T(8,128)(2,1)} %refs_6_.9) | copy-start | bytes 5505028
  37.7 17.8 %copy-start.12 = (f32[2,256,256]{2,1,0:T(8,128)}, f32[2,256,256]{2,1,0:T(8,128)S(1)}, u32[]{:S(2)}) copy-start(f32[2,256,256]{2,1,0:T(8,128)S(1)} %get-tuple-element.42.refs_1_) | copy-start | bytes 1572868
  37.7 23.6 %collective-permute-start.4 = (f32[2,256,256]{2,1,0:T(8,128)S(1)}, f32[2,256,256]{2,1,0:T(8,128)S(1)}, u32[]{:S(2)}, u32[]{:S(2)}) collective-permute-start(f32[2,256,256]{2,1,0:T(8,128)S(1)} %get-tuple-element.41), channel_id=1, source_target_pairs={{0,1},{1,0},{2,3},{3,2},{4,5},{5,4},{6,7},{7,6},{8,9},{9,8},{10,11... | collective-permute-start | bytes 1572872 | tf_op jit(solution)/shard_map/ppermute | solution.py:33
  44.5 11.0 %copy-start.18 = (f32[256,256]{1,0:T(8,128)}, f32[256,256]{1,0:T(8,128)S(1)}, u32[]{:S(2)}) copy-start(f32[256,256]{1,0:T(8,128)S(1)} %collective-permute-done.1.refs_6_) | copy-start | bytes 786436
  45.5 17.7 %copy-start.3 = (bf16[128,7168]{1,0:T(8,128)(2,1)S(1)}, bf16[128,7168]{1,0:T(8,128)(2,1)}, u32[]{:S(2)}) copy-start(bf16[128,7168]{1,0:T(8,128)(2,1)} %refs_6_.9) | copy-start | bytes 5505028
  45.6 15.8 %collective-permute-start.3 = (f32[256,256]{1,0:T(8,128)S(1)}, f32[256,256]{1,0:T(8,128)S(1)}, u32[]{:S(2)}, u32[]{:S(2)}) collective-permute-start(f32[256,256]{1,0:T(8,128)S(1)} %fusion.2), channel_id=1, source_target_pairs={{0,3},{3,0},{1,2},{2,1},{4,7},{7,4},{5,6},{6,5},{8,11},{11,8},{9,1... | collective-permute-start | bytes 786440 | tf_op jit(solution)/shard_map/ppermute | solution.py:33
  55.5 22.1 %collective-permute-start.7 = (f32[2,256,256]{2,1,0:T(8,128)}, f32[2,256,256]{2,1,0:T(8,128)S(1)}, u32[]{:S(2)}, u32[]{:S(2)}) collective-permute-start(f32[2,256,256]{2,1,0:T(8,128)} %get-tuple-element.45), channel_id=1, source_target_pairs={{0,1},{1,0},{2,3},{3,2},{4,5},{5,4},{6,7},{7,6},{8,9},{9,8},{10,11... | collective-permute-start | bytes 1572872 | tf_op jit(solution)/shard_map/ppermute | solution.py:33
  63.0 14.6 %collective-permute-start.6 = (f32[256,256]{1,0:T(8,128)}, f32[256,256]{1,0:T(8,128)}, u32[]{:S(2)}, u32[]{:S(2)}) collective-permute-start(f32[256,256]{1,0:T(8,128)} %fusion.1), channel_id=1, source_target_pairs={{0,3},{3,0},{1,2},{2,1},{4,7},{7,4},{5,6},{6,5},{8,11},{11,8},{9,1... | collective-permute-start | bytes 786440 | tf_op jit(solution)/shard_map/ppermute | solution.py:33
  68.8 10.7 %copy-start.11 = (f32[2,256,256]{2,1,0:T(8,128)S(1)}, f32[2,256,256]{2,1,0:T(8,128)}, u32[]{:S(2)}) copy-start(f32[2,256,256]{2,1,0:T(8,128)} %copy-done.10) | copy-start | bytes 1572868
  68.8 10.6 %copy-start.13 = (f32[2,256,256]{2,1,0:T(8,128)S(1)}, f32[2,256,256]{2,1,0:T(8,128)}, u32[]{:S(2)}) copy-start(f32[2,256,256]{2,1,0:T(8,128)} %copy-done.12) | copy-start | bytes 1572868
  68.8 10.6 %copy-start.15 = (f32[2,256,256]{2,1,0:T(8,128)S(1)}, f32[2,256,256]{2,1,0:T(8,128)}, u32[]{:S(2)}) copy-start(f32[2,256,256]{2,1,0:T(8,128)} %copy-done.14) | copy-start | bytes 1572868
  68.8 10.6 %copy-start.17 = (f32[2,256,256]{2,1,0:T(8,128)S(1)}, f32[2,256,256]{2,1,0:T(8,128)}, u32[]{:S(2)}) copy-start(f32[2,256,256]{2,1,0:T(8,128)} %copy-done.16) | copy-start | bytes 1572868
  68.8 10.6 %copy-start.19 = (f32[256,256]{1,0:T(8,128)S(1)}, f32[256,256]{1,0:T(8,128)}, u32[]{:S(2)}) copy-start(f32[256,256]{1,0:T(8,128)} %copy-done.18) | copy-start | bytes 786436
  68.8 10.6 %copy-start.21 = (f32[256,256]{1,0:T(8,128)S(1)}, f32[256,256]{1,0:T(8,128)}, u32[]{:S(2)}) copy-start(f32[256,256]{1,0:T(8,128)} %copy-done.20) | copy-start | bytes 786436
  77.7 14.2 %collective-permute-start.16 = (f32[64,64,128]{2,1,0:T(8,128)}, f32[64,64,128]{2,1,0:T(8,128)S(1)}, u32[]{:S(2)}, u32[]{:S(2)}) collective-permute-start(f32[64,64,128]{2,1,0:T(8,128)} %collective-permute-done.15.mine), channel_id=1, source_target_pairs={{0,4},{4,0},{8,12},{12,8},{1,5},{5,1},{9,13},{13,9},{2,6},{6,2},{1... | collective-permute-start | bytes 6291464 | tf_op jit(solution)/shard_map/ppermute | solution.py:33
  77.7 11.1 %collective-permute-start.11 = (f32[256,256]{1,0:T(8,128)S(1)}, f32[256,256]{1,0:T(8,128)S(1)}, u32[]{:S(2)}, u32[]{:S(2)}) collective-permute-start(f32[256,256]{1,0:T(8,128)S(1)} %fusion), channel_id=1, source_target_pairs={{0,3},{3,0},{1,2},{2,1},{4,7},{7,4},{5,6},{6,5},{8,11},{11,8},{9,1... | collective-permute-start | bytes 786440 | tf_op jit(solution)/shard_map/ppermute | solution.py:33
  81.0 9.3 %collective-permute-start.8 = (f32[3,32,128]{2,1,0:T(8,128)S(1)}, f32[3,32,128]{2,1,0:T(8,128)S(1)}, u32[]{:S(2)}, u32[]{:S(2)}) collective-permute-start(f32[3,32,128]{2,1,0:T(8,128)S(1)} %get-tuple-element.54), channel_id=1, source_target_pairs={{0,1},{1,0},{2,3},{3,2},{4,5},{5,4},{6,7},{7,6},{8,9},{9,8},{10,11... | collective-permute-start | bytes 147464 | tf_op jit(solution)/shard_map/ppermute | solution.py:33
  81.0 17.0 %collective-permute-start.9 = (f32[3,32,128]{2,1,0:T(8,128)S(1)}, f32[3,32,128]{2,1,0:T(8,128)S(1)}, u32[]{:S(2)}, u32[]{:S(2)}) collective-permute-start(f32[3,32,128]{2,1,0:T(8,128)S(1)} %get-tuple-element.55), channel_id=1, source_target_pairs={{0,2},{2,0},{1,3},{3,1},{4,6},{6,4},{5,7},{7,5},{8,10},{10,8},{9,1... | collective-permute-start | bytes 147464 | tf_op jit(solution)/shard_map/ppermute | solution.py:33
  83.9 14.2 %collective-permute-start.10 = (f32[3,32,128]{2,1,0:T(8,128)S(1)}, f32[3,32,128]{2,1,0:T(8,128)S(1)}, u32[]{:S(2)}, u32[]{:S(2)}) collective-permute-start(f32[3,32,128]{2,1,0:T(8,128)S(1)} %get-tuple-element.56), channel_id=1, source_target_pairs={{0,3},{3,0},{1,2},{2,1},{4,7},{7,4},{5,6},{6,5},{8,11},{11,8},{9,1... | collective-permute-start | bytes 147464 | tf_op jit(solution)/shard_map/ppermute | solution.py:33
  89.6 8.5 %collective-permute-start.12 = (f32[1,32,128]{2,1,0:T(8,128)S(1)}, f32[1,32,128]{2,1,0:T(8,128)S(1)}, u32[]{:S(2)}, u32[]{:S(2)}) collective-permute-start(f32[1,32,128]{2,1,0:T(8,128)S(1)} %get-tuple-element.58), channel_id=1, source_target_pairs={{0,1},{1,0},{2,3},{3,2},{4,5},{5,4},{6,7},{7,6},{8,9},{9,8},{10,11... | collective-permute-start | bytes 49160 | tf_op jit(solution)/shard_map/ppermute | solution.py:33
  90.2 7.8 %collective-permute-start.13 = (f32[1,32,128]{2,1,0:T(8,128)S(1)}, f32[1,32,128]{2,1,0:T(8,128)S(1)}, u32[]{:S(2)}, u32[]{:S(2)}) collective-permute-start(f32[1,32,128]{2,1,0:T(8,128)S(1)} %get-tuple-element.59), channel_id=1, source_target_pairs={{0,2},{2,0},{1,3},{3,1},{4,6},{6,4},{5,7},{7,5},{8,10},{10,8},{9,1... | collective-permute-start | bytes 49160 | tf_op jit(solution)/shard_map/ppermute | solution.py:33
  91.8 6.2 %collective-permute-start.14 = (f32[1,32,128]{2,1,0:T(8,128)S(1)}, f32[1,32,128]{2,1,0:T(8,128)S(1)}, u32[]{:S(2)}, u32[]{:S(2)}) collective-permute-start(f32[1,32,128]{2,1,0:T(8,128)S(1)} %get-tuple-element.60), channel_id=1, source_target_pairs={{0,3},{3,0},{1,2},{2,1},{4,7},{7,4},{5,6},{6,5},{8,11},{11,8},{9,1... | collective-permute-start | bytes 49160 | tf_op jit(solution)/shard_map/ppermute | solution.py:33
  100.9 3.7 %collective-permute-start.17 = (f32[8,256]{1,0:T(8,128)S(1)}, f32[8,256]{1,0:T(8,128)S(1)}, u32[]{:S(2)}, u32[]{:S(2)}) collective-permute-start(f32[8,256]{1,0:T(8,128)S(1)} %shard_map.100), channel_id=1, source_target_pairs={{0,1},{1,0},{2,3},{3,2},{4,5},{5,4},{6,7},{7,6},{8,9},{9,8},{10,11... | collective-permute-start | bytes 24584 | tf_op jit(solution)/shard_map/ppermute | solution.py:33
  104.6 4.5 %collective-permute-start.18 = (f32[8,256]{1,0:T(8,128)S(1)}, f32[8,256]{1,0:T(8,128)S(1)}, u32[]{:S(2)}, u32[]{:S(2)}) collective-permute-start(f32[8,256]{1,0:T(8,128)S(1)} %add.58), channel_id=1, source_target_pairs={{0,2},{2,0},{1,3},{3,1},{4,6},{6,4},{5,7},{7,5},{8,10},{10,8},{9,1... | collective-permute-start | bytes 24584 | tf_op jit(solution)/shard_map/ppermute | solution.py:33
  (10 other events, 23.6 us)

commit v6 on v5

--- a/solution.py
+++ b/solution.py
@@ -167,20 +167,22 @@
     )(dest, *own, *first, *second)
 
 
-def split_kernel(place, mine, other, high, low, flat, sem):
-    count, rows, _ = mine.shape
+def split_kernel(core, *refs):
+    *blocks, high, low, flat, sem = refs
+    count, rows, _ = blocks[0].shape
     moves = [
         [
             pltpu.make_async_copy(x.at[:, r, :], flat.at[n, :, r * K : (r + 1) * K], sem.at[n, r])
             for r in range(rows)
         ]
-        for n, x in enumerate((mine, other))
+        for n, x in enumerate(blocks)
     ]
-    for move in moves[0] + moves[1]:
+    for move in sum(moves, []):
         move.start()
     step = 4
-    for n in range(2):
-        at = pl.ds(pl.multiple_of((place[0] ^ n) * count, 16), count)
+    for n in range(len(blocks)):
+        first = (core[0] ^ n) * count if len(blocks) > 1 else 0
+        at = pl.ds(pl.multiple_of(first, 16), count)
         for r in range(0, rows, step):
             for move in moves[n][r : r + step]:
                 move.wait()
@@ -190,29 +192,32 @@
             low[at, lanes] = l
 
 
-def split(core, mine, other, after=None):
-    count, rows, _ = mine.shape
+def split(core, blocks, after=None):
+    number = len(blocks)
+    count, rows, _ = blocks[0].shape
     if after is not None:
         core = lax.optimization_barrier((core, after))[0]
     return pl.pallas_call(
         split_kernel,
-        in_specs=[SCALARS, OUTSIDE, OUTSIDE],
+        in_specs=[SCALARS] + [OUTSIDE] * number,
         out_specs=[WHOLE] * 2,
-        out_shape=[pltpu.VMEM((2 * count, rows * K), jnp.bfloat16)] * 2,
+        out_shape=[pltpu.VMEM((number * count, rows * K), jnp.bfloat16)] * 2,
         scratch_shapes=[
-            pltpu.VMEM((2, count, rows * K), jnp.float32),
-            pltpu.SemaphoreType.DMA((2, rows)),
+            pltpu.VMEM((number, count, rows * K), jnp.float32),
+            pltpu.SemaphoreType.DMA((number, rows)),
         ],
         compiler_params=pltpu.CompilerParams(vmem_limit_bytes=8 * 2**20),
         cost_estimate=pl.CostEstimate(
-            flops=8 * count * rows * K, bytes_accessed=16 * count * rows * K, transcendentals=0
+            flops=4 * number * count * rows * K,
+            bytes_accessed=8 * number * count * rows * K,
+            transcendentals=0,
         ),
-    )(core, there(mine), there(other))
-
-
-def score_kernel(chunks, pair, chip, dest, *refs):
+    )(core, *[there(x) for x in blocks])
+
+
+def score_kernel(chunks, pair, dp, dest, *refs):
     sets = [refs[4 * n : 4 * n + 4] for n in range(len(chunks))]
-    parts, out, cat = refs[-6:-2], refs[-2], refs[-1]
+    parts, out, cat = refs[-8:-2], refs[-2], refs[-1]
     width = sets[0][0].shape[1]
     count = 4 * pair
     for few, cuts in zip(chunks, sets):
@@ -225,21 +230,23 @@
                 cat[count + dest[n] * pair + j, rows, :] = low.astype(jnp.float32)
     s = jnp.concatenate([cat[:, r, :] for r in range(cat.shape[1])], 1).astype(jnp.bfloat16)
     totals = []
-    for high, low in (parts[:2], parts[2:]):
+    for high, low in (parts[:2], parts[2:4], parts[4:]):
         d = lax.dot_general(s, high[...], ROWS_BY_ROWS, preferred_element_type=jnp.float32)
         d += lax.dot_general(s, low[...], ROWS_BY_ROWS, preferred_element_type=jnp.float32)
         totals.append((d[:count] + d[count:]) * (1.0 / (LEN**0.5 * K)))
-    mine, other = totals
-    first = chip[0] == 0
+    mine, same, mate = totals
+    second = dp[0] % 2 == 1
+    other = jnp.concatenate([jnp.where(second, mate, same), jnp.where(second, same, mate)], 1)
+    first = dp[0] < 2
     total = jnp.concatenate([jnp.where(first, mine, other), jnp.where(first, other, mine)], 1)
     out[...] = total
 
 
-def score(chip, dest, sets, parts, chunks, pair):
+def score(dp, dest, sets, parts, chunks, pair):
     queries, depth = parts[0].shape
     return pl.pallas_call(
         functools.partial(score_kernel, chunks, pair),
-        in_specs=[SCALARS, SCALARS] + [WHOLE] * (4 * len(sets) + 4),
+        in_specs=[SCALARS, SCALARS] + [WHOLE] * (4 * len(sets) + 6),
         out_specs=WHOLE,
         out_shape=pltpu.VMEM((4 * pair, 2 * queries), jnp.float32),
         scratch_shapes=[pltpu.VMEM((8 * pair, depth // K, K), jnp.float32)],
@@ -247,7 +254,7 @@
         cost_estimate=pl.CostEstimate(
             flops=64 * queries * depth, bytes_accessed=8 * queries * depth, transcendentals=0
         ),
-    )(chip, dest, *[cut for cuts in sets for cut in cuts], *parts)
+    )(dp, dest, *[cut for cuts in sets for cut in cuts], *parts)
 
 
 def line(
@@ -282,7 +289,6 @@
         return stay[1] + first[1]
 
     chunks = 2 * pair
-    chip = (dp >> 1).reshape(1)
     dest = jnp.stack([z, z ^ 1, z ^ 2, 3 - z])
     stay, first, second = [], [], []
     (out,) = project(layers, [leaving(0)], load=True)
@@ -298,13 +304,13 @@
             order = (out,)
         else:
             (kept,) = project(layers, [staying(k)], after=order)
-            parts = split(core, queries, other_core, after=kept)
+            parts = split(core, [queries, other_core], after=kept)
             order = (parts[0],)
         stay.append(kept)
         order = across(kept, first[k], order + tuple(second[-1:]))
         second.append(send(order, ACROSS))
     other_chip = lax.optimization_barrier((other_chip, order))[0]
-    parts += split(core, other_chip, send(other_chip, by_core, "dp"))
+    other_both = send(other_chip, by_core, "dp")
     few, last = list(range(chunks - 1)), [chunks - 1]
 
     def cuts_of(these, to):
@@ -314,8 +320,10 @@
         return [own, send(near, NEAR), send(skip, SKIP), send(far, ACROSS)]
 
     early = cuts_of(few, lax.optimization_barrier((dest, order))[0])
-    late = cuts_of(last, dest)
-    partial = score(chip, dest, [early, late], parts, [few, last], pair)
+    parts += split(core, [other_chip], after=early[0])
+    late = cuts_of(last, lax.optimization_barrier((dest, parts[2]))[0])
+    parts += split(core, [other_both])
+    partial = score(dp.reshape(1), dest, [early, late], parts, [few, last], pair)
     partial = partial + send(partial, NEAR)
     return partial + send(partial, SKIP)
 

time: 110 us -> 110 us (level)
  local copies, waits for them, and re-layouts: 5.9 us -> 3.18 us
  waiting for transfers between devices: 25.4 us -> 27.3 us
    unnamed x46 -> x38, local copies, waits for them, and re-layouts: 5.9 us -> 3.18 us
    ppermute x19, waiting for transfers between devices: 25.4 us -> 27.3 us  [send(): return lax.ppermute(x, axis, pairs)]
    pallas_call x2 -> x3, Pallas kernels: 7.97 us -> 8.7 us  [split(): pl.pallas_call(split_kernel, in_specs=[SCALARS] + [OUTSIDE] * number, out...]
  transfers between devices with their start and end apart: 19 -> 19, of which waited for: 7 -> 7; matrix products, arithmetic and copies ran while one was open for 3% -> 3% of each run, Pallas kernels for 40% -> 41%
where the time goes in v6:
time: 110 us; the launch traced here: 109 us
  Pallas kernels  54.4 us (49%)
  waiting for transfers between devices  27.3 us (25%)
  starting transfers between devices  19.7 us (18%)
  other arithmetic  3.93 us (4%)
  local copies, waits for them, and re-layouts  3.18 us (3%)
    pallas_call x5, Pallas kernels, project(): pl.pallas_call(functools.partial(project_kernel, jobs, load), in_specs=[S...  40.5 us
    ppermute x19, waiting for transfers between devices, send(): return lax.ppermute(x, axis, pairs)  27.3 us
    ppermute x19, starting transfers between devices, send(): return lax.ppermute(x, axis, pairs)  19.7 us
    pallas_call x3, Pallas kernels, split(): pl.pallas_call(split_kernel, in_specs=[SCALARS] + [OUTSIDE] * number, out...  8.7 us
    unnamed x38, local copies, waits for them, and re-layouts  3.18 us
    add x4, other arithmetic, across(): return stay[1] + first[1]  2.94 us
    pallas_call x1, Pallas kernels, score(): pl.pallas_call(functools.partial(score_kernel, chunks, pair), in_specs=[S...  2.94 us
    pallas_call x2, Pallas kernels, sketches(): pl.pallas_call(functools.partial(sketch_kernel, count, width), in_specs=[...  2.27 us
  transfers between devices with their start and end apart: 19, of which 7 were waited for; matrix products, arithmetic and copies ran while one was open for 3% of the time, Pallas kernels for 41%

profile of v6, /device:TPU:0, one launch (start us, length us, event | category | flops | bytes accessed | tf_op | source)
XLA Modules:
  0.0 108.9 jit_solution(14667017105808277715)
XLA Ops:
  0.1 6.8 %shard_map.91 = f32[2,256,256]{2,1,0:T(8,128)} custom-call(s32[2]{0:T(128)S(1)} %pad_add_fusion.4.index, bf16[2048,2048]{1,0:T(8,128)(2,1)} %refs_0_.9, bf16[2048,7168]{1,0:T(8,128)(2,1)} %refs_1_.9, bf16[128,2048]{1,0:T(8,128)(2,1)} %refs_2_.9, bf16[128,7168]{1,0:T(8,128)(2,1)} %refs_3_.9, bf16[2048,7168]{1,0:T(8,128)(2,1)} %refs_4_.9, ...), custom_call_target="tpu_custom_call" | custom-call | flops 1207959552 | bytes 9437184 | tf_op jit(solution)/shard_map/pallas_call | solution.py:116
  6.9 3.1 %collective-permute-start = (f32[2,256,256]{2,1,0:T(8,128)}, f32[2,256,256]{2,1,0:T(8,128)S(1)}, u32[]{:S(2)}, u32[]{:S(2)}) collective-permute-start(f32[2,256,256]{2,1,0:T(8,128)} %shard_map.91), channel_id=1, source_target_pairs={{0,1},{1,0},{2,3},{3,2},{4,5},{5,4},{6,7},{7,6},{8,9},{9,8},{10,11... | collective-permute-start | bytes 1572872 | tf_op jit(solution)/shard_map/ppermute | solution.py:33
  10.0 1.5 %collective-permute-start.11 = (f32[64,64,128]{2,1,0:T(8,128)}, f32[64,64,128]{2,1,0:T(8,128)}, u32[]{:S(2)}, u32[]{:S(2)}) collective-permute-start(f32[64,64,128]{2,1,0:T(8,128)} %bitcast.17.refs_0_), channel_id=1, source_target_pairs={{0,8},{8,0},{4,12},{12,4},{1,9},{9,1},{5,13},{13,5},{2,10},{10,2},... | collective-permute-start | bytes 6291464 | tf_op jit(solution)/shard_map/ppermute | solution.py:33
  11.5 9.5 %shard_map.92 = (f32[2,256,256]{2,1,0:T(8,128)}, f32[2,256,256]{2,1,0:T(8,128)S(1)}) custom-call(s32[4]{0:T(128)S(1)} %pad_add_fusion.2.index, bf16[2048,2048]{1,0:T(8,128)(2,1)} %refs_0_.9, bf16[2048,7168]{1,0:T(8,128)(2,1)} %refs_1_.9, bf16[128,2048]{1,0:T(8,128)(2,1)S(1)} %copy-done.4, bf16[128,7168]{1,0:T(8,128)(2,1)S(1)} %copy-done, ...), custom_call_target="tpu_custom_call" | custom-call | flops 2415919104 | bytes 18874368 | tf_op jit(solution)/shard_map/pallas_call | solution.py:116
  21.0 0.8 copy-done.6
  22.3 1.0 fusion.3
  23.3 3.7 %collective-permute-start.1 = (f32[256,256]{1,0:T(8,128)S(1)}, f32[256,256]{1,0:T(8,128)S(1)}, u32[]{:S(2)}, u32[]{:S(2)}) collective-permute-start(f32[256,256]{1,0:T(8,128)S(1)} %fusion.3), channel_id=1, source_target_pairs={{0,3},{3,0},{1,2},{2,1},{4,7},{7,4},{5,6},{6,5},{8,11},{11,8},{9,1... | collective-permute-start | bytes 786440 | tf_op jit(solution)/shard_map/ppermute | solution.py:33
  27.0 1.5 %copy-done.1 = bf16[128,7168]{1,0:T(8,128)(2,1)S(1)} copy-done((bf16[128,7168]{1,0:T(8,128)(2,1)S(1)}, bf16[128,7168]{1,0:T(8,128)(2,1)}, u32[]{:S(2)}) %copy-start.1) | copy-done | bytes 1835032
  28.5 9.2 %shard_map.93 = (f32[2,256,256]{2,1,0:T(8,128)S(1)}, f32[2,256,256]{2,1,0:T(8,128)S(1)}) custom-call(s32[4]{0:T(128)S(1)} %pad_add_fusion.3.index, bf16[2048,2048]{1,0:T(8,128)(2,1)} %refs_0_.9, bf16[2048,7168]{1,0:T(8,128)(2,1)} %refs_1_.9, bf16[128,2048]{1,0:T(8,128)(2,1)S(1)} %copy-done.4, bf16[128,7168]{1,0:T(8,128)(2,1)S(1)} %copy-done, ...), custom_call_target="tpu_custom_call" | custom-call | flops 2415919104 | bytes 18874368 | tf_op jit(solution)/shard_map/pallas_call | solution.py:116
  37.8 6.7 %collective-permute-done.1.refs_6_ = f32[256,256]{1,0:T(8,128)S(1)} collective-permute-done((f32[256,256]{1,0:T(8,128)S(1)}, f32[256,256]{1,0:T(8,128)S(1)}, u32[]{:S(2)}, u32[]{:S(2)}) %collective-permute-start.1) | collective-permute-done | bytes 262176 | tf_op jit(solution)/shard_map/ppermute | solution.py:33
  44.5 1.1 fusion.2
  45.8 9.6 %shard_map.94 = (f32[2,256,256]{2,1,0:T(8,128)}, f32[2,256,256]{2,1,0:T(8,128)S(1)}) custom-call(s32[4]{0:T(128)S(1)} %pad_add_fusion.2.index, bf16[2048,2048]{1,0:T(8,128)(2,1)} %refs_0_.9, bf16[2048,7168]{1,0:T(8,128)(2,1)} %refs_1_.9, bf16[128,2048]{1,0:T(8,128)(2,1)} %refs_2_.9, bf16[128,7168]{1,0:T(8,128)(2,1)} %refs_3_.9, bf16[2048,7168]{1,0:T(8,128)(2,1)} %refs_4_.9, ...), custom_call_target="tpu_custom_call" | custom-call | flops 2415919104 | bytes 18874368 | tf_op jit(solution)/shard_map/pallas_call | solution.py:116
  55.6 5.7 %collective-permute-done.3.refs_7_ = f32[256,256]{1,0:T(8,128)S(1)} collective-permute-done((f32[256,256]{1,0:T(8,128)S(1)}, f32[256,256]{1,0:T(8,128)S(1)}, u32[]{:S(2)}, u32[]{:S(2)}) %collective-permute-start.3) | collective-permute-done | bytes 262176 | tf_op jit(solution)/shard_map/ppermute | solution.py:33
  61.3 0.8 fusion.1
  62.2 0.8 copy-done.10
  63.3 5.5 %shard_map.95.refs_0_ = f32[2,256,256]{2,1,0:T(8,128)S(1)} custom-call(s32[2]{0:T(128)S(1)} %pad_add_fusion.1.index, bf16[2048,2048]{1,0:T(8,128)(2,1)} %refs_0_.9, bf16[2048,7168]{1,0:T(8,128)(2,1)} %refs_1_.9, bf16[128,2048]{1,0:T(8,128)(2,1)} %refs_2_.9, bf16[128,7168]{1,0:T(8,128)(2,1)} %refs_3_.9, bf16[2048,7168]{1,0:T(8,128)(2,1)} %refs_4_.9, ...), custom_call_target="tpu_custom_call" | custom-call | flops 1207959552 | bytes 9437184 | tf_op jit(solution)/shard_map/pallas_call | solution.py:116
  68.8 4.0 %shard_map.96 = (bf16[128,8192]{1,0:T(8,128)(2,1)S(1)}, bf16[128,8192]{1,0:T(8,128)(2,1)S(1)}) custom-call(s32[1]{0:T(128)} %bitcast.16.core, f32[64,64,128]{2,1,0:T(8,128)} %bitcast.17.refs_0_, f32[64,64,128]{2,1,0:T(8,128)} %collective-permute-done.5.refs_1_), custom_call_target="tpu_custom_call" | custom-call | flops 4194304 | bytes 8388608 | tf_op jit(solution)/shard_map/pallas_call | solution.py:200
  72.8 4.8 %collective-permute-done.6.refs_8_ = f32[256,256]{1,0:T(8,128)} collective-permute-done((f32[256,256]{1,0:T(8,128)}, f32[256,256]{1,0:T(8,128)}, u32[]{:S(2)}, u32[]{:S(2)}) %collective-permute-start.6) | collective-permute-done | bytes 262176 | tf_op jit(solution)/shard_map/ppermute | solution.py:33
  78.2 1.5 %shard_map.97 = (f32[3,32,128]{2,1,0:T(8,128)S(1)}, f32[3,32,128]{2,1,0:T(8,128)S(1)}, f32[3,32,128]{2,1,0:T(8,128)S(1)}, f32[3,32,128]{2,1,0:T(8,128)S(1)}) custom-call(s32[4]{0:T(128)S(1)} %pad_add_fusion.dest, f32[2,256,256]{2,1,0:T(8,128)S(1)} %copy-done.7, f32[2,256,256]{2,1,0:T(8,128)S(1)} %copy-done.9, f32[2,256,256]{2,1,0:T(8,128)S(1)} %copy-done.13, ...), custom_call_target="tpu_custom_call" | custom-call | flops 100663296 | bytes 1572864 | tf_op jit(solution)/shard_map/pallas_call | solution.py:157
  79.8 4.1 %collective-permute-start.9 = (f32[3,32,128]{2,1,0:T(8,128)S(1)}, f32[3,32,128]{2,1,0:T(8,128)S(1)}, u32[]{:S(2)}, u32[]{:S(2)}) collective-permute-start(f32[3,32,128]{2,1,0:T(8,128)S(1)} %get-tuple-element.59), channel_id=1, source_target_pairs={{0,2},{2,0},{1,3},{3,1},{4,6},{6,4},{5,7},{7,5},{8,10},{10,8},{9,1... | collective-permute-start | bytes 147464 | tf_op jit(solution)/shard_map/ppermute | solution.py:33
  84.2 2.4 %shard_map.98 = (bf16[64,8192]{1,0:T(8,128)(2,1)S(1)}, bf16[64,8192]{1,0:T(8,128)(2,1)S(1)}) custom-call(s32[1]{0:T(128)} %bitcast.16.core, f32[64,64,128]{2,1,0:T(8,128)} %collective-permute-done.11.refs_0_), custom_call_target="tpu_custom_call" | custom-call | flops 2097152 | bytes 4194304 | tf_op jit(solution)/shard_map/pallas_call | solution.py:200
  86.5 2.3 %collective-permute-done.12.refs_2_ = f32[256,256]{1,0:T(8,128)S(1)} collective-permute-done((f32[256,256]{1,0:T(8,128)S(1)}, f32[256,256]{1,0:T(8,128)S(1)}, u32[]{:S(2)}, u32[]{:S(2)}) %collective-permute-start.12) | collective-permute-done | bytes 262176 | tf_op jit(solution)/shard_map/ppermute | solution.py:33
  88.9 0.8 shard_map.99
  90.1 1.5 %collective-permute-start.14 = (f32[1,32,128]{2,1,0:T(8,128)S(1)}, f32[1,32,128]{2,1,0:T(8,128)S(1)}, u32[]{:S(2)}, u32[]{:S(2)}) collective-permute-start(f32[1,32,128]{2,1,0:T(8,128)S(1)} %get-tuple-element.67), channel_id=1, source_target_pairs={{0,2},{2,0},{1,3},{3,1},{4,6},{6,4},{5,7},{7,5},{8,10},{10,8},{9,1... | collective-permute-start | bytes 49160 | tf_op jit(solution)/shard_map/ppermute | solution.py:33
  91.6 2.5 %collective-permute-start.15 = (f32[1,32,128]{2,1,0:T(8,128)S(1)}, f32[1,32,128]{2,1,0:T(8,128)S(1)}, u32[]{:S(2)}, u32[]{:S(2)}) collective-permute-start(f32[1,32,128]{2,1,0:T(8,128)S(1)} %get-tuple-element.68), channel_id=1, source_target_pairs={{0,3},{3,0},{1,2},{2,1},{4,7},{7,4},{5,6},{6,5},{8,11},{11,8},{9,1... | collective-permute-start | bytes 49160 | tf_op jit(solution)/shard_map/ppermute | solution.py:33
  94.1 2.4 %shard_map.100 = (bf16[64,8192]{1,0:T(8,128)(2,1)S(1)}, bf16[64,8192]{1,0:T(8,128)(2,1)S(1)}) custom-call(s32[1]{0:T(128)} %bitcast.16.core, f32[64,64,128]{2,1,0:T(8,128)} %copy-done.18), custom_call_target="tpu_custom_call" | custom-call | flops 2097152 | bytes 4194304 | tf_op jit(solution)/shard_map/pallas_call | solution.py:200
  96.5 0.6 collective-permute-done.15.refs_7_
  97.1 2.9 %shard_map.101 = f32[8,256]{1,0:T(8,128)S(1)} custom-call(s32[1]{0:T(128)} %bitcast.dp, s32[4]{0:T(128)S(1)} %pad_add_fusion.dest, f32[3,32,128]{2,1,0:T(8,128)S(1)} %get-tuple-element.57.refs_0_, f32[3,32,128]{2,1,0:T(8,128)S(1)} %collective-permute-done.8.refs_1_, f32[3,32,128]{2,1,0:T(8,128)S(1)} %collective-permute-done.9.refs_2_, ...), custom_call_target="tpu_custom_call" | custom-call | flops 67108864 | bytes 8388608 | tf_op jit(solution)/shard_map/pallas_call | solution.py:247
  100.0 3.7 %collective-permute-done.17 = f32[8,256]{1,0:T(8,128)S(1)} collective-permute-done((f32[8,256]{1,0:T(8,128)S(1)}, f32[8,256]{1,0:T(8,128)S(1)}, u32[]{:S(2)}, u32[]{:S(2)}) %collective-permute-start.17) | collective-permute-done | bytes 8224 | tf_op jit(solution)/shard_map/ppermute | solution.py:33
  103.7 1.1 collective-permute-start.18
  104.8 3.5 %collective-permute-done.18 = f32[8,256]{1,0:T(8,128)S(1)} collective-permute-done((f32[8,256]{1,0:T(8,128)S(1)}, f32[8,256]{1,0:T(8,128)S(1)}, u32[]{:S(2)}, u32[]{:S(2)}) %collective-permute-start.18) | collective-permute-done | bytes 8224 | tf_op jit(solution)/shard_map/ppermute | solution.py:33
  108.3 0.6 add.59
  (66 shorter events, 2.8 us)
Async XLA Ops:
  0.1 11.4 %copy-start = (bf16[128,7168]{1,0:T(8,128)(2,1)S(1)}, bf16[128,7168]{1,0:T(8,128)(2,1)}, u32[]{:S(2)}) copy-start(bf16[128,7168]{1,0:T(8,128)(2,1)} %refs_3_.9) | copy-start | bytes 5505028
  0.1 11.4 %copy-start.4 = (bf16[128,2048]{1,0:T(8,128)(2,1)S(1)}, bf16[128,2048]{1,0:T(8,128)(2,1)}, u32[]{:S(2)}) copy-start(bf16[128,2048]{1,0:T(8,128)(2,1)} %refs_2_.9) | copy-start | bytes 1572868
  6.9 15.4 %collective-permute-start = (f32[2,256,256]{2,1,0:T(8,128)}, f32[2,256,256]{2,1,0:T(8,128)S(1)}, u32[]{:S(2)}, u32[]{:S(2)}) collective-permute-start(f32[2,256,256]{2,1,0:T(8,128)} %shard_map.91), channel_id=1, source_target_pairs={{0,1},{1,0},{2,3},{3,2},{4,5},{5,4},{6,7},{7,6},{8,9},{9,8},{10,11... | collective-permute-start | bytes 1572872 | tf_op jit(solution)/shard_map/ppermute | solution.py:33
  9.9 58.9 %collective-permute-start.5 = (f32[64,64,128]{2,1,0:T(8,128)}, f32[64,64,128]{2,1,0:T(8,128)}, u32[]{:S(2)}, u32[]{:S(2)}) collective-permute-start(f32[64,64,128]{2,1,0:T(8,128)} %bitcast.17.refs_0_), channel_id=1, source_target_pairs={{0,4},{4,0},{8,12},{12,8},{1,5},{5,1},{9,13},{13,9},{2,6},{6,2},{1... | collective-permute-start | bytes 6291464 | tf_op jit(solution)/shard_map/ppermute | solution.py:33
  10.0 67.8 %collective-permute-start.11 = (f32[64,64,128]{2,1,0:T(8,128)}, f32[64,64,128]{2,1,0:T(8,128)}, u32[]{:S(2)}, u32[]{:S(2)}) collective-permute-start(f32[64,64,128]{2,1,0:T(8,128)} %bitcast.17.refs_0_), channel_id=1, source_target_pairs={{0,8},{8,0},{4,12},{12,4},{1,9},{9,1},{5,13},{13,5},{2,10},{10,2},... | collective-permute-start | bytes 6291464 | tf_op jit(solution)/shard_map/ppermute | solution.py:33
  11.5 15.5 %copy-start.5 = (bf16[128,2048]{1,0:T(8,128)(2,1)S(1)}, bf16[128,2048]{1,0:T(8,128)(2,1)}, u32[]{:S(2)}) copy-start(bf16[128,2048]{1,0:T(8,128)(2,1)} %refs_7_.9) | copy-start | bytes 1572868
  21.8 22.6 %collective-permute-start.2 = (f32[2,256,256]{2,1,0:T(8,128)}, f32[2,256,256]{2,1,0:T(8,128)}, u32[]{:S(2)}, u32[]{:S(2)}) collective-permute-start(f32[2,256,256]{2,1,0:T(8,128)} %get-tuple-element.41), channel_id=1, source_target_pairs={{0,1},{1,0},{2,3},{3,2},{4,5},{5,4},{6,7},{7,6},{8,9},{9,8},{10,11... | collective-permute-start | bytes 1572872 | tf_op jit(solution)/shard_map/ppermute | solution.py:33
  23.3 21.2 %collective-permute-start.1 = (f32[256,256]{1,0:T(8,128)S(1)}, f32[256,256]{1,0:T(8,128)S(1)}, u32[]{:S(2)}, u32[]{:S(2)}) collective-permute-start(f32[256,256]{1,0:T(8,128)S(1)} %fusion.3), channel_id=1, source_target_pairs={{0,3},{3,0},{1,2},{2,1},{4,7},{7,4},{5,6},{6,5},{8,11},{11,8},{9,1... | collective-permute-start | bytes 786440 | tf_op jit(solution)/shard_map/ppermute | solution.py:33
  28.5 17.3 %copy-start.2 = (bf16[128,7168]{1,0:T(8,128)(2,1)S(1)}, bf16[128,7168]{1,0:T(8,128)(2,1)}, u32[]{:S(2)}) copy-start(bf16[128,7168]{1,0:T(8,128)(2,1)} %refs_6_.9) | copy-start | bytes 5505028
  37.7 17.8 %copy-start.8 = (f32[2,256,256]{2,1,0:T(8,128)}, f32[2,256,256]{2,1,0:T(8,128)S(1)}, u32[]{:S(2)}) copy-start(f32[2,256,256]{2,1,0:T(8,128)S(1)} %get-tuple-element.46.refs_1_) | copy-start | bytes 1572868
  37.7 23.6 %collective-permute-start.4 = (f32[2,256,256]{2,1,0:T(8,128)S(1)}, f32[2,256,256]{2,1,0:T(8,128)S(1)}, u32[]{:S(2)}, u32[]{:S(2)}) collective-permute-start(f32[2,256,256]{2,1,0:T(8,128)S(1)} %get-tuple-element.45), channel_id=1, source_target_pairs={{0,1},{1,0},{2,3},{3,2},{4,5},{5,4},{6,7},{7,6},{8,9},{9,8},{10,11... | collective-permute-start | bytes 1572872 | tf_op jit(solution)/shard_map/ppermute | solution.py:33
  44.5 11.0 %copy-start.14 = (f32[256,256]{1,0:T(8,128)}, f32[256,256]{1,0:T(8,128)S(1)}, u32[]{:S(2)}) copy-start(f32[256,256]{1,0:T(8,128)S(1)} %collective-permute-done.1.refs_6_) | copy-start | bytes 786436
  45.5 17.7 %copy-start.3 = (bf16[128,7168]{1,0:T(8,128)(2,1)S(1)}, bf16[128,7168]{1,0:T(8,128)(2,1)}, u32[]{:S(2)}) copy-start(bf16[128,7168]{1,0:T(8,128)(2,1)} %refs_6_.9) | copy-start | bytes 5505028
  45.6 15.8 %collective-permute-start.3 = (f32[256,256]{1,0:T(8,128)S(1)}, f32[256,256]{1,0:T(8,128)S(1)}, u32[]{:S(2)}, u32[]{:S(2)}) collective-permute-start(f32[256,256]{1,0:T(8,128)S(1)} %fusion.2), channel_id=1, source_target_pairs={{0,3},{3,0},{1,2},{2,1},{4,7},{7,4},{5,6},{6,5},{8,11},{11,8},{9,1... | collective-permute-start | bytes 786440 | tf_op jit(solution)/shard_map/ppermute | solution.py:33
  55.5 22.2 %collective-permute-start.7 = (f32[2,256,256]{2,1,0:T(8,128)}, f32[2,256,256]{2,1,0:T(8,128)S(1)}, u32[]{:S(2)}, u32[]{:S(2)}) collective-permute-start(f32[2,256,256]{2,1,0:T(8,128)} %get-tuple-element.49), channel_id=1, source_target_pairs={{0,1},{1,0},{2,3},{3,2},{4,5},{5,4},{6,7},{7,6},{8,9},{9,8},{10,11... | collective-permute-start | bytes 1572872 | tf_op jit(solution)/shard_map/ppermute | solution.py:33
  62.9 14.7 %collective-permute-start.6 = (f32[256,256]{1,0:T(8,128)}, f32[256,256]{1,0:T(8,128)}, u32[]{:S(2)}, u32[]{:S(2)}) collective-permute-start(f32[256,256]{1,0:T(8,128)} %fusion.1), channel_id=1, source_target_pairs={{0,3},{3,0},{1,2},{2,1},{4,7},{7,4},{5,6},{6,5},{8,11},{11,8},{9,1... | collective-permute-start | bytes 786440 | tf_op jit(solution)/shard_map/ppermute | solution.py:33
  68.8 9.4 %copy-start.7 = (f32[2,256,256]{2,1,0:T(8,128)S(1)}, f32[2,256,256]{2,1,0:T(8,128)}, u32[]{:S(2)}) copy-start(f32[2,256,256]{2,1,0:T(8,128)} %copy-done.6) | copy-start | bytes 1572868
  68.8 9.4 %copy-start.9 = (f32[2,256,256]{2,1,0:T(8,128)S(1)}, f32[2,256,256]{2,1,0:T(8,128)}, u32[]{:S(2)}) copy-start(f32[2,256,256]{2,1,0:T(8,128)} %copy-done.8) | copy-start | bytes 1572868
  68.8 9.4 %copy-start.11 = (f32[2,256,256]{2,1,0:T(8,128)S(1)}, f32[2,256,256]{2,1,0:T(8,128)}, u32[]{:S(2)}) copy-start(f32[2,256,256]{2,1,0:T(8,128)} %copy-done.10) | copy-start | bytes 1572868
  68.8 9.4 %copy-start.13 = (f32[2,256,256]{2,1,0:T(8,128)S(1)}, f32[2,256,256]{2,1,0:T(8,128)}, u32[]{:S(2)}) copy-start(f32[2,256,256]{2,1,0:T(8,128)} %copy-done.12) | copy-start | bytes 1572868
  68.8 9.4 %copy-start.15 = (f32[256,256]{1,0:T(8,128)S(1)}, f32[256,256]{1,0:T(8,128)}, u32[]{:S(2)}) copy-start(f32[256,256]{1,0:T(8,128)} %copy-done.14) | copy-start | bytes 786436
  68.8 9.4 %copy-start.17 = (f32[256,256]{1,0:T(8,128)S(1)}, f32[256,256]{1,0:T(8,128)}, u32[]{:S(2)}) copy-start(f32[256,256]{1,0:T(8,128)} %copy-done.16) | copy-start | bytes 786436
  77.7 13.8 %collective-permute-start.16 = (f32[64,64,128]{2,1,0:T(8,128)}, f32[64,64,128]{2,1,0:T(8,128)S(1)}, u32[]{:S(2)}, u32[]{:S(2)}) collective-permute-start(f32[64,64,128]{2,1,0:T(8,128)} %collective-permute-done.11.refs_0_), channel_id=1, source_target_pairs={{0,4},{4,0},{8,12},{12,8},{1,5},{5,1},{9,13},{13,9},{2,6},{6,2},{1... | collective-permute-start | bytes 6291464 | tf_op jit(solution)/shard_map/ppermute | solution.py:33
  77.8 11.0 %collective-permute-start.12 = (f32[256,256]{1,0:T(8,128)S(1)}, f32[256,256]{1,0:T(8,128)S(1)}, u32[]{:S(2)}, u32[]{:S(2)}) collective-permute-start(f32[256,256]{1,0:T(8,128)S(1)} %fusion), channel_id=1, source_target_pairs={{0,3},{3,0},{1,2},{2,1},{4,7},{7,4},{5,6},{6,5},{8,11},{11,8},{9,1... | collective-permute-start | bytes 786440 | tf_op jit(solution)/shard_map/ppermute | solution.py:33
  79.7 10.3 %collective-permute-start.8 = (f32[3,32,128]{2,1,0:T(8,128)S(1)}, f32[3,32,128]{2,1,0:T(8,128)S(1)}, u32[]{:S(2)}, u32[]{:S(2)}) collective-permute-start(f32[3,32,128]{2,1,0:T(8,128)S(1)} %get-tuple-element.58), channel_id=1, source_target_pairs={{0,1},{1,0},{2,3},{3,2},{4,5},{5,4},{6,7},{7,6},{8,9},{9,8},{10,11... | collective-permute-start | bytes 147464 | tf_op jit(solution)/shard_map/ppermute | solution.py:33
  79.8 16.7 %collective-permute-start.9 = (f32[3,32,128]{2,1,0:T(8,128)S(1)}, f32[3,32,128]{2,1,0:T(8,128)S(1)}, u32[]{:S(2)}, u32[]{:S(2)}) collective-permute-start(f32[3,32,128]{2,1,0:T(8,128)S(1)} %get-tuple-element.59), channel_id=1, source_target_pairs={{0,2},{2,0},{1,3},{3,1},{4,6},{6,4},{5,7},{7,5},{8,10},{10,8},{9,1... | collective-permute-start | bytes 147464 | tf_op jit(solution)/shard_map/ppermute | solution.py:33
  83.9 12.5 %collective-permute-start.10 = (f32[3,32,128]{2,1,0:T(8,128)S(1)}, f32[3,32,128]{2,1,0:T(8,128)S(1)}, u32[]{:S(2)}, u32[]{:S(2)}) collective-permute-start(f32[3,32,128]{2,1,0:T(8,128)S(1)} %get-tuple-element.60), channel_id=1, source_target_pairs={{0,3},{3,0},{1,2},{2,1},{4,7},{7,4},{5,6},{6,5},{8,11},{11,8},{9,1... | collective-permute-start | bytes 147464 | tf_op jit(solution)/shard_map/ppermute | solution.py:33
  89.6 6.9 %collective-permute-start.13 = (f32[1,32,128]{2,1,0:T(8,128)S(1)}, f32[1,32,128]{2,1,0:T(8,128)S(1)}, u32[]{:S(2)}, u32[]{:S(2)}) collective-permute-start(f32[1,32,128]{2,1,0:T(8,128)S(1)} %get-tuple-element.66), channel_id=1, source_target_pairs={{0,1},{1,0},{2,3},{3,2},{4,5},{5,4},{6,7},{7,6},{8,9},{9,8},{10,11... | collective-permute-start | bytes 49160 | tf_op jit(solution)/shard_map/ppermute | solution.py:33
  90.1 6.4 %collective-permute-start.14 = (f32[1,32,128]{2,1,0:T(8,128)S(1)}, f32[1,32,128]{2,1,0:T(8,128)S(1)}, u32[]{:S(2)}, u32[]{:S(2)}) collective-permute-start(f32[1,32,128]{2,1,0:T(8,128)S(1)} %get-tuple-element.67), channel_id=1, source_target_pairs={{0,2},{2,0},{1,3},{3,1},{4,6},{6,4},{5,7},{7,5},{8,10},{10,8},{9,1... | collective-permute-start | bytes 49160 | tf_op jit(solution)/shard_map/ppermute | solution.py:33
  91.6 5.5 %collective-permute-start.15 = (f32[1,32,128]{2,1,0:T(8,128)S(1)}, f32[1,32,128]{2,1,0:T(8,128)S(1)}, u32[]{:S(2)}, u32[]{:S(2)}) collective-permute-start(f32[1,32,128]{2,1,0:T(8,128)S(1)} %get-tuple-element.68), channel_id=1, source_target_pairs={{0,3},{3,0},{1,2},{2,1},{4,7},{7,4},{5,6},{6,5},{8,11},{11,8},{9,1... | collective-permute-start | bytes 49160 | tf_op jit(solution)/shard_map/ppermute | solution.py:33
  100.0 3.7 %collective-permute-start.17 = (f32[8,256]{1,0:T(8,128)S(1)}, f32[8,256]{1,0:T(8,128)S(1)}, u32[]{:S(2)}, u32[]{:S(2)}) collective-permute-start(f32[8,256]{1,0:T(8,128)S(1)} %shard_map.101), channel_id=1, source_target_pairs={{0,1},{1,0},{2,3},{3,2},{4,5},{5,4},{6,7},{7,6},{8,9},{9,8},{10,11... | collective-permute-start | bytes 24584 | tf_op jit(solution)/shard_map/ppermute | solution.py:33
  103.7 4.5 %collective-permute-start.18 = (f32[8,256]{1,0:T(8,128)S(1)}, f32[8,256]{1,0:T(8,128)S(1)}, u32[]{:S(2)}, u32[]{:S(2)}) collective-permute-start(f32[8,256]{1,0:T(8,128)S(1)} %add.58), channel_id=1, source_target_pairs={{0,2},{2,0},{1,3},{3,1},{4,6},{6,4},{5,7},{7,5},{8,10},{10,8},{9,1... | collective-permute-start | bytes 24584 | tf_op jit(solution)/shard_map/ppermute | solution.py:33
  (6 other events, 13.2 us)
